TPU v7x, 128 devices: a whole 4x4x4 slice. The times are simulated.
128 devices in a mesh: bl: 16 (over x, y_hi, core), ch: 8 (over z, y_lo).
Axes of the slice: x: 4, y: 4 (y_hi: 2, y_lo: 2; y = y_hi * 2 + y_lo), z: 4, core: 2. Of those that a mesh axis runs over, the one named last changes fastest.
Arguments:
- uvw_index: int32 [2048], P('bl'), may hold values from 0 to 4095
- row_baseline: int32 [2048], P('bl'), may hold values from 0 to 2015
- flags: int32 [2048, 256], P('bl', 'ch'), may hold values 0 or 1
- uvw_table: bfloat16 [64, 4096], replicated, may hold values from -6 to 6
- baseline_features: bfloat16 [64, 2016], replicated, may hold values from -6 to 6
- w_in: bfloat16 [64, 64], replicated, may hold values from -0.75 to 0.75
- w_out: bfloat16 [64, 2, 65536], P(None, None, 'ch'), may hold values from -0.75 to 0.75
- observed: bfloat16 [2, 65536, 2048], P(None, 'ch', 'bl'), may hold values from -6 to 6
- delay_weight: float32 [65536], replicated, may hold values from 0.25 to 4
Outputs:
- grad_out: float32 [64, 2, 65536], P('bl', None, 'ch')
- grad_in: float32 [64, 64], replicated
- grad_uvw: float32 [64, 4096], replicated
- grad_base: float32 [64, 2016], replicated
All inputs are finite; a program needn't handle non-finite values. No bound on the sum of `flags` on one device may be relied on, other than what follows from the above.
Results may differ from a plain program's by a relative error of at most 0.00035.
The roundings to bfloat16 on the way count: a program that leaves them out, or rounds other values in their place, can miss the bound.
Values sent between devices are 32-bit elements; how exact they have to be, the bound alone decides.
No kernel may reach another device: no remote copies, remote signals or barrier semaphores. Data moves between devices by JAX's collectives and lax.ppermute only.
A program may use at most 128 MiB of HBM per device.

v0:
```python
import functools
import math

import jax
import jax.numpy as jnp
import ml_dtypes
import numpy as np
from jax import lax
from jax.experimental import pallas as pl
from jax.experimental.pallas import tpu as pltpu
from jax.sharding import PartitionSpec as P

BLOCK = 256
NBLOCKS = 256
CHANNELS = 65536
LOSS_SCALE = 0.0625
HIGHEST = lax.Precision.HIGHEST
F32 = jnp.float32
BF16 = jnp.bfloat16
STEP = 8
WIDE = STEP * BLOCK
LANES = 128
PLANES = 4
VMEM = 56 * 2**20


def split_matrix(matrix):
    high = matrix.astype(ml_dtypes.bfloat16)
    low = (matrix - high.astype(np.float64)).astype(ml_dtypes.bfloat16)
    return high, low


def tables():
    n = np.arange(BLOCK)
    product = np.outer(n, n)
    cosine = np.cos(2 * math.pi * (product % BLOCK) / BLOCK)
    sine = np.sin(2 * math.pi * (product % BLOCK) / BLOCK)
    forward = np.block([[cosine, sine], [-sine, cosine]])
    backward = np.block([[cosine, -sine], [sine, cosine]])
    twiddle = 2 * math.pi * product / CHANNELS
    return (
        *split_matrix(forward),
        *split_matrix(backward),
        np.cos(twiddle).astype(np.float32),
        np.sin(twiddle).astype(np.float32),
    )


def taper_table():
    c = np.arange(CHANNELS)
    window = np.full((CHANNELS,), 0.35875)
    for harmonic, term in ((1, -0.48829), (2, 0.14128), (3, -0.01168)):
        window = window + term * np.cos(2 * math.pi * ((c * harmonic) % CHANNELS) / CHANNELS)
    return window.astype(np.float32)


def dot(a, b, dims=(((1,), (0,)), ((), ())), precision=None):
    return lax.dot_general(a, b, dims, precision=precision, preferred_element_type=F32)


NT = (((1,), (1,)), ((), ()))
TN = (((0,), (0,)), ((), ()))


def params(**more):
    return pltpu.CompilerParams(vmem_limit_bytes=VMEM, **more)


def one_hot_rows(index_row, count):
    cells = lax.broadcasted_iota(jnp.int32, (count, index_row.shape[1]), 0)
    return jnp.where(cells == index_row, 1.0, 0.0).astype(BF16)


def trunk_kernel(uvw_ref, base_ref, flags_ref, table_ref, features_ref, w_in_ref, taper_ref,
                 hidden_ref, hidden_t_ref, keep_ref, taper_here_ref):
    taper_here_ref[...] = taper_ref[pl.ds(lax.axis_index("ch"), 1), :]
    summed = dot(table_ref[...], one_hot_rows(uvw_ref[...], table_ref.shape[1]))
    summed = summed + dot(features_ref[...], one_hot_rows(base_ref[...], features_ref.shape[1]))
    inputs = summed.astype(BF16)
    pre_act = dot(w_in_ref[...], inputs, TN)
    hidden = pre_act / (1.0 + jnp.exp(-pre_act))
    hidden_ref[...] = hidden.astype(BF16)
    hidden_t_ref[...] = hidden.T.astype(BF16)
    keep_ref[...] = (1.0 - flags_ref[...].astype(F32)).T.astype(BF16)


def trunk(uvw_index, row_baseline, flags, uvw_table, baseline_features, w_in, taper):
    rows = uvw_index.shape[0]
    units = w_in.shape[1]
    return pl.pallas_call(
        trunk_kernel,
        out_shape=(
            jax.ShapeDtypeStruct((units, rows), BF16),
            jax.ShapeDtypeStruct((rows, units), BF16),
            jax.ShapeDtypeStruct(flags.shape, BF16),
            jax.ShapeDtypeStruct((1, taper.shape[1]), F32),
        ),
        compiler_params=params(),
        name="trunk",
    )(uvw_index[None], row_baseline[None], flags.T, uvw_table, baseline_features, w_in, taper)


def weight_of(keep, taper_row, first_block):
    blocks = keep.shape[1]
    block = lax.broadcasted_iota(jnp.int32, (blocks, WIDE), 0)
    lane = lax.broadcasted_iota(jnp.int32, (blocks, WIDE), 1)
    expand = jnp.where(block == first_block + (lane >> 8), 1.0, 0.0).astype(BF16)
    return dot(keep, expand) * taper_row


def residual_kernel(half, hidden_ref, w_ref, observed_ref, keep_ref, taper_ref, out_ref):
    rows = hidden_ref.shape[0]
    total = observed_ref.shape[2]
    weight = weight_of(keep_ref[...], taper_ref[...], pl.program_id(0) * STEP)
    row = lax.broadcasted_iota(jnp.int32, (rows, total), 0)
    column = lax.broadcasted_iota(jnp.int32, (rows, total), 1)
    pick = jnp.where(column == row + half * rows, -1.0, 0.0).astype(BF16)
    flat = out_ref.reshape(rows * PLANES * STEP, LANES)
    units = w_ref.shape[0]
    pairs = w_ref[...].reshape(2 * units, WIDE)
    unit = lax.broadcasted_iota(jnp.int32, (units, 2 * units), 0)
    place = lax.broadcasted_iota(jnp.int32, (units, 2 * units), 1)
    for q in range(2):
        spread = jnp.where(place == unit * 2 + q, 1.0, 0.0).astype(BF16)
        own = dot(hidden_ref[...], spread).astype(BF16)
        residual = dot(own, pairs) + dot(pick, observed_ref[q], NT)
        residual = residual * weight
        for b in range(STEP):
            for side in range(2):
                start = b * BLOCK + side * LANES
                flat[pl.ds((q * 2 + side) * STEP + b, rows, stride=PLANES * STEP), :] = residual[
                    :, start : start + LANES
                ]


def residual_part(half, halves, hidden_t, w, observed, keep, taper):
    rows = hidden_t.shape[0] // halves
    blocks = keep.shape[1]
    return pl.pallas_call(
        functools.partial(residual_kernel, half),
        grid=(blocks // STEP,),
        in_specs=[
            pl.BlockSpec((rows, hidden_t.shape[1]), lambda g: (half, 0)),
            pl.BlockSpec((w.shape[0], 2, WIDE), lambda g: (0, 0, g)),
            pl.BlockSpec((2, WIDE, observed.shape[2]), lambda g: (0, g, 0)),
            pl.BlockSpec((rows, blocks), lambda g: (half, 0)),
            pl.BlockSpec((1, WIDE), lambda g: (0, g)),
        ],
        out_specs=pl.BlockSpec((rows, PLANES, STEP, LANES), lambda g: (0, 0, g, 0)),
        out_shape=jax.ShapeDtypeStruct((rows, PLANES, blocks, LANES), F32),
        compiler_params=params(),
        cost_estimate=pl.CostEstimate(
            flops=2 * rows * 2 * blocks * BLOCK * 192, bytes_accessed=10 * 2**20, transcendentals=0
        ),
        name=f"residual_{half}",
    )(hidden_t, w, observed, keep, taper)


def halves_of(values):
    high = values.astype(BF16)
    return high, (values - high.astype(F32)).astype(BF16)


def dot_three(a, b):
    return dot(a[0], b[0]) + (dot(a[0], b[1]) + dot(a[1], b[0]))


def delay_kernel(pieces, x_ref, fh_ref, fl_ref, bh_ref, bl_ref, cos_ref, sin_ref, weight_ref, *outs):
    forward = (fh_ref[...], fl_ref[...])
    backward = (bh_ref[...], bl_ref[...])
    cosine, sine = cos_ref[...], sin_ref[...]
    count = x_ref.shape[1]
    members, local = x_ref.shape[0], x_ref.shape[3]
    turned = []
    for i in range(count):
        values = jnp.concatenate(
            [
                jnp.concatenate(
                    [x_ref[:, i, q * 2 + side].reshape(NBLOCKS, LANES) for side in range(2)], axis=1
                )
                for q in range(2)
            ],
            axis=0,
        )
        first = dot_three(forward, halves_of(values))
        real, imag = first[:NBLOCKS], first[NBLOCKS:]
        turned.append(
            jnp.concatenate([real * cosine + imag * sine, imag * cosine - real * sine], axis=1)
        )
    second = dot_three(halves_of(jnp.concatenate(turned, axis=0)), backward)
    factor = weight_ref[...] * (LOSS_SCALE / CHANNELS)
    factor = jnp.concatenate([jnp.concatenate([factor, factor], axis=1)] * count, axis=0)
    third = dot_three(halves_of(second * factor), forward)
    for i in range(count):
        part = third[i * NBLOCKS : (i + 1) * NBLOCKS]
        real, imag = part[:, :BLOCK], part[:, BLOCK:]
        back = jnp.concatenate([real * cosine - imag * sine, imag * cosine + real * sine], axis=0)
        fourth = dot_three(backward, halves_of(back))
        for q in range(2):
            for member in range(members):
                start = q * NBLOCKS + member * local
                for out_ref, size in zip(outs, pieces):
                    for side in range(2):
                        out_ref[member, i, q * 2 + side] = fourth[
                            start : start + size, side * LANES : (side + 1) * LANES
                        ]
                    start += size


def delay_filter(pieces, arrived, constants, weight, count=2):
    members, rows, _, local, _ = arrived.shape
    whole = lambda array: pl.BlockSpec(array.shape, lambda g: (0, 0))
    flops = rows * 4 * 3 * 2 * 512 * 512 * 256
    return pl.pallas_call(
        functools.partial(delay_kernel, pieces),
        grid=(rows // count,),
        in_specs=[
            pl.BlockSpec((members, count, PLANES, local, LANES), lambda g: (0, g, 0, 0, 0)),
            *[whole(array) for array in constants],
            whole(weight),
        ],
        out_specs=[
            pl.BlockSpec((members, count, PLANES, size, LANES), lambda g: (0, g, 0, 0, 0))
            for size in pieces
        ],
        out_shape=[
            jax.ShapeDtypeStruct((members, rows, PLANES, size, LANES), F32) for size in pieces
        ],
        compiler_params=params(),
        cost_estimate=pl.CostEstimate(flops=flops, bytes_accessed=12 * 2**20, transcendentals=0),
        name=f"delay_{len(pieces)}",
    )(arrived, *constants, weight)


def tail_kernel(first, g1_ref, g2_ref, hidden_ref, w_ref, keep_ref, taper_ref, before_ref,
                mine_ref, other_ref, hidden_grad_ref):
    step = pl.program_id(0)
    weight = weight_of(keep_ref[...], taper_ref[...], (first + step) * STEP)
    rows = g1_ref.shape[0]
    flats = [ref.reshape(rows * PLANES * STEP, LANES) for ref in (g1_ref, g2_ref)]

    @pl.when(step == 0)
    def _():
        hidden_grad_ref[...] = before_ref[...]

    total = hidden_grad_ref[...]
    for q in range(2):
        values = jnp.concatenate(
            [
                jnp.concatenate(
                    [
                        flat[pl.ds((q * 2 + side) * STEP + b, rows, stride=PLANES * STEP), :]
                        for b in range(STEP)
                        for side in range(2)
                    ],
                    axis=1,
                )
                for flat in flats
            ],
            axis=0,
        )
        grad_field = (values * weight).astype(BF16)
        grad_out = dot(hidden_ref[...], grad_field)
        units = grad_out.shape[0] // 2
        for d in range(4):
            mine_ref[d, q] = grad_out[d * 8 : (d + 1) * 8]
            other_ref[d, q] = grad_out[units + d * 8 : units + (d + 1) * 8]
        total = total + dot(w_ref[q], grad_field, NT)
    hidden_grad_ref[...] = total


def tail_part(first, count, g1, g2, hidden_order, w, keep, taper, before):
    rows = g1.shape[0]
    units, total_rows = hidden_order.shape
    return pl.pallas_call(
        functools.partial(tail_kernel, first),
        grid=(count,),
        in_specs=[
            pl.BlockSpec((rows, PLANES, STEP, LANES), lambda g: (0, 0, first + g, 0)),
            pl.BlockSpec((rows, PLANES, STEP, LANES), lambda g: (0, 0, g, 0)),
            pl.BlockSpec((units, total_rows), lambda g: (0, 0)),
            pl.BlockSpec((2, units, WIDE), lambda g: (0, 0, first + g)),
            pl.BlockSpec(keep.shape, lambda g: (0, 0)),
            pl.BlockSpec((1, WIDE), lambda g: (0, first + g)),
            pl.BlockSpec((units, total_rows), lambda g: (0, 0)),
        ],
        out_specs=[
            pl.BlockSpec((4, 2, 8, WIDE), lambda g: (0, 0, 0, g)),
            pl.BlockSpec((4, 2, 8, WIDE), lambda g: (0, 0, 0, g)),
            pl.BlockSpec((units, total_rows), lambda g: (0, 0)),
        ],
        out_shape=[
            jax.ShapeDtypeStruct((4, 2, 8, count * WIDE), F32),
            jax.ShapeDtypeStruct((4, 2, 8, count * WIDE), F32),
            jax.ShapeDtypeStruct((units, total_rows), F32),
        ],
        compiler_params=params(),
        cost_estimate=pl.CostEstimate(
            flops=count * 2 * 2 * 2 * 64 * 128 * WIDE, bytes_accessed=count * 4 * 2**20, transcendentals=0
        ),
        name=f"tail_{first}",
    )(g1, g2, hidden_order, w, keep, taper, before)


def terms_of(values, count):
    out = []
    for _ in range(count):
        term = values.astype(BF16)
        out.append(term)
        values = values - term.astype(F32)
    return out


def member_blocks(count):
    apart = [lax.axis_index("bl") ^ m for m in range(count)]
    return [(a // 4, a % 4) for a in apart]


def rows_kernel(index_ref, table_ref, features_ref, w_in_ref, inputs_ref, slope_ref, cells_ref):
    spots = member_blocks(index_ref.shape[0] * index_ref.shape[1])
    cells = jnp.concatenate([index_ref[f, n] for f, n in spots], axis=1).astype(jnp.int32)
    cells_ref[...] = cells
    summed = []
    for which, ref in ((0, table_ref), (1, features_ref)):
        total = 0.0
        for start in range(0, ref.shape[1], 512):
            size = min(512, ref.shape[1] - start)
            picked = one_hot_rows(cells[which : which + 1] - start, size)
            total = total + dot(ref[:, start : start + size], picked)
        summed.append(total)
    inputs = (summed[0] + summed[1]).astype(BF16)
    inputs_ref[...] = inputs
    pre_act = dot(w_in_ref[...], inputs, TN)
    sigmoid = 1.0 / (1.0 + jnp.exp(-pre_act))
    slope_ref[...] = sigmoid * (1.0 + pre_act * (1.0 - sigmoid))


def all_rows(index, uvw_table, baseline_features, w_in):
    rows = index.shape[0] * index.shape[1] * index.shape[3]
    return pl.pallas_call(
        rows_kernel,
        out_shape=[
            jax.ShapeDtypeStruct((w_in.shape[0], rows), BF16),
            jax.ShapeDtypeStruct((w_in.shape[1], rows), F32),
            jax.ShapeDtypeStruct((index.shape[2], rows), jnp.int32),
        ],
        compiler_params=params(),
        cost_estimate=pl.CostEstimate(flops=6 * 10**9, bytes_accessed=2**20, transcendentals=0),
        name="all_rows",
    )(index, uvw_table, baseline_features, w_in)


def scatter_kernel(own_ref, one_ref, two_ref, three_ref, inputs_ref, slope_ref, cells_ref, w_in_ref,
                   grad_in_ref, grad_uvw_ref, grad_base_ref):
    units = w_in_ref.shape[0]
    blocks = []
    for far, n in member_blocks(16):
        block = own_ref[n]
        for k, ref in ((1, one_ref), (2, two_ref), (3, three_ref)):
            block = jnp.where(far == k, ref[n], block)
        blocks.append(block)
    pre_grad = jnp.concatenate(blocks, axis=1) * slope_ref[...]
    grad_terms = jnp.concatenate(terms_of(pre_grad, 2), axis=0)
    parts = dot(inputs_ref[...], grad_terms, NT)
    grad_in_ref[...] = parts[:, :units] + parts[:, units:]
    input_grad = dot(w_in_ref[...], grad_terms[:units]) + dot(w_in_ref[...], grad_terms[units:])
    terms = jnp.concatenate(terms_of(input_grad, 2), axis=0)
    for which, out_ref in ((0, grad_uvw_ref), (1, grad_base_ref)):
        index = cells_ref[which : which + 1, :]
        cells = out_ref.shape[1]
        half = -(-cells // 2 // LANES) * LANES
        upper = index >= half
        index = jnp.where(upper, index - half, index)
        zero = jnp.zeros_like(terms)
        sides = jnp.concatenate(
            [jnp.where(upper, zero, terms), jnp.where(upper, terms, zero)], axis=0
        )
        for start in range(0, half, 512):
            size = min(512, half - start)
            sums = dot(one_hot_rows(index - start, size), sides, NT).T
            for side in range(2):
                first = side * half + start
                wide = min(size, cells - first)
                part = sums[side * 2 * units : (side + 1) * 2 * units, :wide]
                out_ref[:, first : first + wide] = part[:units] + part[units:]


def scatter(blocks, known, w_in, cells, baselines):
    return pl.pallas_call(
        scatter_kernel,
        out_shape=[
            jax.ShapeDtypeStruct(w_in.shape, F32),
            jax.ShapeDtypeStruct((w_in.shape[0], cells), F32),
            jax.ShapeDtypeStruct((w_in.shape[0], baselines), F32),
        ],
        compiler_params=params(),
        cost_estimate=pl.CostEstimate(
            flops=6 * 10**9, bytes_accessed=4 * 2**20, transcendentals=0
        ),
        name="scatter",
    )(*blocks, *known, w_in)


def swap(values, axis, distance):
    size = lax.axis_size(axis)
    return lax.ppermute(values, axis, [(i, i ^ distance) for i in range(size)])


def met(values, axis, distances):
    return [values, *[swap(values, axis, distance) for distance in distances]]


def sum_over_ch(values, *others):
    a, b, c, d = met(values, "ch", (2, 4, 6))
    total = after((a + b) + (c + d), *others)
    return total + swap(total, "ch", 1)


def sum_cores(mine, other, parts):
    return mine + swap(other, "bl", 1)


def sum_far(both):
    ring = lambda d: [(i, (i + 4 * d) % 16) for i in range(16)]
    got = [lax.ppermute(both[d], "bl", ring(d)) for d in (1, 2, 3)]
    return both[0] + got[0] + got[1] + got[2]


def sum_near(total):
    return total[:, :4] + swap(total[:, 4:], "bl", 2)


def together(*values):
    return lax.optimization_barrier(values)


def after(value, *others):
    return lax.optimization_barrier((value, *others))[0]


def body(
    uvw_index, row_baseline, flags, uvw_table, baseline_features, w_in, w_out, observed, delay_weight
):
    members = lax.axis_size("ch")
    rows = uvw_index.shape[0]
    local_blocks = flags.shape[1]
    local_channels = w_out.shape[2]
    half_rows = rows // 2
    per = half_rows // members

    taper = jnp.asarray(taper_table()).reshape(members, local_channels)
    hidden, hidden_t, keep, taper = trunk(
        uvw_index, row_baseline, flags, uvw_table, baseline_features, w_in, taper
    )
    constants = [jnp.asarray(table) for table in tables()]
    weight = delay_weight.reshape(BLOCK, NBLOCKS).T

    def exchange(values):
        size = values.shape[-2]
        return lax.all_to_all(
            values.reshape(members, per, PLANES, size, LANES), "ch", 0, 0, tiled=True
        )

    part = residual_part(0, 2, hidden_t, w_out, observed, keep, taper)
    hidden_t = after(hidden_t, part)
    sent_0 = exchange(part)
    index = jnp.stack([uvw_index, row_baseline]).astype(F32)
    index = jnp.concatenate([index, jnp.zeros((6, rows), F32)], axis=0)
    index = after(index, part)
    index = jnp.stack(met(index, "bl", (4, 8, 12)))
    index = jnp.stack(met(index, "bl", (1, 2, 3)), axis=1)
    part = residual_part(1, 2, hidden_t, w_out, observed, keep, taper)
    sent_1 = exchange(after(part, index))

    me = lax.axis_index("bl")
    order = lax.broadcasted_iota(jnp.int32, hidden.shape[:1], 0)
    core, x_far, y_far, unit = order // 32, (order // 8) % 4, (order // 4) % 2, order % 4
    owner = ((me // 4 + x_far) % 4) * 4 + ((me // 2) % 2 ^ y_far) * 2 + (me % 2 ^ core)
    units = lax.broadcasted_iota(jnp.int32, (hidden.shape[0],) * 2, 1)
    turn = (units == (owner * 4 + unit)[:, None]).astype(BF16)
    hidden_order = dot(turn, hidden).astype(BF16)
    w = w_out.transpose(1, 0, 2)

    (part,) = delay_filter((local_blocks,), sent_0, constants, weight)
    back_0 = exchange(part).reshape(half_rows, PLANES, local_blocks, LANES)
    known = all_rows(after(index, part), uvw_table, baseline_features, w_in)
    sizes = (local_blocks // 2, local_blocks // 2)
    counts = [size // STEP for size in sizes]
    parts = delay_filter(sizes, after(sent_1, part, *known), constants, weight)

    def arrive(part):
        return exchange(part).reshape(half_rows, PLANES, part.shape[-2], LANES)

    piece = arrive(after(parts[0], back_0, hidden_order, w))
    late = after(parts[1], piece)
    mine, other, hidden_grad = tail_part(
        0, counts[0], back_0, piece, hidden_order, w, keep, taper, jnp.zeros(hidden.shape, F32)
    )
    early = sum_cores(mine, other, 1)
    piece = after(arrive(late), early)
    mine, other, hidden_grad = tail_part(
        counts[0], counts[1], back_0, piece, hidden_order, w, keep, taper, hidden_grad
    )
    both = sum_cores(mine, other, 1)
    hidden_grad = sum_over_ch(hidden_grad, both)
    total = sum_far(jnp.concatenate([early, both], axis=3))
    near = jnp.stack(met(hidden_grad, "bl", (1, 2, 3)))
    blocks = met(near, "bl", (4, 8, 12))
    blocks[0] = after(blocks[0], total)
    grad_out = sum_near(total).transpose(1, 0, 2)
    grad_in, grad_uvw, grad_base = scatter(
        blocks, known, w_in, uvw_table.shape[1], baseline_features.shape[1]
    )
    return (grad_out, grad_in, grad_uvw, grad_base)


def solution(mesh):
    return jax.shard_map(
        body,
        mesh=mesh,
        in_specs=(
            P("bl"),
            P("bl"),
            P("bl", "ch"),
            P(),
            P(),
            P(),
            P(None, None, "ch"),
            P(None, "ch", "bl"),
            P(),
        ),
        out_specs=(P("bl", None, "ch"), P(), P(), P()),
        check_vma=False,
    )
```

profile of v0, /device:TPU:1, one launch (start us, length us, event | category | flops | bytes accessed | tf_op | source)
XLA Modules:
  0.0 292.0 jit_solution(10490830408042185479)
XLA Ops:
  0.6 2.6 trunk.1
  3.3 8.2 %residual_0.1 = f32[64,4,32,128]{3,2,1,0:T(8,128)} custom-call(bf16[128,64]{1,0:T(8,128)(2,1)} %get-tuple-element.35.hidden_ref, bf16[64,2,8192]{2,1,0:T(2,128)(2,1)} %w_ref.3, bf16[2,8192,128]{2,1,0:T(8,128)(2,1)} %observed_ref.3, bf16[128,32]{1,0:T(8,128)(2,1)} %get-tuple-element.33.keep_ref, f32[1,8192]{1,0:T(1,128)} %get-tuple-element.34.taper_ref), custom_call_target="tpu_custom_call" | custom-call | flops 402653184 | bytes 10485760 | tf_op jit(solution)/shard_map/residual_0/pallas_call | solution.py:139
  11.5 7.0 %all-to-all-start = ((f32[8,8,4,32,128]{4,3,2,1,0:T(8,128)}), f32[8,8,4,32,128]{4,3,2,1,0:T(8,128)}, u32[]{:S(2)}, u32[]{:S(2)}) async-start(f32[8,8,4,32,128]{4,3,2,1,0:T(8,128)} %bitcast.50), calls=%async_computation | async-start | bytes 8388608 | tf_op jit(solution)/shard_map/all_to_all | solution.py:460
  18.5 1.3 collective-permute-start
  19.8 2.4 collective-permute-start.1
  22.4 1.3 collective-permute-done.1
  23.8 2.6 collective-permute-done.2
  26.3 2.3 collective-permute-start.3
  28.6 2.6 collective-permute-start.4
  31.7 8.1 %residual_1.1 = f32[64,4,32,128]{3,2,1,0:T(8,128)} custom-call(bf16[128,64]{1,0:T(8,128)(2,1)} %get-tuple-element.35.hidden_ref, bf16[64,2,8192]{2,1,0:T(2,128)(2,1)} %w_ref.3, bf16[2,8192,128]{2,1,0:T(8,128)(2,1)} %observed_ref.3, bf16[128,32]{1,0:T(8,128)(2,1)} %get-tuple-element.33.keep_ref, f32[1,8192]{1,0:T(1,128)} %get-tuple-element.34.taper_ref), custom_call_target="tpu_custom_call" | custom-call | flops 402653184 | bytes 10485760 | tf_op jit(solution)/shard_map/residual_1/pallas_call | solution.py:139
  39.8 27.3 %collective-permute-done.4 = f32[4,8,128]{2,1,0:T(8,128)S(1)} collective-permute-done((f32[4,8,128]{2,1,0:T(8,128)S(1)}, f32[4,8,128]{2,1,0:T(8,128)S(1)}, u32[]{:S(2)}, u32[]{:S(2)}) %collective-permute-start.4) | collective-permute-done | bytes 16416 | tf_op jit(solution)/shard_map/ppermute | solution.py:406
  67.1 1.5 collective-permute-done.5
  69.3 4.7 %all-to-all-start.2 = ((f32[8,8,4,32,128]{4,3,2,1,0:T(8,128)}), f32[8,8,4,32,128]{4,3,2,1,0:T(8,128)}, u32[]{:S(2)}, u32[]{:S(2)}) async-start(f32[8,8,4,32,128]{4,3,2,1,0:T(8,128)} %bitcast.51), calls=%async_computation.2 | async-start | bytes 8388608 | tf_op jit(solution)/shard_map/all_to_all | solution.py:460
  74.9 17.9 %delay_1.1 = f32[8,8,4,32,128]{4,3,2,1,0:T(8,128)} custom-call(f32[8,8,4,32,128]{4,3,2,1,0:T(8,128)} %all-to-all-done.x_ref, bf16[512,512]{1,0:T(8,128)(2,1)} %constant.128.clone.fh_ref, bf16[512,512]{1,0:T(8,128)(2,1)} %constant.129.clone.fl_ref, bf16[512,512]{1,0:T(8,128)(2,1)} %constant.130.clone.bh_ref, bf16[512,512]{1,0:T(8,128)(2,1)} %constant.131.clone.bl_ref, ...), custom_call_target="tpu_custom_call" | custom-call | flops 12884901888 | bytes 12582912 | tf_op jit(solution)/shard_map/delay_1/pallas_call | solution.py:214
  92.8 30.1 %all-to-all-done.2.x_ref = f32[8,8,4,32,128]{4,3,2,1,0:T(8,128)} async-done(((f32[8,8,4,32,128]{4,3,2,1,0:T(8,128)}), f32[8,8,4,32,128]{4,3,2,1,0:T(8,128)}, u32[]{:S(2)}, u32[]{:S(2)}) %all-to-all-start.2) | async-done | bytes 4194336 | tf_op jit(solution)/shard_map/all_to_all | solution.py:460
  122.9 4.7 %all-to-all-start.1 = ((f32[8,8,4,32,128]{4,3,2,1,0:T(8,128)}), f32[8,8,4,32,128]{4,3,2,1,0:T(8,128)}, u32[]{:S(2)}, u32[]{:S(2)}) async-start(f32[8,8,4,32,128]{4,3,2,1,0:T(8,128)} %delay_1.1), calls=%async_computation.1 | async-start | bytes 8388608 | tf_op jit(solution)/shard_map/all_to_all | solution.py:460
  127.7 2.5 copy.32
  131.0 6.7 %all_rows.1 = (bf16[64,2048]{1,0:T(8,128)(2,1)}, f32[64,2048]{1,0:T(8,128)}, s32[8,2048]{1,0:T(8,128)}) custom-call(f32[4,4,8,128]{3,2,1,0:T(8,128)} %pad_maximum_fusion.2.index_ref, bf16[64,4096]{1,0:T(8,128)(2,1)} %table_ref.3, bf16[64,2016]{1,0:T(8,128)(2,1)} %features_ref.3, bf16[64,64]{1,0:T(8,128)(2,1)} %w_in_ref.5), custom_call_target="tpu_custom_call" | custom-call | flops 6000000000 | bytes 1048576 | tf_op jit(solution)/shard_map/all_rows/pallas_call | solution.py:340
  137.7 18.0 %delay_2.1 = (f32[8,8,4,16,128]{4,3,2,1,0:T(8,128)}, f32[8,8,4,16,128]{4,3,2,1,0:T(8,128)}) custom-call(f32[8,8,4,32,128]{4,3,2,1,0:T(8,128)} %all-to-all-done.2.x_ref, bf16[512,512]{1,0:T(8,128)(2,1)} %constant.128.clone.fh_ref, bf16[512,512]{1,0:T(8,128)(2,1)} %constant.129.clone.fl_ref, bf16[512,512]{1,0:T(8,128)(2,1)} %constant.130.clone.bh_ref, ...), custom_call_target="tpu_custom_call" | custom-call | flops 12884901888 | bytes 12582912 | tf_op jit(solution)/shard_map/delay_2/pallas_call | solution.py:214
  155.7 19.8 %all-to-all-done.1 = f32[8,8,4,32,128]{4,3,2,1,0:T(8,128)} async-done(((f32[8,8,4,32,128]{4,3,2,1,0:T(8,128)}), f32[8,8,4,32,128]{4,3,2,1,0:T(8,128)}, u32[]{:S(2)}, u32[]{:S(2)}) %all-to-all-start.1) | async-done | bytes 4194336 | tf_op jit(solution)/shard_map/all_to_all | solution.py:460
  175.4 29.3 %all_to_all.25 = f32[8,8,4,16,128]{4,3,2,1,0:T(8,128)} all-to-all(f32[8,8,4,16,128]{4,3,2,1,0:T(8,128)} %get-tuple-element.45), channel_id=1, replica_groups=mesh['bl'=16,'ch'=8] {'ch'}, dimensions={0} | all-to-all | bytes 4194304 | tf_op jit(solution)/shard_map/all_to_all | solution.py:460
  204.8 3.6 %all-to-all-start.4 = ((f32[8,8,4,16,128]{4,3,2,1,0:T(8,128)}), f32[8,8,4,16,128]{4,3,2,1,0:T(8,128)S(1)}, u32[]{:S(2)}, u32[]{:S(2)}) async-start(f32[8,8,4,16,128]{4,3,2,1,0:T(8,128)} %get-tuple-element.49), calls=%async_computation.4 | async-start | bytes 4194304 | tf_op jit(solution)/shard_map/all_to_all | solution.py:460
  209.0 6.6 %tail_0.1 = (f32[4,2,8,4096]{3,2,1,0:T(8,128)}, f32[4,2,8,4096]{3,2,1,0:T(8,128)}, f32[64,128]{1,0:T(8,128)}) custom-call(f32[64,4,32,128]{3,2,1,0:T(8,128)} %bitcast.5.g1_ref, f32[64,4,16,128]{3,2,1,0:T(8,128)} %bitcast.53, bf16[64,128]{1,0:T(8,128)(2,1)} %convolution_convert_fusion.hidden_ref, bf16[2,64,8192]{2,1,0:T(8,128)(2,1)} %bitcast.48, ...), custom_call_target="tpu_custom_call" | custom-call | flops 268435456 | bytes 8388608 | tf_op jit(solution)/shard_map/tail_0/pallas_call | solution.py:275
  215.6 3.5 %collective-permute-start.6 = (f32[4,2,8,4096]{3,2,1,0:T(8,128)}, f32[4,2,8,4096]{3,2,1,0:T(8,128)S(1)}, u32[]{:S(2)}, u32[]{:S(2)}) collective-permute-start(f32[4,2,8,4096]{3,2,1,0:T(8,128)} %get-tuple-element.47), channel_id=1, source_target_pairs={{0,8},{8,0},{16,24},{24,16},{32,40},{40,32},{48,56},{56,48},{64,72... | collective-permute-start | bytes 3145736 | tf_op jit(solution)/shard_map/ppermute | solution.py:406
  219.2 2.5 collective-permute-done.6
  221.7 1.3 add.132
  223.0 9.1 %all-to-all-done.4 = f32[8,8,4,16,128]{4,3,2,1,0:T(8,128)S(1)} async-done(((f32[8,8,4,16,128]{4,3,2,1,0:T(8,128)}), f32[8,8,4,16,128]{4,3,2,1,0:T(8,128)S(1)}, u32[]{:S(2)}, u32[]{:S(2)}) %all-to-all-start.4) | async-done | bytes 2097184 | tf_op jit(solution)/shard_map/all_to_all | solution.py:460
  232.1 1.4 copy-done.1
  233.4 6.6 %tail_2.1 = (f32[4,2,8,4096]{3,2,1,0:T(8,128)}, f32[4,2,8,4096]{3,2,1,0:T(8,128)}, f32[64,128]{1,0:T(8,128)}) custom-call(f32[64,4,32,128]{3,2,1,0:T(8,128)} %bitcast.5.g1_ref, f32[64,4,16,128]{3,2,1,0:T(8,128)} %bitcast.52, bf16[64,128]{1,0:T(8,128)(2,1)} %convolution_convert_fusion.hidden_ref, bf16[2,64,8192]{2,1,0:T(8,128)(2,1)} %bitcast.49, ...), custom_call_target="tpu_custom_call" | custom-call | flops 268435456 | bytes 8388608 | tf_op jit(solution)/shard_map/tail_2/pallas_call | solution.py:275
  240.0 4.3 %collective-permute-start.7 = (f32[4,2,8,4096]{3,2,1,0:T(8,128)}, f32[4,2,8,4096]{3,2,1,0:T(8,128)S(1)}, u32[]{:S(2)}, u32[]{:S(2)}) collective-permute-start(f32[4,2,8,4096]{3,2,1,0:T(8,128)} %get-tuple-element.53), channel_id=1, source_target_pairs={{0,8},{8,0},{16,24},{24,16},{32,40},{40,32},{48,56},{56,48},{64,72... | collective-permute-start | bytes 3145736 | tf_op jit(solution)/shard_map/ppermute | solution.py:406
  244.3 2.5 collective-permute-done.7
  246.8 1.3 add.133
  248.2 2.5 collective-permute-start.10
  250.8 1.7 collective-permute-start.9
  252.5 1.8 collective-permute-start.13
  254.3 1.3 collective-permute-done.12
  256.8 3.1 %collective-permute-done.14 = f32[64,128]{1,0:T(8,128)S(1)} collective-permute-done((f32[64,128]{1,0:T(8,128)S(1)}, f32[64,128]{1,0:T(8,128)S(1)}, u32[]{:S(2)}, u32[]{:S(2)}) %collective-permute-start.14) | collective-permute-done | bytes 32800 | tf_op jit(solution)/shard_map/ppermute | solution.py:406
  260.5 2.5 collective-permute-done.15
  263.0 3.8 %collective-permute-start.16 = (f32[64,128]{1,0:T(8,128)S(1)}, f32[64,128]{1,0:T(8,128)S(1)}, u32[]{:S(2)}, u32[]{:S(2)}) collective-permute-start(f32[64,128]{1,0:T(8,128)S(1)} %add.141), channel_id=1, source_target_pairs={{0,8},{8,0},{16,24},{24,16},{32,40},{40,32},{48,56},{56,48},{64,72... | collective-permute-start | bytes 98312 | tf_op jit(solution)/shard_map/ppermute | solution.py:406
  268.0 2.0 collective-permute-start.18
  270.0 1.4 collective-permute-done.17
  271.4 1.8 collective-permute-done.18
  273.2 1.3 collective-permute-start.19
  275.3 1.8 collective-permute-start.21
  277.3 2.0 collective-permute-start.11
  279.4 2.4 collective-permute-done.20.two_ref
  281.7 2.5 collective-permute-done.21.three_ref
  284.9 6.1 %scatter.1 = (f32[64,64]{1,0:T(8,128)}, f32[64,4096]{1,0:T(8,128)}, f32[64,2016]{1,0:T(8,128)}) custom-call(f32[4,64,128]{2,1,0:T(8,128)} %copy-done.3, f32[4,64,128]{2,1,0:T(8,128)} %copy-done.7, f32[4,64,128]{2,1,0:T(8,128)} %copy-done.8, f32[4,64,128]{2,1,0:T(8,128)} %copy-done.9, bf16[64,2048]{1,0:T(8,128)(2,1)} %get-tuple-element.39.inputs_ref, ...), custom_call_target="tpu_custom_call" | custom-call | flops 6000000000 | bytes 4194304 | tf_op jit(solution)/shard_map/scatter/pallas_call | solution.py:389
  (56 shorter events, 9.5 us)
Async XLA Ops:
  11.5 7.0 %copy-start.5 = (s32[128]{0:T(128)S(1)}, s32[128]{0:T(128)}, u32[]{:S(2)}) copy-start(s32[128]{0:T(128)} %param.16) | copy-start | bytes 1540
  11.5 7.0 %copy-start.6 = (s32[128]{0:T(128)S(1)}, s32[128]{0:T(128)}, u32[]{:S(2)}) copy-start(s32[128]{0:T(128)} %param.17) | copy-start | bytes 1540
  11.5 57.8 %all-to-all-start = ((f32[8,8,4,32,128]{4,3,2,1,0:T(8,128)}), f32[8,8,4,32,128]{4,3,2,1,0:T(8,128)}, u32[]{:S(2)}, u32[]{:S(2)}) async-start(f32[8,8,4,32,128]{4,3,2,1,0:T(8,128)} %bitcast.50), calls=%async_computation | async-start | bytes 8388608 | tf_op jit(solution)/shard_map/all_to_all | solution.py:460
  18.5 3.9 %collective-permute-start = (f32[8,128]{1,0:T(8,128)S(1)}, f32[8,128]{1,0:T(8,128)S(1)}, u32[]{:S(2)}, u32[]{:S(2)}) collective-permute-start(f32[8,128]{1,0:T(8,128)S(1)} %concatenate.6), channel_id=1, source_target_pairs={{0,32},{8,40},{16,48},{24,56},{32,0},{40,8},{48,16},{56,24},{64,96... | collective-permute-start | bytes 12296 | tf_op jit(solution)/shard_map/ppermute | solution.py:406
  19.8 4.0 %collective-permute-start.1 = (f32[8,128]{1,0:T(8,128)S(1)}, f32[8,128]{1,0:T(8,128)S(1)}, u32[]{:S(2)}, u32[]{:S(2)}) collective-permute-start(f32[8,128]{1,0:T(8,128)S(1)} %concatenate.6), channel_id=1, source_target_pairs={{0,64},{8,72},{16,80},{24,88},{32,96},{40,104},{48,112},{56,120},{... | collective-permute-start | bytes 12296 | tf_op jit(solution)/shard_map/ppermute | solution.py:406
  22.2 4.1 %collective-permute-start.2 = (f32[8,128]{1,0:T(8,128)S(1)}, f32[8,128]{1,0:T(8,128)S(1)}, u32[]{:S(2)}, u32[]{:S(2)}) collective-permute-start(f32[8,128]{1,0:T(8,128)S(1)} %concatenate.6), channel_id=1, source_target_pairs={{0,96},{8,104},{16,112},{24,120},{32,64},{40,72},{48,80},{56,88},{... | collective-permute-start | bytes 12296 | tf_op jit(solution)/shard_map/ppermute | solution.py:406
  26.3 13.5 %collective-permute-start.3 = (f32[4,8,128]{2,1,0:T(8,128)S(1)}, f32[4,8,128]{2,1,0:T(8,128)S(1)}, u32[]{:S(2)}, u32[]{:S(2)}) collective-permute-start(f32[4,8,128]{2,1,0:T(8,128)S(1)} %get-tuple-element.72), channel_id=1, source_target_pairs={{0,8},{8,0},{16,24},{24,16},{32,40},{40,32},{48,56},{56,48},{64,72... | collective-permute-start | bytes 49160 | tf_op jit(solution)/shard_map/ppermute | solution.py:406
  28.6 38.5 %collective-permute-start.4 = (f32[4,8,128]{2,1,0:T(8,128)S(1)}, f32[4,8,128]{2,1,0:T(8,128)S(1)}, u32[]{:S(2)}, u32[]{:S(2)}) collective-permute-start(f32[4,8,128]{2,1,0:T(8,128)S(1)} %get-tuple-element.72), channel_id=1, source_target_pairs={{0,16},{8,24},{16,0},{24,8},{32,48},{40,56},{48,32},{56,40},{64,80... | collective-permute-start | bytes 49160 | tf_op jit(solution)/shard_map/ppermute | solution.py:406
  31.2 37.4 %collective-permute-start.5 = (f32[4,8,128]{2,1,0:T(8,128)S(1)}, f32[4,8,128]{2,1,0:T(8,128)S(1)}, u32[]{:S(2)}, u32[]{:S(2)}) collective-permute-start(f32[4,8,128]{2,1,0:T(8,128)S(1)} %get-tuple-element.72), channel_id=1, source_target_pairs={{0,24},{8,16},{16,8},{24,0},{32,56},{40,48},{48,40},{56,32},{64,88... | collective-permute-start | bytes 49160 | tf_op jit(solution)/shard_map/ppermute | solution.py:406
  69.3 4.7 %copy-start.2 = (f32[65536]{0:T(1024)S(1)}, f32[65536]{0:T(1024)}, u32[]{:S(2)}) copy-start(f32[65536]{0:T(1024)} %param.24) | copy-start | bytes 786436
  69.3 53.7 %all-to-all-start.2 = ((f32[8,8,4,32,128]{4,3,2,1,0:T(8,128)}), f32[8,8,4,32,128]{4,3,2,1,0:T(8,128)}, u32[]{:S(2)}, u32[]{:S(2)}) async-start(f32[8,8,4,32,128]{4,3,2,1,0:T(8,128)} %bitcast.51), calls=%async_computation.2 | async-start | bytes 8388608 | tf_op jit(solution)/shard_map/all_to_all | solution.py:460
  92.8 34.9 %copy-start = (bf16[64,2,8192]{2,1,0:T(2,128)(2,1)S(1)}, bf16[64,2,8192]{2,1,0:T(2,128)(2,1)}, u32[]{:S(2)}) copy-start(bf16[64,2,8192]{2,1,0:T(2,128)(2,1)} %w_ref.3) | copy-start | bytes 6291460
  122.9 52.5 %all-to-all-start.1 = ((f32[8,8,4,32,128]{4,3,2,1,0:T(8,128)}), f32[8,8,4,32,128]{4,3,2,1,0:T(8,128)}, u32[]{:S(2)}, u32[]{:S(2)}) async-start(f32[8,8,4,32,128]{4,3,2,1,0:T(8,128)} %delay_1.1), calls=%async_computation.1 | async-start | bytes 8388608 | tf_op jit(solution)/shard_map/all_to_all | solution.py:460
  127.7 2.5 copy-start.10
  204.8 27.3 %all-to-all-start.4 = ((f32[8,8,4,16,128]{4,3,2,1,0:T(8,128)}), f32[8,8,4,16,128]{4,3,2,1,0:T(8,128)S(1)}, u32[]{:S(2)}, u32[]{:S(2)}) async-start(f32[8,8,4,16,128]{4,3,2,1,0:T(8,128)} %get-tuple-element.49), calls=%async_computation.4 | async-start | bytes 4194304 | tf_op jit(solution)/shard_map/all_to_all | solution.py:460
  215.6 6.0 %collective-permute-start.6 = (f32[4,2,8,4096]{3,2,1,0:T(8,128)}, f32[4,2,8,4096]{3,2,1,0:T(8,128)S(1)}, u32[]{:S(2)}, u32[]{:S(2)}) collective-permute-start(f32[4,2,8,4096]{3,2,1,0:T(8,128)} %get-tuple-element.47), channel_id=1, source_target_pairs={{0,8},{8,0},{16,24},{24,16},{32,40},{40,32},{48,56},{56,48},{64,72... | collective-permute-start | bytes 3145736 | tf_op jit(solution)/shard_map/ppermute | solution.py:406
  232.1 1.4 copy-start.1
  240.0 6.8 %collective-permute-start.7 = (f32[4,2,8,4096]{3,2,1,0:T(8,128)}, f32[4,2,8,4096]{3,2,1,0:T(8,128)S(1)}, u32[]{:S(2)}, u32[]{:S(2)}) collective-permute-start(f32[4,2,8,4096]{3,2,1,0:T(8,128)} %get-tuple-element.53), channel_id=1, source_target_pairs={{0,8},{8,0},{16,24},{24,16},{32,40},{40,32},{48,56},{56,48},{64,72... | collective-permute-start | bytes 3145736 | tf_op jit(solution)/shard_map/ppermute | solution.py:406
  248.1 4.4 %copy-start.4 = (f32[64,128]{1,0:T(8,128)S(1)}, f32[64,128]{1,0:T(8,128)}, u32[]{:S(2)}) copy-start(f32[64,128]{1,0:T(8,128)} %get-tuple-element.54) | copy-start | bytes 98308
  248.2 27.0 %collective-permute-start.10 = (f32[2,8,8192]{2,1,0:T(8,128)S(1)}, f32[2,8,8192]{2,1,0:T(8,128)S(1)}, u32[]{:S(2)}, u32[]{:S(2)}) collective-permute-start(f32[2,8,8192]{2,1,0:T(8,128)S(1)} %get-tuple-element.69), channel_id=1, source_target_pairs={{0,96},{8,104},{16,112},{24,120},{32,0},{40,8},{48,16},{56,24},{64... | collective-permute-start | bytes 1572872 | tf_op jit(solution)/shard_map/ppermute | solution.py:425
  250.8 26.3 %collective-permute-start.8 = (f32[2,8,8192]{2,1,0:T(8,128)S(1)}, f32[2,8,8192]{2,1,0:T(8,128)S(1)}, u32[]{:S(2)}, u32[]{:S(2)}) collective-permute-start(f32[2,8,8192]{2,1,0:T(8,128)S(1)} %get-tuple-element.68), channel_id=1, source_target_pairs={{0,32},{8,40},{16,48},{24,56},{32,64},{40,72},{48,80},{56,88},{64,... | collective-permute-start | bytes 1572872 | tf_op jit(solution)/shard_map/ppermute | solution.py:425
  250.8 26.3 %collective-permute-start.9 = (f32[2,8,8192]{2,1,0:T(8,128)S(1)}, f32[2,8,8192]{2,1,0:T(8,128)S(1)}, u32[]{:S(2)}, u32[]{:S(2)}) collective-permute-start(f32[2,8,8192]{2,1,0:T(8,128)S(1)} %get-tuple-element.70), channel_id=1, source_target_pairs={{0,64},{8,72},{16,80},{24,88},{32,96},{40,104},{48,112},{56,120},{... | collective-permute-start | bytes 1572872 | tf_op jit(solution)/shard_map/ppermute | solution.py:425
  252.5 3.1 %collective-permute-start.12 = (f32[64,128]{1,0:T(8,128)S(1)}, f32[64,128]{1,0:T(8,128)S(1)}, u32[]{:S(2)}, u32[]{:S(2)}) collective-permute-start(f32[64,128]{1,0:T(8,128)S(1)} %copy-done.4), channel_id=1, source_target_pairs={{0,2},{1,3},{2,0},{3,1},{4,6},{5,7},{6,4},{7,5},{8,10},{9,11},{10,... | collective-permute-start | bytes 98312 | tf_op jit(solution)/shard_map/ppermute | solution.py:406
  252.5 4.3 %collective-permute-start.13 = (f32[64,128]{1,0:T(8,128)S(1)}, f32[64,128]{1,0:T(8,128)S(1)}, u32[]{:S(2)}, u32[]{:S(2)}) collective-permute-start(f32[64,128]{1,0:T(8,128)S(1)} %copy-done.4), channel_id=1, source_target_pairs={{0,4},{1,5},{2,6},{3,7},{4,0},{5,1},{6,2},{7,3},{8,12},{9,13},{10,... | collective-permute-start | bytes 98312 | tf_op jit(solution)/shard_map/ppermute | solution.py:406
  255.6 4.3 %collective-permute-start.14 = (f32[64,128]{1,0:T(8,128)S(1)}, f32[64,128]{1,0:T(8,128)S(1)}, u32[]{:S(2)}, u32[]{:S(2)}) collective-permute-start(f32[64,128]{1,0:T(8,128)S(1)} %copy-done.4), channel_id=1, source_target_pairs={{0,6},{1,7},{2,4},{3,5},{4,2},{5,3},{6,0},{7,1},{8,14},{9,15},{10,... | collective-permute-start | bytes 98312 | tf_op jit(solution)/shard_map/ppermute | solution.py:406
  259.9 3.1 %collective-permute-start.15 = (f32[64,128]{1,0:T(8,128)S(1)}, f32[64,128]{1,0:T(8,128)S(1)}, u32[]{:S(2)}, u32[]{:S(2)}) collective-permute-start(f32[64,128]{1,0:T(8,128)S(1)} %add_add_fusion), channel_id=1, source_target_pairs={{0,1},{1,0},{2,3},{3,2},{4,5},{5,4},{6,7},{7,6},{8,9},{9,8},{10,11... | collective-permute-start | bytes 98312 | tf_op jit(solution)/shard_map/ppermute | solution.py:406
  263.0 5.0 %collective-permute-start.16 = (f32[64,128]{1,0:T(8,128)S(1)}, f32[64,128]{1,0:T(8,128)S(1)}, u32[]{:S(2)}, u32[]{:S(2)}) collective-permute-start(f32[64,128]{1,0:T(8,128)S(1)} %add.141), channel_id=1, source_target_pairs={{0,8},{8,0},{16,24},{24,16},{32,40},{40,32},{48,56},{56,48},{64,72... | collective-permute-start | bytes 98312 | tf_op jit(solution)/shard_map/ppermute | solution.py:406
  266.8 4.6 %collective-permute-start.17 = (f32[64,128]{1,0:T(8,128)S(1)}, f32[64,128]{1,0:T(8,128)S(1)}, u32[]{:S(2)}, u32[]{:S(2)}) collective-permute-start(f32[64,128]{1,0:T(8,128)S(1)} %add.141), channel_id=1, source_target_pairs={{0,16},{8,24},{16,0},{24,8},{32,48},{40,56},{48,32},{56,40},{64,80... | collective-permute-start | bytes 98312 | tf_op jit(solution)/shard_map/ppermute | solution.py:406
  268.0 5.2 %collective-permute-start.18 = (f32[64,128]{1,0:T(8,128)S(1)}, f32[64,128]{1,0:T(8,128)S(1)}, u32[]{:S(2)}, u32[]{:S(2)}) collective-permute-start(f32[64,128]{1,0:T(8,128)S(1)} %add.141), channel_id=1, source_target_pairs={{0,24},{8,16},{16,8},{24,0},{32,56},{40,48},{48,40},{56,32},{64,88... | collective-permute-start | bytes 98312 | tf_op jit(solution)/shard_map/ppermute | solution.py:406
  273.2 4.1 %copy-start.3 = (f32[4,64,128]{2,1,0:T(8,128)}, f32[4,64,128]{2,1,0:T(8,128)S(1)}, u32[]{:S(2)}) copy-start(f32[4,64,128]{2,1,0:T(8,128)S(1)} %pad_maximum_fusion.1.own_ref) | copy-start | bytes 393220
  273.2 6.2 %collective-permute-start.19 = (f32[4,64,128]{2,1,0:T(8,128)S(1)}, f32[4,64,128]{2,1,0:T(8,128)S(1)}, u32[]{:S(2)}, u32[]{:S(2)}) collective-permute-start(f32[4,64,128]{2,1,0:T(8,128)S(1)} %pad_maximum_fusion.1.own_ref), channel_id=1, source_target_pairs={{0,32},{8,40},{16,48},{24,56},{32,0},{40,8},{48,16},{56,24},{64,96... | collective-permute-start | bytes 393224 | tf_op jit(solution)/shard_map/ppermute | solution.py:406
  274.5 7.3 %collective-permute-start.20 = (f32[4,64,128]{2,1,0:T(8,128)S(1)}, f32[4,64,128]{2,1,0:T(8,128)S(1)}, u32[]{:S(2)}, u32[]{:S(2)}) collective-permute-start(f32[4,64,128]{2,1,0:T(8,128)S(1)} %pad_maximum_fusion.1.own_ref), channel_id=1, source_target_pairs={{0,64},{8,72},{16,80},{24,88},{32,96},{40,104},{48,112},{56,120},{... | collective-permute-start | bytes 393224 | tf_op jit(solution)/shard_map/ppermute | solution.py:406
  275.3 9.0 %collective-permute-start.21 = (f32[4,64,128]{2,1,0:T(8,128)S(1)}, f32[4,64,128]{2,1,0:T(8,128)S(1)}, u32[]{:S(2)}, u32[]{:S(2)}) collective-permute-start(f32[4,64,128]{2,1,0:T(8,128)S(1)} %pad_maximum_fusion.1.own_ref), channel_id=1, source_target_pairs={{0,96},{8,104},{16,112},{24,120},{32,64},{40,72},{48,80},{56,88},{... | collective-permute-start | bytes 393224 | tf_op jit(solution)/shard_map/ppermute | solution.py:406
  277.3 13.7 %collective-permute-start.11 = (f32[2,4,8192]{2,1,0:T(4,128)S(1)}, f32[2,4,8192]{2,1,0:T(4,128)S(1)}, u32[]{:S(2)}, u32[]{:S(2)}) collective-permute-start(f32[2,4,8192]{2,1,0:T(4,128)S(1)} %slice.31), channel_id=1, source_target_pairs={{0,16},{8,24},{16,0},{24,8},{32,48},{40,56},{48,32},{56,40},{64,80... | collective-permute-start | bytes 786440 | tf_op jit(solution)/shard_map/ppermute | solution.py:406
  279.4 4.9 %copy-start.7 = (f32[4,64,128]{2,1,0:T(8,128)}, f32[4,64,128]{2,1,0:T(8,128)S(1)}, u32[]{:S(2)}) copy-start(f32[4,64,128]{2,1,0:T(8,128)S(1)} %collective-permute-done.19.one_ref) | copy-start | bytes 393220
  281.7 2.5 copy-start.8
  284.3 0.7 copy-start.9
where the time goes:
time: 293 us; the launch traced here: 292 us
  waiting for transfers between devices  112 us (38%)
  Pallas kernels  80.8 us (28%)
  starting transfers between devices  57.7 us (20%)
  blocking collectives  29.3 us (10%)
  local copies, waits for them, and re-layouts  7.04 us (2%)
  other arithmetic  3.65 us (1%)
    all_to_all x4, waiting for transfers between devices, exchange(): lax.all_to_all(values.reshape(members, per, PLANES, size, LANES), 'ch', 0...  58.9 us
    ppermute x19, waiting for transfers between devices, swap(): return lax.ppermute(values, axis, [(i, i ^ distance) for i in range(size)])  52.9 us
    pallas_call x2, Pallas kernels, delay_filter(): pl.pallas_call(functools.partial(delay_kernel, pieces), grid=(rows // cou...  35.9 us
    ppermute x19, starting transfers between devices, swap(): return lax.ppermute(values, axis, [(i, i ^ distance) for i in range(size)])  33.3 us
    all_to_all x1, blocking collectives, exchange(): lax.all_to_all(values.reshape(members, per, PLANES, size, LANES), 'ch', 0...  29.3 us
    all_to_all x4, starting transfers between devices, exchange(): lax.all_to_all(values.reshape(members, per, PLANES, size, LANES), 'ch', 0...  20.1 us
    pallas_call x2, Pallas kernels, residual_part(): pl.pallas_call(functools.partial(residual_kernel, half), grid=(blocks //...  16.3 us
    pallas_call x2, Pallas kernels, tail_part(): pl.pallas_call(functools.partial(tail_kernel, first), grid=(count,), in_s...  13.2 us
  transfers between devices with their start and end apart: 26, of which 17 were waited for; matrix products, arithmetic and copies ran while one was open for 2% of the time, Pallas kernels for 22%

commit v1 on v0

--- a/solution.py
+++ b/solution.py
@@ -21,7 +21,7 @@
 WIDE = STEP * BLOCK
 LANES = 128
 PLANES = 4
-VMEM = 56 * 2**20
+VMEM = 63 * 2**20
 
 
 def split_matrix(matrix):
@@ -62,8 +62,8 @@
 TN = (((0,), (0,)), ((), ()))
 
 
-def params(**more):
-    return pltpu.CompilerParams(vmem_limit_bytes=VMEM, **more)
+def params(vmem=VMEM):
+    return pltpu.CompilerParams(vmem_limit_bytes=vmem)
 
 
 def one_hot_rows(index_row, count):
@@ -108,13 +108,13 @@
     return dot(keep, expand) * taper_row
 
 
-def residual_kernel(half, hidden_ref, w_ref, observed_ref, keep_ref, taper_ref, out_ref):
-    rows = hidden_ref.shape[0]
+def residual_kernel(first_row, rows, hidden_ref, w_ref, observed_ref, keep_ref, taper_ref, out_ref):
     total = observed_ref.shape[2]
-    weight = weight_of(keep_ref[...], taper_ref[...], pl.program_id(0) * STEP)
+    own_rows = slice(first_row, first_row + rows)
+    weight = weight_of(keep_ref[own_rows], taper_ref[...], pl.program_id(0) * STEP)
     row = lax.broadcasted_iota(jnp.int32, (rows, total), 0)
     column = lax.broadcasted_iota(jnp.int32, (rows, total), 1)
-    pick = jnp.where(column == row + half * rows, -1.0, 0.0).astype(BF16)
+    pick = jnp.where(column == row + first_row, -1.0, 0.0).astype(BF16)
     flat = out_ref.reshape(rows * PLANES * STEP, LANES)
     units = w_ref.shape[0]
     pairs = w_ref[...].reshape(2 * units, WIDE)
@@ -122,7 +122,7 @@
     place = lax.broadcasted_iota(jnp.int32, (units, 2 * units), 1)
     for q in range(2):
         spread = jnp.where(place == unit * 2 + q, 1.0, 0.0).astype(BF16)
-        own = dot(hidden_ref[...], spread).astype(BF16)
+        own = dot(hidden_ref[own_rows], spread).astype(BF16)
         residual = dot(own, pairs) + dot(pick, observed_ref[q], NT)
         residual = residual * weight
         for b in range(STEP):
@@ -133,17 +133,16 @@
                 ]
 
 
-def residual_part(half, halves, hidden_t, w, observed, keep, taper):
-    rows = hidden_t.shape[0] // halves
+def residual_part(first_row, rows, hidden_t, w, observed, keep, taper):
     blocks = keep.shape[1]
     return pl.pallas_call(
-        functools.partial(residual_kernel, half),
+        functools.partial(residual_kernel, first_row, rows),
         grid=(blocks // STEP,),
         in_specs=[
-            pl.BlockSpec((rows, hidden_t.shape[1]), lambda g: (half, 0)),
+            pl.BlockSpec(hidden_t.shape, lambda g: (0, 0)),
             pl.BlockSpec((w.shape[0], 2, WIDE), lambda g: (0, 0, g)),
             pl.BlockSpec((2, WIDE, observed.shape[2]), lambda g: (0, g, 0)),
-            pl.BlockSpec((rows, blocks), lambda g: (half, 0)),
+            pl.BlockSpec(keep.shape, lambda g: (0, 0)),
             pl.BlockSpec((1, WIDE), lambda g: (0, g)),
         ],
         out_specs=pl.BlockSpec((rows, PLANES, STEP, LANES), lambda g: (0, 0, g, 0)),
@@ -152,7 +151,7 @@
         cost_estimate=pl.CostEstimate(
             flops=2 * rows * 2 * blocks * BLOCK * 192, bytes_accessed=10 * 2**20, transcendentals=0
         ),
-        name=f"residual_{half}",
+        name=f"residual_{first_row}",
     )(hidden_t, w, observed, keep, taper)
 
 
@@ -236,8 +235,9 @@
                 mine_ref, other_ref, hidden_grad_ref):
     step = pl.program_id(0)
     weight = weight_of(keep_ref[...], taper_ref[...], (first + step) * STEP)
-    rows = g1_ref.shape[0]
-    flats = [ref.reshape(rows * PLANES * STEP, LANES) for ref in (g1_ref, g2_ref)]
+    flats = [
+        (ref.shape[0], ref.reshape(ref.shape[0] * PLANES * STEP, LANES)) for ref in (g1_ref, g2_ref)
+    ]
 
     @pl.when(step == 0)
     def _():
@@ -255,7 +255,7 @@
                     ],
                     axis=1,
                 )
-                for flat in flats
+                for rows, flat in flats
             ],
             axis=0,
         )
@@ -270,14 +270,13 @@
 
 
 def tail_part(first, count, g1, g2, hidden_order, w, keep, taper, before):
-    rows = g1.shape[0]
     units, total_rows = hidden_order.shape
     return pl.pallas_call(
         functools.partial(tail_kernel, first),
         grid=(count,),
         in_specs=[
-            pl.BlockSpec((rows, PLANES, STEP, LANES), lambda g: (0, 0, first + g, 0)),
-            pl.BlockSpec((rows, PLANES, STEP, LANES), lambda g: (0, 0, g, 0)),
+            pl.BlockSpec((g1.shape[0], PLANES, STEP, LANES), lambda g: (0, 0, first + g, 0)),
+            pl.BlockSpec((g2.shape[0], PLANES, STEP, LANES), lambda g: (0, 0, g, 0)),
             pl.BlockSpec((units, total_rows), lambda g: (0, 0)),
             pl.BlockSpec((2, units, WIDE), lambda g: (0, 0, first + g)),
             pl.BlockSpec(keep.shape, lambda g: (0, 0)),
@@ -393,7 +392,7 @@
             jax.ShapeDtypeStruct((w_in.shape[0], cells), F32),
             jax.ShapeDtypeStruct((w_in.shape[0], baselines), F32),
         ],
-        compiler_params=params(),
+        compiler_params=params(32 * 2**20),
         cost_estimate=pl.CostEstimate(
             flops=6 * 10**9, bytes_accessed=4 * 2**20, transcendentals=0
         ),
@@ -445,8 +444,7 @@
     rows = uvw_index.shape[0]
     local_blocks = flags.shape[1]
     local_channels = w_out.shape[2]
-    half_rows = rows // 2
-    per = half_rows // members
+    head_rows = rows * 4 // 16
 
     taper = jnp.asarray(taper_table()).reshape(members, local_channels)
     hidden, hidden_t, keep, taper = trunk(
@@ -458,10 +456,13 @@
     def exchange(values):
         size = values.shape[-2]
         return lax.all_to_all(
-            values.reshape(members, per, PLANES, size, LANES), "ch", 0, 0, tiled=True
+            values.reshape(members, -1, PLANES, size, LANES), "ch", 0, 0, tiled=True
         )
 
-    part = residual_part(0, 2, hidden_t, w_out, observed, keep, taper)
+    def arrive(part):
+        return exchange(part).reshape(-1, PLANES, part.shape[-2], LANES)
+
+    part = residual_part(0, head_rows, hidden_t, w_out, observed, keep, taper)
     hidden_t = after(hidden_t, part)
     sent_0 = exchange(part)
     index = jnp.stack([uvw_index, row_baseline]).astype(F32)
@@ -469,7 +470,7 @@
     index = after(index, part)
     index = jnp.stack(met(index, "bl", (4, 8, 12)))
     index = jnp.stack(met(index, "bl", (1, 2, 3)), axis=1)
-    part = residual_part(1, 2, hidden_t, w_out, observed, keep, taper)
+    part = residual_part(head_rows, rows - head_rows, hidden_t, w_out, observed, keep, taper)
     sent_1 = exchange(after(part, index))
 
     me = lax.axis_index("bl")
@@ -482,32 +483,30 @@
     w = w_out.transpose(1, 0, 2)
 
     (part,) = delay_filter((local_blocks,), sent_0, constants, weight)
-    back_0 = exchange(part).reshape(half_rows, PLANES, local_blocks, LANES)
     known = all_rows(after(index, part), uvw_table, baseline_features, w_in)
-    sizes = (local_blocks // 2, local_blocks // 2)
+    part = after(part, hidden_order, w, *known)
+    back_0 = arrive(part)
+    sizes = (local_blocks * 16 // 32, local_blocks * 16 // 32)
     counts = [size // STEP for size in sizes]
-    parts = delay_filter(sizes, after(sent_1, part, *known), constants, weight)
-
-    def arrive(part):
-        return exchange(part).reshape(half_rows, PLANES, part.shape[-2], LANES)
-
-    piece = arrive(after(parts[0], back_0, hidden_order, w))
+    parts = delay_filter(sizes, after(sent_1, part), constants, weight)
+
+    piece = arrive(after(parts[0], back_0))
     late = after(parts[1], piece)
     mine, other, hidden_grad = tail_part(
         0, counts[0], back_0, piece, hidden_order, w, keep, taper, jnp.zeros(hidden.shape, F32)
     )
-    early = sum_cores(mine, other, 1)
-    piece = after(arrive(late), early)
+    both = sum_cores(mine, other, 1)
+    piece = after(arrive(late), both)
+    first = sum_far(both)
     mine, other, hidden_grad = tail_part(
         counts[0], counts[1], back_0, piece, hidden_order, w, keep, taper, hidden_grad
     )
     both = sum_cores(mine, other, 1)
-    hidden_grad = sum_over_ch(hidden_grad, both)
-    total = sum_far(jnp.concatenate([early, both], axis=3))
-    near = jnp.stack(met(hidden_grad, "bl", (1, 2, 3)))
+    hidden_grad = sum_over_ch(hidden_grad, both, first)
+    second = sum_far(both)
+    near = after(jnp.stack(met(hidden_grad, "bl", (1, 2, 3))), second)
     blocks = met(near, "bl", (4, 8, 12))
-    blocks[0] = after(blocks[0], total)
-    grad_out = sum_near(total).transpose(1, 0, 2)
+    grad_out = sum_near(jnp.concatenate([first, second], axis=2)).transpose(1, 0, 2)
     grad_in, grad_uvw, grad_base = scatter(
         blocks, known, w_in, uvw_table.shape[1], baseline_features.shape[1]
     )

time: 293 us -> 284 us (0.969)
  waiting for transfers between devices: 112 us -> 85.5 us
  blocking collectives: 29.3 us -> 40.9 us
  starting transfers between devices: 57.7 us -> 63.9 us
    ppermute x19, waiting for transfers between devices: 52.9 us -> 21.8 us  [swap(): return lax.ppermute(values, axis, [(i, i ^ distance) for i in range(size)])]
    all_to_all x1, blocking collectives: 29.3 us -> 40.9 us  [exchange(): lax.all_to_all(values.reshape(members, -1, PLANES, size, LANES), 'ch', 0,...]
    ppermute x3 -> x6, starting transfers between devices: 4.29 us -> 9.69 us  [sum_far(): got = [lax.ppermute(both[d], 'bl', ring(d)) for d in (1, 2, 3)]]
    all_to_all x4, waiting for transfers between devices: 58.9 us -> 63.7 us  [exchange(): lax.all_to_all(values.reshape(members, -1, PLANES, size, LANES), 'ch', 0,...]
  transfers between devices with their start and end apart: 26 -> 29, of which waited for: 17 -> 14; matrix products, arithmetic and copies ran while one was open for 2% -> 4% of each run, Pallas kernels for 22% -> 25%
where the time goes in v1:
time: 284 us; the launch traced here: 283 us
  waiting for transfers between devices  85.5 us (30%)
  Pallas kernels  79.6 us (28%)
  starting transfers between devices  63.9 us (22%)
  blocking collectives  40.9 us (14%)
  local copies, waits for them, and re-layouts  6.87 us (2%)
  other arithmetic  4.64 us (2%)
    all_to_all x4, waiting for transfers between devices, exchange(): lax.all_to_all(values.reshape(members, -1, PLANES, size, LANES), 'ch', 0,...  63.7 us
    all_to_all x1, blocking collectives, exchange(): lax.all_to_all(values.reshape(members, -1, PLANES, size, LANES), 'ch', 0,...  40.9 us
    pallas_call x2, Pallas kernels, delay_filter(): pl.pallas_call(functools.partial(delay_kernel, pieces), grid=(rows // cou...  35.9 us
    ppermute x19, starting transfers between devices, swap(): return lax.ppermute(values, axis, [(i, i ^ distance) for i in range(size)])  33.1 us
    ppermute x19, waiting for transfers between devices, swap(): return lax.ppermute(values, axis, [(i, i ^ distance) for i in range(size)])  21.8 us
    all_to_all x4, starting transfers between devices, exchange(): lax.all_to_all(values.reshape(members, -1, PLANES, size, LANES), 'ch', 0,...  21.1 us
    pallas_call x2, Pallas kernels, residual_part(): pl.pallas_call(functools.partial(residual_kernel, first_row, rows), grid=...  16.1 us
    pallas_call x2, Pallas kernels, tail_part(): pl.pallas_call(functools.partial(tail_kernel, first), grid=(count,), in_s...  13.5 us
  transfers between devices with their start and end apart: 29, of which 14 were waited for; matrix products, arithmetic and copies ran while one was open for 4% of the time, Pallas kernels for 25%

profile of v1, /device:TPU:1, one launch (start us, length us, event | category | flops | bytes accessed | tf_op | source)
XLA Modules:
  0.0 283.1 jit_solution(11299350185148836855)
XLA Ops:
  0.6 2.6 trunk.1
  3.3 6.6 %residual_0.1 = f32[32,4,32,128]{3,2,1,0:T(8,128)} custom-call(bf16[128,64]{1,0:T(8,128)(2,1)} %get-tuple-element.43.hidden_ref, bf16[64,2,8192]{2,1,0:T(2,128)(2,1)} %w_ref.3, bf16[2,8192,128]{2,1,0:T(8,128)(2,1)} %observed_ref.3, bf16[128,32]{1,0:T(8,128)(2,1)} %get-tuple-element.34.keep_ref, f32[1,8192]{1,0:T(1,128)} %get-tuple-element.35.taper_ref), custom_call_target="tpu_custom_call" | custom-call | flops 201326592 | bytes 10485760 | tf_op jit(solution)/shard_map/residual_0/pallas_call | solution.py:138
  9.9 7.0 %all-to-all-start = ((f32[8,4,4,32,128]{4,3,2,1,0:T(8,128)}), f32[8,4,4,32,128]{4,3,2,1,0:T(8,128)}, u32[]{:S(2)}, u32[]{:S(2)}) async-start(f32[8,4,4,32,128]{4,3,2,1,0:T(8,128)} %bitcast.66), calls=%async_computation | async-start | bytes 4194304 | tf_op jit(solution)/shard_map/all_to_all | solution.py:458
  17.0 1.3 collective-permute-start
  18.3 2.5 collective-permute-start.1
  20.9 1.3 collective-permute-done.1
  22.2 2.6 collective-permute-done.2
  24.8 2.3 collective-permute-start.3
  27.1 2.6 collective-permute-start.4
  30.2 9.4 %residual_32.1 = f32[96,4,32,128]{3,2,1,0:T(8,128)} custom-call(bf16[128,64]{1,0:T(8,128)(2,1)} %get-tuple-element.43.hidden_ref, bf16[64,2,8192]{2,1,0:T(2,128)(2,1)} %w_ref.3, bf16[2,8192,128]{2,1,0:T(8,128)(2,1)} %observed_ref.3, bf16[128,32]{1,0:T(8,128)(2,1)} %get-tuple-element.34.keep_ref, f32[1,8192]{1,0:T(1,128)} %get-tuple-element.35.taper_ref), custom_call_target="tpu_custom_call" | custom-call | flops 603979776 | bytes 10485760 | tf_op jit(solution)/shard_map/residual_32/pallas_call | solution.py:138
  39.7 3.5 %collective-permute-done.4 = f32[4,8,128]{2,1,0:T(8,128)S(1)} collective-permute-done((f32[4,8,128]{2,1,0:T(8,128)S(1)}, f32[4,8,128]{2,1,0:T(8,128)S(1)}, u32[]{:S(2)}, u32[]{:S(2)}) %collective-permute-start.4) | collective-permute-done | bytes 16416 | tf_op jit(solution)/shard_map/ppermute | solution.py:405
  43.1 1.5 collective-permute-done.5
  45.3 5.1 %all-to-all-start.2 = ((f32[8,12,4,32,128]{4,3,2,1,0:T(8,128)}), f32[8,12,4,32,128]{4,3,2,1,0:T(8,128)}, u32[]{:S(2)}, u32[]{:S(2)}) async-start(f32[8,12,4,32,128]{4,3,2,1,0:T(8,128)} %bitcast.62), calls=%async_computation.2 | async-start | bytes 12582912 | tf_op jit(solution)/shard_map/all_to_all | solution.py:458
  50.4 2.5 copy.32
  54.6 10.4 %delay_1.1 = f32[8,4,4,32,128]{4,3,2,1,0:T(8,128)} custom-call(f32[8,4,4,32,128]{4,3,2,1,0:T(8,128)} %all-to-all-done.x_ref, bf16[512,512]{1,0:T(8,128)(2,1)} %constant.128.clone.fh_ref, bf16[512,512]{1,0:T(8,128)(2,1)} %constant.129.clone.fl_ref, bf16[512,512]{1,0:T(8,128)(2,1)} %constant.130.clone.bh_ref, bf16[512,512]{1,0:T(8,128)(2,1)} %constant.131.clone.bl_ref, ...), custom_call_target="tpu_custom_call" | custom-call | flops 6442450944 | bytes 12582912 | tf_op jit(solution)/shard_map/delay_1/pallas_call | solution.py:213
  65.1 6.6 %all_rows.1 = (bf16[64,2048]{1,0:T(8,128)(2,1)}, f32[64,2048]{1,0:T(8,128)}, s32[8,2048]{1,0:T(8,128)}) custom-call(f32[4,4,8,128]{3,2,1,0:T(8,128)} %pad_maximum_fusion.2.index_ref, bf16[64,4096]{1,0:T(8,128)(2,1)} %table_ref.3, bf16[64,2016]{1,0:T(8,128)(2,1)} %features_ref.3, bf16[64,64]{1,0:T(8,128)(2,1)} %w_in_ref.5), custom_call_target="tpu_custom_call" | custom-call | flops 6000000000 | bytes 1048576 | tf_op jit(solution)/shard_map/all_rows/pallas_call | solution.py:339
  71.7 49.9 %all-to-all-done.2.x_ref = f32[8,12,4,32,128]{4,3,2,1,0:T(8,128)} async-done(((f32[8,12,4,32,128]{4,3,2,1,0:T(8,128)}), f32[8,12,4,32,128]{4,3,2,1,0:T(8,128)}, u32[]{:S(2)}, u32[]{:S(2)}) %all-to-all-start.2) | async-done | bytes 6291488 | tf_op jit(solution)/shard_map/all_to_all | solution.py:458
  121.6 4.4 %all-to-all-start.1 = ((f32[8,4,4,32,128]{4,3,2,1,0:T(8,128)}), f32[8,4,4,32,128]{4,3,2,1,0:T(8,128)}, u32[]{:S(2)}, u32[]{:S(2)}) async-start(f32[8,4,4,32,128]{4,3,2,1,0:T(8,128)} %delay_1.1), calls=%async_computation.1 | async-start | bytes 4194304 | tf_op jit(solution)/shard_map/all_to_all | solution.py:458
  126.0 25.5 %delay_2.1 = (f32[8,12,4,16,128]{4,3,2,1,0:T(8,128)}, f32[8,12,4,16,128]{4,3,2,1,0:T(8,128)}) custom-call(f32[8,12,4,32,128]{4,3,2,1,0:T(8,128)} %all-to-all-done.2.x_ref, bf16[512,512]{1,0:T(8,128)(2,1)} %constant.128.clone.fh_ref, bf16[512,512]{1,0:T(8,128)(2,1)} %constant.129.clone.fl_ref, bf16[512,512]{1,0:T(8,128)(2,1)} %constant.130.clone.bh_ref, ...), custom_call_target="tpu_custom_call" | custom-call | flops 19327352832 | bytes 12582912 | tf_op jit(solution)/shard_map/delay_2/pallas_call | solution.py:213
  151.6 40.9 %all_to_all.25 = f32[8,12,4,16,128]{4,3,2,1,0:T(8,128)} all-to-all(f32[8,12,4,16,128]{4,3,2,1,0:T(8,128)} %get-tuple-element.47), channel_id=1, replica_groups=mesh['bl'=16,'ch'=8] {'ch'}, dimensions={0} | all-to-all | bytes 6291456 | tf_op jit(solution)/shard_map/all_to_all | solution.py:458
  192.5 4.7 %all-to-all-start.4 = ((f32[8,12,4,16,128]{4,3,2,1,0:T(8,128)}), f32[8,12,4,16,128]{4,3,2,1,0:T(8,128)}, u32[]{:S(2)}, u32[]{:S(2)}) async-start(f32[8,12,4,16,128]{4,3,2,1,0:T(8,128)} %get-tuple-element.51), calls=%async_computation.4 | async-start | bytes 6291456 | tf_op jit(solution)/shard_map/all_to_all | solution.py:458
  197.8 6.7 %tail_0.1 = (f32[4,2,8,4096]{3,2,1,0:T(8,128)}, f32[4,2,8,4096]{3,2,1,0:T(8,128)}, f32[64,128]{1,0:T(8,128)}) custom-call(f32[32,4,32,128]{3,2,1,0:T(8,128)} %bitcast.17.g1_ref, f32[96,4,16,128]{3,2,1,0:T(8,128)} %bitcast.65, bf16[64,128]{1,0:T(8,128)(2,1)} %convolution_convert_fusion.hidden_ref, bf16[2,64,8192]{2,1,0:T(8,128)(2,1)} %bitcast.63, ...), custom_call_target="tpu_custom_call" | custom-call | flops 268435456 | bytes 8388608 | tf_op jit(solution)/shard_map/tail_0/pallas_call | solution.py:274
  204.5 3.3 %collective-permute-start.6 = (f32[4,2,8,4096]{3,2,1,0:T(8,128)}, f32[4,2,8,4096]{3,2,1,0:T(8,128)S(1)}, u32[]{:S(2)}, u32[]{:S(2)}) collective-permute-start(f32[4,2,8,4096]{3,2,1,0:T(8,128)} %get-tuple-element.49), channel_id=1, source_target_pairs={{0,8},{8,0},{16,24},{24,16},{32,40},{40,32},{48,56},{56,48},{64,72... | collective-permute-start | bytes 3145736 | tf_op jit(solution)/shard_map/ppermute | solution.py:405
  207.8 2.5 collective-permute-done.6
  210.3 1.3 add.141
  213.5 1.2 collective-permute-start.7
  214.7 2.5 collective-permute-start.8
  217.2 1.1 collective-permute-start.9
  218.3 13.7 %all-to-all-done.4 = f32[8,12,4,16,128]{4,3,2,1,0:T(8,128)} async-done(((f32[8,12,4,16,128]{4,3,2,1,0:T(8,128)}), f32[8,12,4,16,128]{4,3,2,1,0:T(8,128)}, u32[]{:S(2)}, u32[]{:S(2)}) %all-to-all-start.4) | async-done | bytes 3145760 | tf_op jit(solution)/shard_map/all_to_all | solution.py:458
  232.0 6.8 %tail_2.1 = (f32[4,2,8,4096]{3,2,1,0:T(8,128)}, f32[4,2,8,4096]{3,2,1,0:T(8,128)}, f32[64,128]{1,0:T(8,128)}) custom-call(f32[32,4,32,128]{3,2,1,0:T(8,128)} %bitcast.17.g1_ref, f32[96,4,16,128]{3,2,1,0:T(8,128)} %bitcast.24.g2_ref, bf16[64,128]{1,0:T(8,128)(2,1)} %convolution_convert_fusion.hidden_ref, bf16[2,64,8192]{2,1,0:T(8,128)(2,1)} %bitcast.64, ...), custom_call_target="tpu_custom_call" | custom-call | flops 268435456 | bytes 8388608 | tf_op jit(solution)/shard_map/tail_2/pallas_call | solution.py:274
  238.8 4.2 %collective-permute-start.10 = (f32[4,2,8,4096]{3,2,1,0:T(8,128)}, f32[4,2,8,4096]{3,2,1,0:T(8,128)S(1)}, u32[]{:S(2)}, u32[]{:S(2)}) collective-permute-start(f32[4,2,8,4096]{3,2,1,0:T(8,128)} %get-tuple-element.55), channel_id=1, source_target_pairs={{0,8},{8,0},{16,24},{24,16},{32,40},{40,32},{48,56},{56,48},{64,72... | collective-permute-start | bytes 3145736 | tf_op jit(solution)/shard_map/ppermute | solution.py:405
  243.0 1.0 fusion.8
  244.1 2.0 collective-permute-start.16
  246.1 1.9 collective-permute-start.17
  248.0 1.4 add.145
  249.5 1.3 collective-permute-start.11
  250.7 2.5 collective-permute-start.12
  253.2 1.1 collective-permute-start.13
  255.0 2.5 collective-permute-done.18
  257.5 2.6 collective-permute-start.19
  261.0 2.4 collective-permute-start.21
  263.3 1.4 collective-permute-done.20
  264.7 1.1 collective-permute-done.21
  266.3 2.6 collective-permute-start.23
  269.9 2.5 collective-permute-start.14
  272.4 2.4 collective-permute-done.23.two_ref
  274.8 2.5 collective-permute-done.24.three_ref
  277.4 4.8 %scatter.1 = (f32[64,64]{1,0:T(8,128)}, f32[64,4096]{1,0:T(8,128)}, f32[64,2016]{1,0:T(8,128)}) custom-call(f32[4,64,128]{2,1,0:T(8,128)S(1)} %pad_maximum_fusion.1.own_ref, f32[4,64,128]{2,1,0:T(8,128)S(1)} %collective-permute-done.22.one_ref, f32[4,64,128]{2,1,0:T(8,128)S(1)} %collective-permute-done.23.two_ref, ...), custom_call_target="tpu_custom_call" | custom-call | flops 6000000000 | bytes 4194304 | tf_op jit(solution)/shard_map/scatter/pallas_call | solution.py:388
  (64 shorter events, 9.9 us)
Async XLA Ops:
  9.9 7.0 %copy-start.8 = (s32[128]{0:T(128)S(1)}, s32[128]{0:T(128)}, u32[]{:S(2)}) copy-start(s32[128]{0:T(128)} %param.16) | copy-start | bytes 1540
  9.9 7.0 %copy-start.9 = (s32[128]{0:T(128)S(1)}, s32[128]{0:T(128)}, u32[]{:S(2)}) copy-start(s32[128]{0:T(128)} %param.17) | copy-start | bytes 1540
  9.9 35.3 %all-to-all-start = ((f32[8,4,4,32,128]{4,3,2,1,0:T(8,128)}), f32[8,4,4,32,128]{4,3,2,1,0:T(8,128)}, u32[]{:S(2)}, u32[]{:S(2)}) async-start(f32[8,4,4,32,128]{4,3,2,1,0:T(8,128)} %bitcast.66), calls=%async_computation | async-start | bytes 4194304 | tf_op jit(solution)/shard_map/all_to_all | solution.py:458
  17.0 3.9 %collective-permute-start = (f32[8,128]{1,0:T(8,128)S(1)}, f32[8,128]{1,0:T(8,128)S(1)}, u32[]{:S(2)}, u32[]{:S(2)}) collective-permute-start(f32[8,128]{1,0:T(8,128)S(1)} %concatenate.6), channel_id=1, source_target_pairs={{0,32},{8,40},{16,48},{24,56},{32,0},{40,8},{48,16},{56,24},{64,96... | collective-permute-start | bytes 12296 | tf_op jit(solution)/shard_map/ppermute | solution.py:405
  18.3 4.0 %collective-permute-start.1 = (f32[8,128]{1,0:T(8,128)S(1)}, f32[8,128]{1,0:T(8,128)S(1)}, u32[]{:S(2)}, u32[]{:S(2)}) collective-permute-start(f32[8,128]{1,0:T(8,128)S(1)} %concatenate.6), channel_id=1, source_target_pairs={{0,64},{8,72},{16,80},{24,88},{32,96},{40,104},{48,112},{56,120},{... | collective-permute-start | bytes 12296 | tf_op jit(solution)/shard_map/ppermute | solution.py:405
  20.7 4.1 %collective-permute-start.2 = (f32[8,128]{1,0:T(8,128)S(1)}, f32[8,128]{1,0:T(8,128)S(1)}, u32[]{:S(2)}, u32[]{:S(2)}) collective-permute-start(f32[8,128]{1,0:T(8,128)S(1)} %concatenate.6), channel_id=1, source_target_pairs={{0,96},{8,104},{16,112},{24,120},{32,64},{40,72},{48,80},{56,88},{... | collective-permute-start | bytes 12296 | tf_op jit(solution)/shard_map/ppermute | solution.py:405
  24.8 14.9 %collective-permute-start.3 = (f32[4,8,128]{2,1,0:T(8,128)S(1)}, f32[4,8,128]{2,1,0:T(8,128)S(1)}, u32[]{:S(2)}, u32[]{:S(2)}) collective-permute-start(f32[4,8,128]{2,1,0:T(8,128)S(1)} %get-tuple-element.77), channel_id=1, source_target_pairs={{0,8},{8,0},{16,24},{24,16},{32,40},{40,32},{48,56},{56,48},{64,72... | collective-permute-start | bytes 49160 | tf_op jit(solution)/shard_map/ppermute | solution.py:405
  27.1 16.1 %collective-permute-start.4 = (f32[4,8,128]{2,1,0:T(8,128)S(1)}, f32[4,8,128]{2,1,0:T(8,128)S(1)}, u32[]{:S(2)}, u32[]{:S(2)}) collective-permute-start(f32[4,8,128]{2,1,0:T(8,128)S(1)} %get-tuple-element.77), channel_id=1, source_target_pairs={{0,16},{8,24},{16,0},{24,8},{32,48},{40,56},{48,32},{56,40},{64,80... | collective-permute-start | bytes 49160 | tf_op jit(solution)/shard_map/ppermute | solution.py:405
  29.7 14.9 %collective-permute-start.5 = (f32[4,8,128]{2,1,0:T(8,128)S(1)}, f32[4,8,128]{2,1,0:T(8,128)S(1)}, u32[]{:S(2)}, u32[]{:S(2)}) collective-permute-start(f32[4,8,128]{2,1,0:T(8,128)S(1)} %get-tuple-element.77), channel_id=1, source_target_pairs={{0,24},{8,16},{16,8},{24,0},{32,56},{40,48},{48,40},{56,32},{64,88... | collective-permute-start | bytes 49160 | tf_op jit(solution)/shard_map/ppermute | solution.py:405
  45.3 5.1 %copy-start.4 = (bf16[64,2,8192]{2,1,0:T(2,128)(2,1)S(1)}, bf16[64,2,8192]{2,1,0:T(2,128)(2,1)}, u32[]{:S(2)}) copy-start(bf16[64,2,8192]{2,1,0:T(2,128)(2,1)} %w_ref.3) | copy-start | bytes 6291460
  45.3 76.3 %all-to-all-start.2 = ((f32[8,12,4,32,128]{4,3,2,1,0:T(8,128)}), f32[8,12,4,32,128]{4,3,2,1,0:T(8,128)}, u32[]{:S(2)}, u32[]{:S(2)}) async-start(f32[8,12,4,32,128]{4,3,2,1,0:T(8,128)} %bitcast.62), calls=%async_computation.2 | async-start | bytes 12582912 | tf_op jit(solution)/shard_map/all_to_all | solution.py:458
  50.3 2.5 copy-start.6
  50.4 3.5 %copy-start.10 = (bf16[64,128]{1,0:T(8,128)(2,1)S(1)}, bf16[64,128]{1,0:T(8,128)(2,1)}, u32[]{:S(2)}) copy-start(bf16[64,128]{1,0:T(8,128)(2,1)} %get-tuple-element.36) | copy-start | bytes 49156
  121.6 29.9 %all-to-all-start.1 = ((f32[8,4,4,32,128]{4,3,2,1,0:T(8,128)}), f32[8,4,4,32,128]{4,3,2,1,0:T(8,128)}, u32[]{:S(2)}, u32[]{:S(2)}) async-start(f32[8,4,4,32,128]{4,3,2,1,0:T(8,128)} %delay_1.1), calls=%async_computation.1 | async-start | bytes 4194304 | tf_op jit(solution)/shard_map/all_to_all | solution.py:458
  192.5 39.5 %all-to-all-start.4 = ((f32[8,12,4,16,128]{4,3,2,1,0:T(8,128)}), f32[8,12,4,16,128]{4,3,2,1,0:T(8,128)}, u32[]{:S(2)}, u32[]{:S(2)}) async-start(f32[8,12,4,16,128]{4,3,2,1,0:T(8,128)} %get-tuple-element.51), calls=%async_computation.4 | async-start | bytes 6291456 | tf_op jit(solution)/shard_map/all_to_all | solution.py:458
  204.5 5.8 %collective-permute-start.6 = (f32[4,2,8,4096]{3,2,1,0:T(8,128)}, f32[4,2,8,4096]{3,2,1,0:T(8,128)S(1)}, u32[]{:S(2)}, u32[]{:S(2)}) collective-permute-start(f32[4,2,8,4096]{3,2,1,0:T(8,128)} %get-tuple-element.49), channel_id=1, source_target_pairs={{0,8},{8,0},{16,24},{24,16},{32,40},{40,32},{48,56},{56,48},{64,72... | collective-permute-start | bytes 3145736 | tf_op jit(solution)/shard_map/ppermute | solution.py:405
  211.6 1.0 copy-start.5
  213.5 29.5 %collective-permute-start.7 = (f32[2,8,4096]{2,1,0:T(8,128)}, f32[2,8,4096]{2,1,0:T(8,128)S(1)}, u32[]{:S(2)}, u32[]{:S(2)}) collective-permute-start(f32[2,8,4096]{2,1,0:T(8,128)} %get-tuple-element.70), channel_id=1, source_target_pairs={{0,32},{8,40},{16,48},{24,56},{32,64},{40,72},{48,80},{56,88},{64,... | collective-permute-start | bytes 786440 | tf_op jit(solution)/shard_map/ppermute | solution.py:424
  214.7 28.3 %collective-permute-start.8 = (f32[2,8,4096]{2,1,0:T(8,128)}, f32[2,8,4096]{2,1,0:T(8,128)S(1)}, u32[]{:S(2)}, u32[]{:S(2)}) collective-permute-start(f32[2,8,4096]{2,1,0:T(8,128)} %get-tuple-element.72), channel_id=1, source_target_pairs={{0,64},{8,72},{16,80},{24,88},{32,96},{40,104},{48,112},{56,120},{... | collective-permute-start | bytes 786440 | tf_op jit(solution)/shard_map/ppermute | solution.py:424
  217.2 25.8 %collective-permute-start.9 = (f32[2,8,4096]{2,1,0:T(8,128)}, f32[2,8,4096]{2,1,0:T(8,128)S(1)}, u32[]{:S(2)}, u32[]{:S(2)}) collective-permute-start(f32[2,8,4096]{2,1,0:T(8,128)} %get-tuple-element.71), channel_id=1, source_target_pairs={{0,96},{8,104},{16,112},{24,120},{32,0},{40,8},{48,16},{56,24},{64... | collective-permute-start | bytes 786440 | tf_op jit(solution)/shard_map/ppermute | solution.py:424
  238.8 15.6 %copy-start.7 = (f32[64,128]{1,0:T(8,128)S(1)}, f32[64,128]{1,0:T(8,128)}, u32[]{:S(2)}) copy-start(f32[64,128]{1,0:T(8,128)} %get-tuple-element.56) | copy-start | bytes 98308
  238.8 9.2 %collective-permute-start.10 = (f32[4,2,8,4096]{3,2,1,0:T(8,128)}, f32[4,2,8,4096]{3,2,1,0:T(8,128)S(1)}, u32[]{:S(2)}, u32[]{:S(2)}) collective-permute-start(f32[4,2,8,4096]{3,2,1,0:T(8,128)} %get-tuple-element.55), channel_id=1, source_target_pairs={{0,8},{8,0},{16,24},{24,16},{32,40},{40,32},{48,56},{56,48},{64,72... | collective-permute-start | bytes 3145736 | tf_op jit(solution)/shard_map/ppermute | solution.py:405
  244.0 9.2 %collective-permute-start.15 = (f32[64,128]{1,0:T(8,128)}, f32[64,128]{1,0:T(8,128)S(1)}, u32[]{:S(2)}, u32[]{:S(2)}) collective-permute-start(f32[64,128]{1,0:T(8,128)} %get-tuple-element.56), channel_id=1, source_target_pairs={{0,2},{1,3},{2,0},{3,1},{4,6},{5,7},{6,4},{7,5},{8,10},{9,11},{10,... | collective-permute-start | bytes 98312 | tf_op jit(solution)/shard_map/ppermute | solution.py:405
  244.1 10.2 %collective-permute-start.16 = (f32[64,128]{1,0:T(8,128)}, f32[64,128]{1,0:T(8,128)S(1)}, u32[]{:S(2)}, u32[]{:S(2)}) collective-permute-start(f32[64,128]{1,0:T(8,128)} %get-tuple-element.56), channel_id=1, source_target_pairs={{0,4},{1,5},{2,6},{3,7},{4,0},{5,1},{6,2},{7,3},{8,12},{9,13},{10,... | collective-permute-start | bytes 98312 | tf_op jit(solution)/shard_map/ppermute | solution.py:405
  246.1 8.2 %collective-permute-start.17 = (f32[64,128]{1,0:T(8,128)}, f32[64,128]{1,0:T(8,128)S(1)}, u32[]{:S(2)}, u32[]{:S(2)}) collective-permute-start(f32[64,128]{1,0:T(8,128)} %get-tuple-element.56), channel_id=1, source_target_pairs={{0,6},{1,7},{2,4},{3,5},{4,2},{5,3},{6,0},{7,1},{8,14},{9,15},{10,... | collective-permute-start | bytes 98312 | tf_op jit(solution)/shard_map/ppermute | solution.py:405
  248.0 29.4 %copy-start = (bf16[64,64]{1,0:T(8,128)(2,1)S(1)}, bf16[64,64]{1,0:T(8,128)(2,1)}, u32[]{:S(2)}) copy-start(bf16[64,64]{1,0:T(8,128)(2,1)} %w_in_ref.5) | copy-start | bytes 24580
  248.0 29.4 %copy-start.1 = (f32[64,2048]{1,0:T(8,128)S(1)}, f32[64,2048]{1,0:T(8,128)}, u32[]{:S(2)}) copy-start(f32[64,2048]{1,0:T(8,128)} %get-tuple-element.40.slope_ref) | copy-start | bytes 1572868
  248.0 29.4 %copy-start.2 = (bf16[64,2048]{1,0:T(8,128)(2,1)S(1)}, bf16[64,2048]{1,0:T(8,128)(2,1)}, u32[]{:S(2)}) copy-start(bf16[64,2048]{1,0:T(8,128)(2,1)} %get-tuple-element.39.inputs_ref) | copy-start | bytes 786436
  248.0 29.4 %copy-start.3 = (s32[8,2048]{1,0:T(8,128)S(1)}, s32[8,2048]{1,0:T(8,128)}, u32[]{:S(2)}) copy-start(s32[8,2048]{1,0:T(8,128)} %get-tuple-element.41.cells_ref) | copy-start | bytes 196612
  249.5 16.4 %collective-permute-start.11 = (f32[2,8,4096]{2,1,0:T(8,128)S(1)}, f32[2,8,4096]{2,1,0:T(8,128)S(1)}, u32[]{:S(2)}, u32[]{:S(2)}) collective-permute-start(f32[2,8,4096]{2,1,0:T(8,128)S(1)} %get-tuple-element.73), channel_id=1, source_target_pairs={{0,32},{8,40},{16,48},{24,56},{32,64},{40,72},{48,80},{56,88},{64,... | collective-permute-start | bytes 786440 | tf_op jit(solution)/shard_map/ppermute | solution.py:424
  250.7 15.1 %collective-permute-start.12 = (f32[2,8,4096]{2,1,0:T(8,128)S(1)}, f32[2,8,4096]{2,1,0:T(8,128)S(1)}, u32[]{:S(2)}, u32[]{:S(2)}) collective-permute-start(f32[2,8,4096]{2,1,0:T(8,128)S(1)} %get-tuple-element.75), channel_id=1, source_target_pairs={{0,64},{8,72},{16,80},{24,88},{32,96},{40,104},{48,112},{56,120},{... | collective-permute-start | bytes 786440 | tf_op jit(solution)/shard_map/ppermute | solution.py:424
  253.2 12.6 %collective-permute-start.13 = (f32[2,8,4096]{2,1,0:T(8,128)S(1)}, f32[2,8,4096]{2,1,0:T(8,128)S(1)}, u32[]{:S(2)}, u32[]{:S(2)}) collective-permute-start(f32[2,8,4096]{2,1,0:T(8,128)S(1)} %get-tuple-element.74), channel_id=1, source_target_pairs={{0,96},{8,104},{16,112},{24,120},{32,0},{40,8},{48,16},{56,24},{64... | collective-permute-start | bytes 786440 | tf_op jit(solution)/shard_map/ppermute | solution.py:424
  254.4 3.1 %collective-permute-start.18 = (f32[64,128]{1,0:T(8,128)S(1)}, f32[64,128]{1,0:T(8,128)S(1)}, u32[]{:S(2)}, u32[]{:S(2)}) collective-permute-start(f32[64,128]{1,0:T(8,128)S(1)} %add_add_fusion), channel_id=1, source_target_pairs={{0,1},{1,0},{2,3},{3,2},{4,5},{5,4},{6,7},{7,6},{8,9},{9,8},{10,11... | collective-permute-start | bytes 98312 | tf_op jit(solution)/shard_map/ppermute | solution.py:405
  257.5 3.4 %collective-permute-start.19 = (f32[64,128]{1,0:T(8,128)S(1)}, f32[64,128]{1,0:T(8,128)S(1)}, u32[]{:S(2)}, u32[]{:S(2)}) collective-permute-start(f32[64,128]{1,0:T(8,128)S(1)} %add.153), channel_id=1, source_target_pairs={{0,8},{8,0},{16,24},{24,16},{32,40},{40,32},{48,56},{56,48},{64,72... | collective-permute-start | bytes 98312 | tf_op jit(solution)/shard_map/ppermute | solution.py:405
  260.1 4.6 %collective-permute-start.20 = (f32[64,128]{1,0:T(8,128)S(1)}, f32[64,128]{1,0:T(8,128)S(1)}, u32[]{:S(2)}, u32[]{:S(2)}) collective-permute-start(f32[64,128]{1,0:T(8,128)S(1)} %add.153), channel_id=1, source_target_pairs={{0,16},{8,24},{16,0},{24,8},{32,48},{40,56},{48,32},{56,40},{64,80... | collective-permute-start | bytes 98312 | tf_op jit(solution)/shard_map/ppermute | solution.py:405
  261.0 4.9 %collective-permute-start.21 = (f32[64,128]{1,0:T(8,128)S(1)}, f32[64,128]{1,0:T(8,128)S(1)}, u32[]{:S(2)}, u32[]{:S(2)}) collective-permute-start(f32[64,128]{1,0:T(8,128)S(1)} %add.153), channel_id=1, source_target_pairs={{0,24},{8,16},{16,8},{24,0},{32,56},{40,48},{48,40},{56,32},{64,88... | collective-permute-start | bytes 98312 | tf_op jit(solution)/shard_map/ppermute | solution.py:405
  265.9 6.5 %collective-permute-start.22 = (f32[4,64,128]{2,1,0:T(8,128)S(1)}, f32[4,64,128]{2,1,0:T(8,128)S(1)}, u32[]{:S(2)}, u32[]{:S(2)}) collective-permute-start(f32[4,64,128]{2,1,0:T(8,128)S(1)} %pad_maximum_fusion.1.own_ref), channel_id=1, source_target_pairs={{0,32},{8,40},{16,48},{24,56},{32,0},{40,8},{48,16},{56,24},{64,96... | collective-permute-start | bytes 393224 | tf_op jit(solution)/shard_map/ppermute | solution.py:405
  266.3 8.5 %collective-permute-start.23 = (f32[4,64,128]{2,1,0:T(8,128)S(1)}, f32[4,64,128]{2,1,0:T(8,128)S(1)}, u32[]{:S(2)}, u32[]{:S(2)}) collective-permute-start(f32[4,64,128]{2,1,0:T(8,128)S(1)} %pad_maximum_fusion.1.own_ref), channel_id=1, source_target_pairs={{0,64},{8,72},{16,80},{24,88},{32,96},{40,104},{48,112},{56,120},{... | collective-permute-start | bytes 393224 | tf_op jit(solution)/shard_map/ppermute | solution.py:405
  268.9 8.4 %collective-permute-start.24 = (f32[4,64,128]{2,1,0:T(8,128)S(1)}, f32[4,64,128]{2,1,0:T(8,128)S(1)}, u32[]{:S(2)}, u32[]{:S(2)}) collective-permute-start(f32[4,64,128]{2,1,0:T(8,128)S(1)} %pad_maximum_fusion.1.own_ref), channel_id=1, source_target_pairs={{0,96},{8,104},{16,112},{24,120},{32,64},{40,72},{48,80},{56,88},{... | collective-permute-start | bytes 393224 | tf_op jit(solution)/shard_map/ppermute | solution.py:405
  269.9 12.2 %collective-permute-start.14 = (f32[2,4,8192]{2,1,0:T(4,128)S(1)}, f32[2,4,8192]{2,1,0:T(4,128)S(1)}, u32[]{:S(2)}, u32[]{:S(2)}) collective-permute-start(f32[2,4,8192]{2,1,0:T(4,128)S(1)} %pad_maximum_fusion), channel_id=1, source_target_pairs={{0,16},{8,24},{16,0},{24,8},{32,48},{40,56},{48,32},{56,40},{64,80... | collective-permute-start | bytes 786440 | tf_op jit(solution)/shard_map/ppermute | solution.py:405

commit v2 on v1

--- a/solution.py
+++ b/solution.py
@@ -120,10 +120,13 @@
     pairs = w_ref[...].reshape(2 * units, WIDE)
     unit = lax.broadcasted_iota(jnp.int32, (units, 2 * units), 0)
     place = lax.broadcasted_iota(jnp.int32, (units, 2 * units), 1)
+    spread = jnp.concatenate(
+        [jnp.where(place == unit * 2 + q, 1.0, 0.0).astype(BF16) for q in range(2)], axis=1
+    )
+    own = dot(hidden_ref[own_rows], spread).astype(BF16)
+    fields = dot(jnp.concatenate([own[:, : 2 * units], own[:, 2 * units :]], axis=0), pairs)
     for q in range(2):
-        spread = jnp.where(place == unit * 2 + q, 1.0, 0.0).astype(BF16)
-        own = dot(hidden_ref[own_rows], spread).astype(BF16)
-        residual = dot(own, pairs) + dot(pick, observed_ref[q], NT)
+        residual = fields[q * rows : (q + 1) * rows] + dot(pick, observed_ref[q], NT)
         residual = residual * weight
         for b in range(STEP):
             for side in range(2):
@@ -232,67 +235,68 @@
 
 
 def tail_kernel(first, g1_ref, g2_ref, hidden_ref, w_ref, keep_ref, taper_ref, before_ref,
-                mine_ref, other_ref, hidden_grad_ref):
+                mine_ref, other_ref, hidden_grad_ref, weight_ref):
     step = pl.program_id(0)
-    weight = weight_of(keep_ref[...], taper_ref[...], (first + step) * STEP)
     flats = [
-        (ref.shape[0], ref.reshape(ref.shape[0] * PLANES * STEP, LANES)) for ref in (g1_ref, g2_ref)
+        (ref.shape[0], ref.reshape(ref.shape[0] * 2 * STEP, LANES)) for ref in (g1_ref, g2_ref)
     ]
 
-    @pl.when(step == 0)
+    @pl.when(pl.program_id(1) == 0)
+    def _():
+        weight_ref[...] = weight_of(keep_ref[...], taper_ref[...], (first + step) * STEP)
+
+    @pl.when((step == 0) & (pl.program_id(1) == 0))
     def _():
         hidden_grad_ref[...] = before_ref[...]
 
-    total = hidden_grad_ref[...]
-    for q in range(2):
-        values = jnp.concatenate(
-            [
-                jnp.concatenate(
-                    [
-                        flat[pl.ds((q * 2 + side) * STEP + b, rows, stride=PLANES * STEP), :]
-                        for b in range(STEP)
-                        for side in range(2)
-                    ],
-                    axis=1,
-                )
-                for rows, flat in flats
-            ],
-            axis=0,
-        )
-        grad_field = (values * weight).astype(BF16)
-        grad_out = dot(hidden_ref[...], grad_field)
-        units = grad_out.shape[0] // 2
-        for d in range(4):
-            mine_ref[d, q] = grad_out[d * 8 : (d + 1) * 8]
-            other_ref[d, q] = grad_out[units + d * 8 : units + (d + 1) * 8]
-        total = total + dot(w_ref[q], grad_field, NT)
-    hidden_grad_ref[...] = total
+    values = jnp.concatenate(
+        [
+            jnp.concatenate(
+                [
+                    flat[pl.ds(side * STEP + b, rows, stride=2 * STEP), :]
+                    for b in range(STEP)
+                    for side in range(2)
+                ],
+                axis=1,
+            )
+            for rows, flat in flats
+        ],
+        axis=0,
+    )
+    grad_field = (values * weight_ref[...]).astype(BF16)
+    grad_out = dot(hidden_ref[...], grad_field)
+    units = grad_out.shape[0] // 2
+    for d in range(4):
+        mine_ref[d, 0] = grad_out[d * 8 : (d + 1) * 8]
+        other_ref[d, 0] = grad_out[units + d * 8 : units + (d + 1) * 8]
+    hidden_grad_ref[...] += dot(w_ref[0], grad_field, NT)
 
 
 def tail_part(first, count, g1, g2, hidden_order, w, keep, taper, before):
     units, total_rows = hidden_order.shape
     return pl.pallas_call(
         functools.partial(tail_kernel, first),
-        grid=(count,),
+        grid=(count, 2),
         in_specs=[
-            pl.BlockSpec((g1.shape[0], PLANES, STEP, LANES), lambda g: (0, 0, first + g, 0)),
-            pl.BlockSpec((g2.shape[0], PLANES, STEP, LANES), lambda g: (0, 0, g, 0)),
-            pl.BlockSpec((units, total_rows), lambda g: (0, 0)),
-            pl.BlockSpec((2, units, WIDE), lambda g: (0, 0, first + g)),
-            pl.BlockSpec(keep.shape, lambda g: (0, 0)),
-            pl.BlockSpec((1, WIDE), lambda g: (0, first + g)),
-            pl.BlockSpec((units, total_rows), lambda g: (0, 0)),
+            pl.BlockSpec((g1.shape[0], 2, STEP, LANES), lambda g, q: (0, q, first + g, 0)),
+            pl.BlockSpec((g2.shape[0], 2, STEP, LANES), lambda g, q: (0, q, g, 0)),
+            pl.BlockSpec((units, total_rows), lambda g, q: (0, 0)),
+            pl.BlockSpec((1, units, WIDE), lambda g, q: (q, 0, first + g)),
+            pl.BlockSpec(keep.shape, lambda g, q: (0, 0)),
+            pl.BlockSpec((1, WIDE), lambda g, q: (0, first + g)),
+            pl.BlockSpec((units, total_rows), lambda g, q: (0, 0)),
         ],
         out_specs=[
-            pl.BlockSpec((4, 2, 8, WIDE), lambda g: (0, 0, 0, g)),
-            pl.BlockSpec((4, 2, 8, WIDE), lambda g: (0, 0, 0, g)),
-            pl.BlockSpec((units, total_rows), lambda g: (0, 0)),
+            pl.BlockSpec((4, 1, 8, WIDE), lambda g, q: (0, q, 0, g)),
+            pl.BlockSpec((4, 1, 8, WIDE), lambda g, q: (0, q, 0, g)),
+            pl.BlockSpec((units, total_rows), lambda g, q: (0, 0)),
         ],
         out_shape=[
             jax.ShapeDtypeStruct((4, 2, 8, count * WIDE), F32),
             jax.ShapeDtypeStruct((4, 2, 8, count * WIDE), F32),
             jax.ShapeDtypeStruct((units, total_rows), F32),
         ],
+        scratch_shapes=[pltpu.VMEM((total_rows, WIDE), F32)],
         compiler_params=params(),
         cost_estimate=pl.CostEstimate(
             flops=count * 2 * 2 * 2 * 64 * 128 * WIDE, bytes_accessed=count * 4 * 2**20, transcendentals=0
@@ -444,7 +448,7 @@
     rows = uvw_index.shape[0]
     local_blocks = flags.shape[1]
     local_channels = w_out.shape[2]
-    head_rows = rows * 4 // 16
+    head_rows = rows * 6 // 16
 
     taper = jnp.asarray(taper_table()).reshape(members, local_channels)
     hidden, hidden_t, keep, taper = trunk(
@@ -464,12 +468,14 @@
 
     part = residual_part(0, head_rows, hidden_t, w_out, observed, keep, taper)
     hidden_t = after(hidden_t, part)
-    sent_0 = exchange(part)
     index = jnp.stack([uvw_index, row_baseline]).astype(F32)
     index = jnp.concatenate([index, jnp.zeros((6, rows), F32)], axis=0)
+    index = jnp.stack([index, swap(index, "bl", 2)])
+    sent_0 = exchange(after(part, index))
     index = after(index, part)
+    across = swap(index, "bl", 1)
+    index = jnp.stack([index[0], across[0], index[1], across[1]])
     index = jnp.stack(met(index, "bl", (4, 8, 12)))
-    index = jnp.stack(met(index, "bl", (1, 2, 3)), axis=1)
     part = residual_part(head_rows, rows - head_rows, hidden_t, w_out, observed, keep, taper)
     sent_1 = exchange(after(part, index))
 

time: 284 us -> 283 us (level)
  waiting for transfers between devices: 85.5 us -> 91.9 us
  blocking collectives: 40.9 us -> 36 us
    all_to_all x4, waiting for transfers between devices: 63.7 us -> 77.6 us  [exchange(): lax.all_to_all(values.reshape(members, -1, PLANES, size, LANES), 'ch', 0,...]
    ppermute x19 -> x18, waiting for transfers between devices: 21.8 us -> 14.2 us  [swap(): return lax.ppermute(values, axis, [(i, i ^ distance) for i in range(size)])]
    all_to_all x1, blocking collectives: 40.9 us -> 36 us  [exchange(): lax.all_to_all(values.reshape(members, -1, PLANES, size, LANES), 'ch', 0,...]
    ppermute x19 -> x18, starting transfers between devices: 33.1 us -> 32.2 us  [swap(): return lax.ppermute(values, axis, [(i, i ^ distance) for i in range(size)])]
  transfers between devices with their start and end apart: 29 -> 28, of which waited for: 14 -> 11; matrix products, arithmetic and copies ran while one was open for 4% -> 4% of each run, Pallas kernels for 25% -> 28%
where the time goes in v2:
time: 283 us; the launch traced here: 282 us
  waiting for transfers between devices  91.9 us (32%)
  Pallas kernels  78.2 us (28%)
  starting transfers between devices  61.7 us (22%)
  blocking collectives  36 us (13%)
  local copies, waits for them, and re-layouts  6.89 us (2%)
  other arithmetic  5.32 us (2%)
    all_to_all x4, waiting for transfers between devices, exchange(): lax.all_to_all(values.reshape(members, -1, PLANES, size, LANES), 'ch', 0,...  77.6 us
    all_to_all x1, blocking collectives, exchange(): lax.all_to_all(values.reshape(members, -1, PLANES, size, LANES), 'ch', 0,...  36 us
    pallas_call x2, Pallas kernels, delay_filter(): pl.pallas_call(functools.partial(delay_kernel, pieces), grid=(rows // cou...  35.9 us
    ppermute x18, starting transfers between devices, swap(): return lax.ppermute(values, axis, [(i, i ^ distance) for i in range(size)])  32.2 us
    all_to_all x4, starting transfers between devices, exchange(): lax.all_to_all(values.reshape(members, -1, PLANES, size, LANES), 'ch', 0,...  19.8 us
    pallas_call x2, Pallas kernels, residual_part(): pl.pallas_call(functools.partial(residual_kernel, first_row, rows), grid=...  16.4 us
    ppermute x18, waiting for transfers between devices, swap(): return lax.ppermute(values, axis, [(i, i ^ distance) for i in range(size)])  14.2 us
    pallas_call x2, Pallas kernels, tail_part(): pl.pallas_call(functools.partial(tail_kernel, first), grid=(count, 2), in...  11.9 us
  transfers between devices with their start and end apart: 28, of which 11 were waited for; matrix products, arithmetic and copies ran while one was open for 4% of the time, Pallas kernels for 28%

profile of v2, /device:TPU:1, one launch (start us, length us, event | category | flops | bytes accessed | tf_op | source)
XLA Modules:
  0.0 281.6 jit_solution(5274759677170837270)
XLA Ops:
  1.3 3.8 %collective-permute-start = (f32[8,128]{1,0:T(8,128)S(1)}, f32[8,128]{1,0:T(8,128)S(1)}, u32[]{:S(2)}, u32[]{:S(2)}) collective-permute-start(f32[8,128]{1,0:T(8,128)S(1)} %get-tuple-element.85), channel_id=1, source_target_pairs={{0,16},{8,24},{16,0},{24,8},{32,48},{40,56},{48,32},{56,40},{64,80... | collective-permute-start | bytes 12296 | tf_op jit(solution)/shard_map/ppermute | solution.py:409
  5.1 2.6 trunk.1
  7.8 7.2 %residual_0.1 = f32[48,4,32,128]{3,2,1,0:T(8,128)} custom-call(bf16[128,64]{1,0:T(8,128)(2,1)} %get-tuple-element.45.hidden_ref, bf16[64,2,8192]{2,1,0:T(2,128)(2,1)} %w_ref.3, bf16[2,8192,128]{2,1,0:T(8,128)(2,1)} %observed_ref.3, bf16[128,32]{1,0:T(8,128)(2,1)} %get-tuple-element.35.keep_ref, f32[1,8192]{1,0:T(1,128)} %get-tuple-element.36.taper_ref), custom_call_target="tpu_custom_call" | custom-call | flops 301989888 | bytes 10485760 | tf_op jit(solution)/shard_map/residual_0/pallas_call | solution.py:141
  15.0 5.2 %all-to-all-start = ((f32[8,6,4,32,128]{4,3,2,1,0:T(8,128)}), f32[8,6,4,32,128]{4,3,2,1,0:T(8,128)}, u32[]{:S(2)}, u32[]{:S(2)}) async-start(f32[8,6,4,32,128]{4,3,2,1,0:T(8,128)} %bitcast.58), calls=%async_computation | async-start | bytes 6291456 | tf_op jit(solution)/shard_map/all_to_all | solution.py:462
  20.2 1.2 collective-permute-start.1
  22.2 2.7 collective-permute-start.3
  25.8 9.1 %residual_48.1 = f32[80,4,32,128]{3,2,1,0:T(8,128)} custom-call(bf16[128,64]{1,0:T(8,128)(2,1)} %get-tuple-element.45.hidden_ref, bf16[64,2,8192]{2,1,0:T(2,128)(2,1)} %w_ref.3, bf16[2,8192,128]{2,1,0:T(8,128)(2,1)} %observed_ref.3, bf16[128,32]{1,0:T(8,128)(2,1)} %get-tuple-element.35.keep_ref, f32[1,8192]{1,0:T(1,128)} %get-tuple-element.36.taper_ref), custom_call_target="tpu_custom_call" | custom-call | flops 503316480 | bytes 10485760 | tf_op jit(solution)/shard_map/residual_48/pallas_call | solution.py:141
  35.6 21.7 %all-to-all-done.x_ref = f32[8,6,4,32,128]{4,3,2,1,0:T(8,128)} async-done(((f32[8,6,4,32,128]{4,3,2,1,0:T(8,128)}), f32[8,6,4,32,128]{4,3,2,1,0:T(8,128)}, u32[]{:S(2)}, u32[]{:S(2)}) %all-to-all-start) | async-done | bytes 3145760 | tf_op jit(solution)/shard_map/all_to_all | solution.py:462
  57.3 5.0 %all-to-all-start.2 = ((f32[8,10,4,32,128]{4,3,2,1,0:T(8,128)}), f32[8,10,4,32,128]{4,3,2,1,0:T(8,128)}, u32[]{:S(2)}, u32[]{:S(2)}) async-start(f32[8,10,4,32,128]{4,3,2,1,0:T(8,128)} %bitcast.55), calls=%async_computation.2 | async-start | bytes 10485760 | tf_op jit(solution)/shard_map/all_to_all | solution.py:462
  62.4 2.5 copy.26
  66.6 14.2 %delay_1.1 = f32[8,6,4,32,128]{4,3,2,1,0:T(8,128)} custom-call(f32[8,6,4,32,128]{4,3,2,1,0:T(8,128)} %all-to-all-done.x_ref, bf16[512,512]{1,0:T(8,128)(2,1)} %constant.128.clone.fh_ref, bf16[512,512]{1,0:T(8,128)(2,1)} %constant.129.clone.fl_ref, bf16[512,512]{1,0:T(8,128)(2,1)} %constant.130.clone.bh_ref, bf16[512,512]{1,0:T(8,128)(2,1)} %constant.131.clone.bl_ref, ...), custom_call_target="tpu_custom_call" | custom-call | flops 9663676416 | bytes 12582912 | tf_op jit(solution)/shard_map/delay_1/pallas_call | solution.py:216
  80.8 6.6 %all_rows.1 = (bf16[64,2048]{1,0:T(8,128)(2,1)}, f32[64,2048]{1,0:T(8,128)}, s32[8,2048]{1,0:T(8,128)}) custom-call(f32[4,4,8,128]{3,2,1,0:T(8,128)} %pad_maximum_fusion.2.index_ref, bf16[64,4096]{1,0:T(8,128)(2,1)} %table_ref.3, bf16[64,2016]{1,0:T(8,128)(2,1)} %features_ref.3, bf16[64,64]{1,0:T(8,128)(2,1)} %w_in_ref.5), custom_call_target="tpu_custom_call" | custom-call | flops 6000000000 | bytes 1048576 | tf_op jit(solution)/shard_map/all_rows/pallas_call | solution.py:343
  87.4 33.3 %all-to-all-done.2.x_ref = f32[8,10,4,32,128]{4,3,2,1,0:T(8,128)} async-done(((f32[8,10,4,32,128]{4,3,2,1,0:T(8,128)}), f32[8,10,4,32,128]{4,3,2,1,0:T(8,128)}, u32[]{:S(2)}, u32[]{:S(2)}) %all-to-all-start.2) | async-done | bytes 5242912 | tf_op jit(solution)/shard_map/all_to_all | solution.py:462
  120.7 5.0 %all-to-all-start.1 = ((f32[8,6,4,32,128]{4,3,2,1,0:T(8,128)}), f32[8,6,4,32,128]{4,3,2,1,0:T(8,128)}, u32[]{:S(2)}, u32[]{:S(2)}) async-start(f32[8,6,4,32,128]{4,3,2,1,0:T(8,128)} %delay_1.1), calls=%async_computation.1 | async-start | bytes 6291456 | tf_op jit(solution)/shard_map/all_to_all | solution.py:462
  125.7 21.7 %delay_2.1 = (f32[8,10,4,16,128]{4,3,2,1,0:T(8,128)}, f32[8,10,4,16,128]{4,3,2,1,0:T(8,128)}) custom-call(f32[8,10,4,32,128]{4,3,2,1,0:T(8,128)} %all-to-all-done.2.x_ref, bf16[512,512]{1,0:T(8,128)(2,1)} %constant.128.clone.fh_ref, bf16[512,512]{1,0:T(8,128)(2,1)} %constant.129.clone.fl_ref, bf16[512,512]{1,0:T(8,128)(2,1)} %constant.130.clone.bh_ref, ...), custom_call_target="tpu_custom_call" | custom-call | flops 16106127360 | bytes 12582912 | tf_op jit(solution)/shard_map/delay_2/pallas_call | solution.py:216
  147.4 14.2 %all-to-all-done.1 = f32[8,6,4,32,128]{4,3,2,1,0:T(8,128)} async-done(((f32[8,6,4,32,128]{4,3,2,1,0:T(8,128)}), f32[8,6,4,32,128]{4,3,2,1,0:T(8,128)}, u32[]{:S(2)}, u32[]{:S(2)}) %all-to-all-start.1) | async-done | bytes 3145760 | tf_op jit(solution)/shard_map/all_to_all | solution.py:462
  161.5 36.0 %all_to_all.25 = f32[8,10,4,16,128]{4,3,2,1,0:T(8,128)} all-to-all(f32[8,10,4,16,128]{4,3,2,1,0:T(8,128)} %get-tuple-element.49), channel_id=1, replica_groups=mesh['bl'=16,'ch'=8] {'ch'}, dimensions={0} | all-to-all | bytes 5242880 | tf_op jit(solution)/shard_map/all_to_all | solution.py:462
  197.5 4.6 %all-to-all-start.4 = ((f32[8,10,4,16,128]{4,3,2,1,0:T(8,128)}), f32[8,10,4,16,128]{4,3,2,1,0:T(8,128)}, u32[]{:S(2)}, u32[]{:S(2)}) async-start(f32[8,10,4,16,128]{4,3,2,1,0:T(8,128)} %get-tuple-element.53), calls=%async_computation.4 | async-start | bytes 5242880 | tf_op jit(solution)/shard_map/all_to_all | solution.py:462
  202.8 5.9 %tail_0.1 = (f32[4,2,8,4096]{3,2,1,0:T(8,128)}, f32[4,2,8,4096]{3,2,1,0:T(8,128)}, f32[64,128]{1,0:T(8,128)}) custom-call(f32[48,4,32,128]{3,2,1,0:T(8,128)} %bitcast.12.g1_ref, f32[80,4,16,128]{3,2,1,0:T(8,128)} %bitcast.59, bf16[64,128]{1,0:T(8,128)(2,1)} %convolution_convert_fusion.hidden_ref, bf16[2,64,8192]{2,1,0:T(8,128)(2,1)} %bitcast.56, ...), custom_call_target="tpu_custom_call" | custom-call | flops 268435456 | bytes 8388608 | tf_op jit(solution)/shard_map/tail_0/pallas_call | solution.py:277
  208.7 3.4 %collective-permute-start.5 = (f32[4,2,8,4096]{3,2,1,0:T(8,128)}, f32[4,2,8,4096]{3,2,1,0:T(8,128)S(1)}, u32[]{:S(2)}, u32[]{:S(2)}) collective-permute-start(f32[4,2,8,4096]{3,2,1,0:T(8,128)} %get-tuple-element.51), channel_id=1, source_target_pairs={{0,8},{8,0},{16,24},{24,16},{32,40},{40,32},{48,56},{56,48},{64,72... | collective-permute-start | bytes 3145736 | tf_op jit(solution)/shard_map/ppermute | solution.py:409
  212.1 2.5 collective-permute-done.5
  214.6 1.3 add.141
  215.9 1.0 copy-done.5
  217.8 1.2 collective-permute-start.6
  219.0 2.5 collective-permute-start.7
  221.5 1.1 collective-permute-start.8
  222.6 8.5 %all-to-all-done.4 = f32[8,10,4,16,128]{4,3,2,1,0:T(8,128)} async-done(((f32[8,10,4,16,128]{4,3,2,1,0:T(8,128)}), f32[8,10,4,16,128]{4,3,2,1,0:T(8,128)}, u32[]{:S(2)}, u32[]{:S(2)}) %all-to-all-start.4) | async-done | bytes 2621472 | tf_op jit(solution)/shard_map/all_to_all | solution.py:462
  231.1 6.0 %tail_2.1 = (f32[4,2,8,4096]{3,2,1,0:T(8,128)}, f32[4,2,8,4096]{3,2,1,0:T(8,128)}, f32[64,128]{1,0:T(8,128)}) custom-call(f32[48,4,32,128]{3,2,1,0:T(8,128)} %bitcast.12.g1_ref, f32[80,4,16,128]{3,2,1,0:T(8,128)} %bitcast.19.g2_ref, bf16[64,128]{1,0:T(8,128)(2,1)} %convolution_convert_fusion.hidden_ref, bf16[2,64,8192]{2,1,0:T(8,128)(2,1)} %bitcast.57, ...), custom_call_target="tpu_custom_call" | custom-call | flops 268435456 | bytes 8388608 | tf_op jit(solution)/shard_map/tail_2/pallas_call | solution.py:277
  237.1 4.4 %collective-permute-start.9 = (f32[4,2,8,4096]{3,2,1,0:T(8,128)}, f32[4,2,8,4096]{3,2,1,0:T(8,128)S(1)}, u32[]{:S(2)}, u32[]{:S(2)}) collective-permute-start(f32[4,2,8,4096]{3,2,1,0:T(8,128)} %get-tuple-element.57), channel_id=1, source_target_pairs={{0,8},{8,0},{16,24},{24,16},{32,40},{40,32},{48,56},{56,48},{64,72... | collective-permute-start | bytes 3145736 | tf_op jit(solution)/shard_map/ppermute | solution.py:409
  241.5 1.0 fusion.8
  242.6 1.7 collective-permute-start.15
  244.4 2.1 collective-permute-start.16
  246.5 1.4 add.145
  248.0 1.3 collective-permute-start.10
  249.2 2.5 collective-permute-start.11
  251.7 1.1 collective-permute-start.12
  253.5 2.5 collective-permute-done.17
  256.0 2.6 collective-permute-start.18
  258.6 1.6 collective-permute-start.19
  260.2 1.7 collective-permute-start.20
  261.8 1.4 collective-permute-done.19
  263.2 1.9 collective-permute-done.20
  265.6 1.8 collective-permute-start.22
  267.4 1.7 collective-permute-start.23
  269.2 1.5 collective-permute-start.13
  270.7 2.7 collective-permute-done.22.two_ref
  273.3 2.5 collective-permute-done.23.three_ref
  275.9 4.8 %scatter.1 = (f32[64,64]{1,0:T(8,128)}, f32[64,4096]{1,0:T(8,128)}, f32[64,2016]{1,0:T(8,128)}) custom-call(f32[4,64,128]{2,1,0:T(8,128)S(1)} %pad_maximum_fusion.1.own_ref, f32[4,64,128]{2,1,0:T(8,128)S(1)} %collective-permute-done.21.one_ref, f32[4,64,128]{2,1,0:T(8,128)S(1)} %collective-permute-done.22.two_ref, ...), custom_call_target="tpu_custom_call" | custom-call | flops 6000000000 | bytes 4194304 | tf_op jit(solution)/shard_map/scatter/pallas_call | solution.py:392
  (61 shorter events, 8.7 us)
Async XLA Ops:
  1.3 13.7 %collective-permute-start = (f32[8,128]{1,0:T(8,128)S(1)}, f32[8,128]{1,0:T(8,128)S(1)}, u32[]{:S(2)}, u32[]{:S(2)}) collective-permute-start(f32[8,128]{1,0:T(8,128)S(1)} %get-tuple-element.85), channel_id=1, source_target_pairs={{0,16},{8,24},{16,0},{24,8},{32,48},{40,56},{48,32},{56,40},{64,80... | collective-permute-start | bytes 12296 | tf_op jit(solution)/shard_map/ppermute | solution.py:409
  15.0 42.3 %all-to-all-start = ((f32[8,6,4,32,128]{4,3,2,1,0:T(8,128)}), f32[8,6,4,32,128]{4,3,2,1,0:T(8,128)}, u32[]{:S(2)}, u32[]{:S(2)}) async-start(f32[8,6,4,32,128]{4,3,2,1,0:T(8,128)} %bitcast.58), calls=%async_computation | async-start | bytes 6291456 | tf_op jit(solution)/shard_map/all_to_all | solution.py:462
  20.2 2.1 collective-permute-start.1
  22.2 12.7 %collective-permute-start.3 = (f32[4,8,128]{2,1,0:T(8,128)S(1)}, f32[4,8,128]{2,1,0:T(8,128)S(1)}, u32[]{:S(2)}, u32[]{:S(2)}) collective-permute-start(f32[4,8,128]{2,1,0:T(8,128)S(1)} %get-tuple-element.79), channel_id=1, source_target_pairs={{0,64},{8,72},{16,80},{24,88},{32,96},{40,104},{48,112},{56,120},{... | collective-permute-start | bytes 49160 | tf_op jit(solution)/shard_map/ppermute | solution.py:409
  25.0 10.0 %collective-permute-start.4 = (f32[4,8,128]{2,1,0:T(8,128)S(1)}, f32[4,8,128]{2,1,0:T(8,128)S(1)}, u32[]{:S(2)}, u32[]{:S(2)}) collective-permute-start(f32[4,8,128]{2,1,0:T(8,128)S(1)} %get-tuple-element.79), channel_id=1, source_target_pairs={{0,96},{8,104},{16,112},{24,120},{32,64},{40,72},{48,80},{56,88},{... | collective-permute-start | bytes 49160 | tf_op jit(solution)/shard_map/ppermute | solution.py:409
  25.8 9.1 %collective-permute-start.2 = (f32[4,8,128]{2,1,0:T(8,128)S(1)}, f32[4,8,128]{2,1,0:T(8,128)S(1)}, u32[]{:S(2)}, u32[]{:S(2)}) collective-permute-start(f32[4,8,128]{2,1,0:T(8,128)S(1)} %get-tuple-element.79), channel_id=1, source_target_pairs={{0,32},{8,40},{16,48},{24,56},{32,0},{40,8},{48,16},{56,24},{64,96... | collective-permute-start | bytes 49160 | tf_op jit(solution)/shard_map/ppermute | solution.py:409
  57.3 5.1 %copy-start.4 = (bf16[64,2,8192]{2,1,0:T(2,128)(2,1)S(1)}, bf16[64,2,8192]{2,1,0:T(2,128)(2,1)}, u32[]{:S(2)}) copy-start(bf16[64,2,8192]{2,1,0:T(2,128)(2,1)} %w_ref.3) | copy-start | bytes 6291460
  57.3 63.4 %all-to-all-start.2 = ((f32[8,10,4,32,128]{4,3,2,1,0:T(8,128)}), f32[8,10,4,32,128]{4,3,2,1,0:T(8,128)}, u32[]{:S(2)}, u32[]{:S(2)}) async-start(f32[8,10,4,32,128]{4,3,2,1,0:T(8,128)} %bitcast.55), calls=%async_computation.2 | async-start | bytes 10485760 | tf_op jit(solution)/shard_map/all_to_all | solution.py:462
  62.3 2.5 copy-start.6
  62.3 3.5 %copy-start.8 = (bf16[64,128]{1,0:T(8,128)(2,1)S(1)}, bf16[64,128]{1,0:T(8,128)(2,1)}, u32[]{:S(2)}) copy-start(bf16[64,128]{1,0:T(8,128)(2,1)} %get-tuple-element.38) | copy-start | bytes 49156
  120.7 40.8 %all-to-all-start.1 = ((f32[8,6,4,32,128]{4,3,2,1,0:T(8,128)}), f32[8,6,4,32,128]{4,3,2,1,0:T(8,128)}, u32[]{:S(2)}, u32[]{:S(2)}) async-start(f32[8,6,4,32,128]{4,3,2,1,0:T(8,128)} %delay_1.1), calls=%async_computation.1 | async-start | bytes 6291456 | tf_op jit(solution)/shard_map/all_to_all | solution.py:462
  197.5 33.6 %all-to-all-start.4 = ((f32[8,10,4,16,128]{4,3,2,1,0:T(8,128)}), f32[8,10,4,16,128]{4,3,2,1,0:T(8,128)}, u32[]{:S(2)}, u32[]{:S(2)}) async-start(f32[8,10,4,16,128]{4,3,2,1,0:T(8,128)} %get-tuple-element.53), calls=%async_computation.4 | async-start | bytes 5242880 | tf_op jit(solution)/shard_map/all_to_all | solution.py:462
  208.7 5.9 %collective-permute-start.5 = (f32[4,2,8,4096]{3,2,1,0:T(8,128)}, f32[4,2,8,4096]{3,2,1,0:T(8,128)S(1)}, u32[]{:S(2)}, u32[]{:S(2)}) collective-permute-start(f32[4,2,8,4096]{3,2,1,0:T(8,128)} %get-tuple-element.51), channel_id=1, source_target_pairs={{0,8},{8,0},{16,24},{24,16},{32,40},{40,32},{48,56},{56,48},{64,72... | collective-permute-start | bytes 3145736 | tf_op jit(solution)/shard_map/ppermute | solution.py:409
  215.9 1.0 copy-start.5
  217.8 23.7 %collective-permute-start.6 = (f32[2,8,4096]{2,1,0:T(8,128)}, f32[2,8,4096]{2,1,0:T(8,128)S(1)}, u32[]{:S(2)}, u32[]{:S(2)}) collective-permute-start(f32[2,8,4096]{2,1,0:T(8,128)} %get-tuple-element.72), channel_id=1, source_target_pairs={{0,32},{8,40},{16,48},{24,56},{32,64},{40,72},{48,80},{56,88},{64,... | collective-permute-start | bytes 786440 | tf_op jit(solution)/shard_map/ppermute | solution.py:428
  219.0 22.5 %collective-permute-start.7 = (f32[2,8,4096]{2,1,0:T(8,128)}, f32[2,8,4096]{2,1,0:T(8,128)S(1)}, u32[]{:S(2)}, u32[]{:S(2)}) collective-permute-start(f32[2,8,4096]{2,1,0:T(8,128)} %get-tuple-element.74), channel_id=1, source_target_pairs={{0,64},{8,72},{16,80},{24,88},{32,96},{40,104},{48,112},{56,120},{... | collective-permute-start | bytes 786440 | tf_op jit(solution)/shard_map/ppermute | solution.py:428
  221.5 20.0 %collective-permute-start.8 = (f32[2,8,4096]{2,1,0:T(8,128)}, f32[2,8,4096]{2,1,0:T(8,128)S(1)}, u32[]{:S(2)}, u32[]{:S(2)}) collective-permute-start(f32[2,8,4096]{2,1,0:T(8,128)} %get-tuple-element.73), channel_id=1, source_target_pairs={{0,96},{8,104},{16,112},{24,120},{32,0},{40,8},{48,16},{56,24},{64... | collective-permute-start | bytes 786440 | tf_op jit(solution)/shard_map/ppermute | solution.py:428
  237.1 15.8 %copy-start.7 = (f32[64,128]{1,0:T(8,128)S(1)}, f32[64,128]{1,0:T(8,128)}, u32[]{:S(2)}) copy-start(f32[64,128]{1,0:T(8,128)} %get-tuple-element.58) | copy-start | bytes 98308
  237.1 9.4 %collective-permute-start.9 = (f32[4,2,8,4096]{3,2,1,0:T(8,128)}, f32[4,2,8,4096]{3,2,1,0:T(8,128)S(1)}, u32[]{:S(2)}, u32[]{:S(2)}) collective-permute-start(f32[4,2,8,4096]{3,2,1,0:T(8,128)} %get-tuple-element.57), channel_id=1, source_target_pairs={{0,8},{8,0},{16,24},{24,16},{32,40},{40,32},{48,56},{56,48},{64,72... | collective-permute-start | bytes 3145736 | tf_op jit(solution)/shard_map/ppermute | solution.py:409
  242.5 9.2 %collective-permute-start.14 = (f32[64,128]{1,0:T(8,128)}, f32[64,128]{1,0:T(8,128)S(1)}, u32[]{:S(2)}, u32[]{:S(2)}) collective-permute-start(f32[64,128]{1,0:T(8,128)} %get-tuple-element.58), channel_id=1, source_target_pairs={{0,2},{1,3},{2,0},{3,1},{4,6},{5,7},{6,4},{7,5},{8,10},{9,11},{10,... | collective-permute-start | bytes 98312 | tf_op jit(solution)/shard_map/ppermute | solution.py:409
  242.6 10.2 %collective-permute-start.15 = (f32[64,128]{1,0:T(8,128)}, f32[64,128]{1,0:T(8,128)S(1)}, u32[]{:S(2)}, u32[]{:S(2)}) collective-permute-start(f32[64,128]{1,0:T(8,128)} %get-tuple-element.58), channel_id=1, source_target_pairs={{0,4},{1,5},{2,6},{3,7},{4,0},{5,1},{6,2},{7,3},{8,12},{9,13},{10,... | collective-permute-start | bytes 98312 | tf_op jit(solution)/shard_map/ppermute | solution.py:409
  244.4 8.5 %collective-permute-start.16 = (f32[64,128]{1,0:T(8,128)}, f32[64,128]{1,0:T(8,128)S(1)}, u32[]{:S(2)}, u32[]{:S(2)}) collective-permute-start(f32[64,128]{1,0:T(8,128)} %get-tuple-element.58), channel_id=1, source_target_pairs={{0,6},{1,7},{2,4},{3,5},{4,2},{5,3},{6,0},{7,1},{8,14},{9,15},{10,... | collective-permute-start | bytes 98312 | tf_op jit(solution)/shard_map/ppermute | solution.py:409
  246.5 29.4 %copy-start = (bf16[64,64]{1,0:T(8,128)(2,1)S(1)}, bf16[64,64]{1,0:T(8,128)(2,1)}, u32[]{:S(2)}) copy-start(bf16[64,64]{1,0:T(8,128)(2,1)} %w_in_ref.5) | copy-start | bytes 24580
  246.5 29.4 %copy-start.1 = (f32[64,2048]{1,0:T(8,128)S(1)}, f32[64,2048]{1,0:T(8,128)}, u32[]{:S(2)}) copy-start(f32[64,2048]{1,0:T(8,128)} %get-tuple-element.42.slope_ref) | copy-start | bytes 1572868
  246.5 29.4 %copy-start.2 = (bf16[64,2048]{1,0:T(8,128)(2,1)S(1)}, bf16[64,2048]{1,0:T(8,128)(2,1)}, u32[]{:S(2)}) copy-start(bf16[64,2048]{1,0:T(8,128)(2,1)} %get-tuple-element.41.inputs_ref) | copy-start | bytes 786436
  246.5 29.4 %copy-start.3 = (s32[8,2048]{1,0:T(8,128)S(1)}, s32[8,2048]{1,0:T(8,128)}, u32[]{:S(2)}) copy-start(s32[8,2048]{1,0:T(8,128)} %get-tuple-element.43.cells_ref) | copy-start | bytes 196612
  248.0 17.1 %collective-permute-start.10 = (f32[2,8,4096]{2,1,0:T(8,128)S(1)}, f32[2,8,4096]{2,1,0:T(8,128)S(1)}, u32[]{:S(2)}, u32[]{:S(2)}) collective-permute-start(f32[2,8,4096]{2,1,0:T(8,128)S(1)} %get-tuple-element.75), channel_id=1, source_target_pairs={{0,32},{8,40},{16,48},{24,56},{32,64},{40,72},{48,80},{56,88},{64,... | collective-permute-start | bytes 786440 | tf_op jit(solution)/shard_map/ppermute | solution.py:428
  249.2 15.8 %collective-permute-start.11 = (f32[2,8,4096]{2,1,0:T(8,128)S(1)}, f32[2,8,4096]{2,1,0:T(8,128)S(1)}, u32[]{:S(2)}, u32[]{:S(2)}) collective-permute-start(f32[2,8,4096]{2,1,0:T(8,128)S(1)} %get-tuple-element.77), channel_id=1, source_target_pairs={{0,64},{8,72},{16,80},{24,88},{32,96},{40,104},{48,112},{56,120},{... | collective-permute-start | bytes 786440 | tf_op jit(solution)/shard_map/ppermute | solution.py:428
  251.7 13.4 %collective-permute-start.12 = (f32[2,8,4096]{2,1,0:T(8,128)S(1)}, f32[2,8,4096]{2,1,0:T(8,128)S(1)}, u32[]{:S(2)}, u32[]{:S(2)}) collective-permute-start(f32[2,8,4096]{2,1,0:T(8,128)S(1)} %get-tuple-element.76), channel_id=1, source_target_pairs={{0,96},{8,104},{16,112},{24,120},{32,0},{40,8},{48,16},{56,24},{64... | collective-permute-start | bytes 786440 | tf_op jit(solution)/shard_map/ppermute | solution.py:428
  252.9 3.1 %collective-permute-start.17 = (f32[64,128]{1,0:T(8,128)S(1)}, f32[64,128]{1,0:T(8,128)S(1)}, u32[]{:S(2)}, u32[]{:S(2)}) collective-permute-start(f32[64,128]{1,0:T(8,128)S(1)} %add_add_fusion), channel_id=1, source_target_pairs={{0,1},{1,0},{2,3},{3,2},{4,5},{5,4},{6,7},{7,6},{8,9},{9,8},{10,11... | collective-permute-start | bytes 98312 | tf_op jit(solution)/shard_map/ppermute | solution.py:409
  256.0 4.1 %collective-permute-start.18 = (f32[64,128]{1,0:T(8,128)S(1)}, f32[64,128]{1,0:T(8,128)S(1)}, u32[]{:S(2)}, u32[]{:S(2)}) collective-permute-start(f32[64,128]{1,0:T(8,128)S(1)} %add.153), channel_id=1, source_target_pairs={{0,8},{8,0},{16,24},{24,16},{32,40},{40,32},{48,56},{56,48},{64,72... | collective-permute-start | bytes 98312 | tf_op jit(solution)/shard_map/ppermute | solution.py:409
  258.6 4.6 %collective-permute-start.19 = (f32[64,128]{1,0:T(8,128)S(1)}, f32[64,128]{1,0:T(8,128)S(1)}, u32[]{:S(2)}, u32[]{:S(2)}) collective-permute-start(f32[64,128]{1,0:T(8,128)S(1)} %add.153), channel_id=1, source_target_pairs={{0,16},{8,24},{16,0},{24,8},{32,48},{40,56},{48,32},{56,40},{64,80... | collective-permute-start | bytes 98312 | tf_op jit(solution)/shard_map/ppermute | solution.py:409
  260.2 4.9 %collective-permute-start.20 = (f32[64,128]{1,0:T(8,128)S(1)}, f32[64,128]{1,0:T(8,128)S(1)}, u32[]{:S(2)}, u32[]{:S(2)}) collective-permute-start(f32[64,128]{1,0:T(8,128)S(1)} %add.153), channel_id=1, source_target_pairs={{0,24},{8,16},{16,8},{24,0},{32,56},{40,48},{48,40},{56,32},{64,88... | collective-permute-start | bytes 98312 | tf_op jit(solution)/shard_map/ppermute | solution.py:409
  265.2 5.5 %collective-permute-start.21 = (f32[4,64,128]{2,1,0:T(8,128)S(1)}, f32[4,64,128]{2,1,0:T(8,128)S(1)}, u32[]{:S(2)}, u32[]{:S(2)}) collective-permute-start(f32[4,64,128]{2,1,0:T(8,128)S(1)} %pad_maximum_fusion.1.own_ref), channel_id=1, source_target_pairs={{0,32},{8,40},{16,48},{24,56},{32,0},{40,8},{48,16},{56,24},{64,96... | collective-permute-start | bytes 393224 | tf_op jit(solution)/shard_map/ppermute | solution.py:409
  265.6 7.8 %collective-permute-start.22 = (f32[4,64,128]{2,1,0:T(8,128)S(1)}, f32[4,64,128]{2,1,0:T(8,128)S(1)}, u32[]{:S(2)}, u32[]{:S(2)}) collective-permute-start(f32[4,64,128]{2,1,0:T(8,128)S(1)} %pad_maximum_fusion.1.own_ref), channel_id=1, source_target_pairs={{0,64},{8,72},{16,80},{24,88},{32,96},{40,104},{48,112},{56,120},{... | collective-permute-start | bytes 393224 | tf_op jit(solution)/shard_map/ppermute | solution.py:409
  267.4 8.4 %collective-permute-start.23 = (f32[4,64,128]{2,1,0:T(8,128)S(1)}, f32[4,64,128]{2,1,0:T(8,128)S(1)}, u32[]{:S(2)}, u32[]{:S(2)}) collective-permute-start(f32[4,64,128]{2,1,0:T(8,128)S(1)} %pad_maximum_fusion.1.own_ref), channel_id=1, source_target_pairs={{0,96},{8,104},{16,112},{24,120},{32,64},{40,72},{48,80},{56,88},{... | collective-permute-start | bytes 393224 | tf_op jit(solution)/shard_map/ppermute | solution.py:409
  269.2 11.5 %collective-permute-start.13 = (f32[2,4,8192]{2,1,0:T(4,128)S(1)}, f32[2,4,8192]{2,1,0:T(4,128)S(1)}, u32[]{:S(2)}, u32[]{:S(2)}) collective-permute-start(f32[2,4,8192]{2,1,0:T(4,128)S(1)} %pad_maximum_fusion), channel_id=1, source_target_pairs={{0,16},{8,24},{16,0},{24,8},{32,48},{40,56},{48,32},{56,40},{64,80... | collective-permute-start | bytes 786440 | tf_op jit(solution)/shard_map/ppermute | solution.py:409

commit v3 on v2

--- a/solution.py
+++ b/solution.py
@@ -209,7 +209,7 @@
                     start += size
 
 
-def delay_filter(pieces, arrived, constants, weight, count=2):
+def delay_filter(pieces, arrived, constants, weight, count=4):
     members, rows, _, local, _ = arrived.shape
     whole = lambda array: pl.BlockSpec(array.shape, lambda g: (0, 0))
     flops = rows * 4 * 3 * 2 * 512 * 512 * 256
@@ -448,7 +448,7 @@
     rows = uvw_index.shape[0]
     local_blocks = flags.shape[1]
     local_channels = w_out.shape[2]
-    head_rows = rows * 6 // 16
+    head_rows = rows * 4 // 16
 
     taper = jnp.asarray(taper_table()).reshape(members, local_channels)
     hidden, hidden_t, keep, taper = trunk(

time: 283 us -> 281 us (level)
  waiting for transfers between devices: 91.9 us -> 85.8 us
  blocking collectives: 36 us -> 41.4 us
    all_to_all x4, waiting for transfers between devices: 77.6 us -> 71.9 us  [exchange(): lax.all_to_all(values.reshape(members, -1, PLANES, size, LANES), 'ch', 0,...]
    all_to_all x1, blocking collectives: 36 us -> 41.4 us  [exchange(): lax.all_to_all(values.reshape(members, -1, PLANES, size, LANES), 'ch', 0,...]
  transfers between devices with their start and end apart: 28 -> 28, of which waited for: 11 -> 10; matrix products, arithmetic and copies ran while one was open for 4% -> 4% of each run, Pallas kernels for 28% -> 28%
where the time goes in v3:
time: 281 us
  waiting for transfers between devices  85.8 us (31%)
  Pallas kernels  77.2 us (27%)
  starting transfers between devices  62.4 us (22%)
  blocking collectives  41.4 us (15%)
  local copies, waits for them, and re-layouts  6.87 us (2%)
  other arithmetic  5.32 us (2%)
    all_to_all x4, waiting for transfers between devices, exchange(): lax.all_to_all(values.reshape(members, -1, PLANES, size, LANES), 'ch', 0,...  71.9 us
    all_to_all x1, blocking collectives, exchange(): lax.all_to_all(values.reshape(members, -1, PLANES, size, LANES), 'ch', 0,...  41.4 us
    pallas_call x2, Pallas kernels, delay_filter(): pl.pallas_call(functools.partial(delay_kernel, pieces), grid=(rows // cou...  35 us
    ppermute x18, starting transfers between devices, swap(): return lax.ppermute(values, axis, [(i, i ^ distance) for i in range(size)])  32.6 us
    all_to_all x4, starting transfers between devices, exchange(): lax.all_to_all(values.reshape(members, -1, PLANES, size, LANES), 'ch', 0,...  19.7 us
    pallas_call x2, Pallas kernels, residual_part(): pl.pallas_call(functools.partial(residual_kernel, first_row, rows), grid=...  16.2 us
    ppermute x18, waiting for transfers between devices, swap(): return lax.ppermute(values, axis, [(i, i ^ distance) for i in range(size)])  13.8 us
    pallas_call x2, Pallas kernels, tail_part(): pl.pallas_call(functools.partial(tail_kernel, first), grid=(count, 2), in...  11.9 us
  transfers between devices with their start and end apart: 28, of which 10 were waited for; matrix products, arithmetic and copies ran while one was open for 4% of the time, Pallas kernels for 28%

profile of v3, /device:TPU:1, one launch (start us, length us, event | category | flops | bytes accessed | tf_op | source)
XLA Modules:
  0.0 280.6 jit_solution(9442327298358927539)
XLA Ops:
  1.3 3.8 %collective-permute-start = (f32[8,128]{1,0:T(8,128)S(1)}, f32[8,128]{1,0:T(8,128)S(1)}, u32[]{:S(2)}, u32[]{:S(2)}) collective-permute-start(f32[8,128]{1,0:T(8,128)S(1)} %get-tuple-element.85), channel_id=1, source_target_pairs={{0,16},{8,24},{16,0},{24,8},{32,48},{40,56},{48,32},{56,40},{64,80... | collective-permute-start | bytes 12296 | tf_op jit(solution)/shard_map/ppermute | solution.py:409
  5.1 2.6 trunk.1
  7.8 6.4 %residual_0.1 = f32[32,4,32,128]{3,2,1,0:T(8,128)} custom-call(bf16[128,64]{1,0:T(8,128)(2,1)} %get-tuple-element.45.hidden_ref, bf16[64,2,8192]{2,1,0:T(2,128)(2,1)} %w_ref.3, bf16[2,8192,128]{2,1,0:T(8,128)(2,1)} %observed_ref.3, bf16[128,32]{1,0:T(8,128)(2,1)} %get-tuple-element.35.keep_ref, f32[1,8192]{1,0:T(1,128)} %get-tuple-element.36.taper_ref), custom_call_target="tpu_custom_call" | custom-call | flops 201326592 | bytes 10485760 | tf_op jit(solution)/shard_map/residual_0/pallas_call | solution.py:141
  14.2 5.2 %all-to-all-start = ((f32[8,4,4,32,128]{4,3,2,1,0:T(8,128)}), f32[8,4,4,32,128]{4,3,2,1,0:T(8,128)}, u32[]{:S(2)}, u32[]{:S(2)}) async-start(f32[8,4,4,32,128]{4,3,2,1,0:T(8,128)} %bitcast.59), calls=%async_computation | async-start | bytes 4194304 | tf_op jit(solution)/shard_map/all_to_all | solution.py:462
  19.4 1.2 collective-permute-start.1
  21.4 2.7 collective-permute-start.3
  25.0 9.8 %residual_32.1 = f32[96,4,32,128]{3,2,1,0:T(8,128)} custom-call(bf16[128,64]{1,0:T(8,128)(2,1)} %get-tuple-element.45.hidden_ref, bf16[64,2,8192]{2,1,0:T(2,128)(2,1)} %w_ref.3, bf16[2,8192,128]{2,1,0:T(8,128)(2,1)} %observed_ref.3, bf16[128,32]{1,0:T(8,128)(2,1)} %get-tuple-element.35.keep_ref, f32[1,8192]{1,0:T(1,128)} %get-tuple-element.36.taper_ref), custom_call_target="tpu_custom_call" | custom-call | flops 603979776 | bytes 10485760 | tf_op jit(solution)/shard_map/residual_32/pallas_call | solution.py:141
  35.5 9.7 %all-to-all-done.x_ref = f32[8,4,4,32,128]{4,3,2,1,0:T(8,128)} async-done(((f32[8,4,4,32,128]{4,3,2,1,0:T(8,128)}), f32[8,4,4,32,128]{4,3,2,1,0:T(8,128)}, u32[]{:S(2)}, u32[]{:S(2)}) %all-to-all-start) | async-done | bytes 2097184 | tf_op jit(solution)/shard_map/all_to_all | solution.py:462
  45.3 5.1 %all-to-all-start.2 = ((f32[8,12,4,32,128]{4,3,2,1,0:T(8,128)}), f32[8,12,4,32,128]{4,3,2,1,0:T(8,128)}, u32[]{:S(2)}, u32[]{:S(2)}) async-start(f32[8,12,4,32,128]{4,3,2,1,0:T(8,128)} %bitcast.55), calls=%async_computation.2 | async-start | bytes 12582912 | tf_op jit(solution)/shard_map/all_to_all | solution.py:462
  50.4 2.5 copy.26
  54.6 10.6 %delay_1.1 = f32[8,4,4,32,128]{4,3,2,1,0:T(8,128)} custom-call(f32[8,4,4,32,128]{4,3,2,1,0:T(8,128)} %all-to-all-done.x_ref, bf16[512,512]{1,0:T(8,128)(2,1)} %constant.128.clone.fh_ref, bf16[512,512]{1,0:T(8,128)(2,1)} %constant.129.clone.fl_ref, bf16[512,512]{1,0:T(8,128)(2,1)} %constant.130.clone.bh_ref, bf16[512,512]{1,0:T(8,128)(2,1)} %constant.131.clone.bl_ref, ...), custom_call_target="tpu_custom_call" | custom-call | flops 6442450944 | bytes 12582912 | tf_op jit(solution)/shard_map/delay_1/pallas_call | solution.py:216
  65.2 6.6 %all_rows.1 = (bf16[64,2048]{1,0:T(8,128)(2,1)}, f32[64,2048]{1,0:T(8,128)}, s32[8,2048]{1,0:T(8,128)}) custom-call(f32[4,4,8,128]{3,2,1,0:T(8,128)} %pad_maximum_fusion.2.index_ref, bf16[64,4096]{1,0:T(8,128)(2,1)} %table_ref.3, bf16[64,2016]{1,0:T(8,128)(2,1)} %features_ref.3, bf16[64,64]{1,0:T(8,128)(2,1)} %w_in_ref.5), custom_call_target="tpu_custom_call" | custom-call | flops 6000000000 | bytes 1048576 | tf_op jit(solution)/shard_map/all_rows/pallas_call | solution.py:343
  71.8 48.2 %all-to-all-done.2.x_ref = f32[8,12,4,32,128]{4,3,2,1,0:T(8,128)} async-done(((f32[8,12,4,32,128]{4,3,2,1,0:T(8,128)}), f32[8,12,4,32,128]{4,3,2,1,0:T(8,128)}, u32[]{:S(2)}, u32[]{:S(2)}) %all-to-all-start.2) | async-done | bytes 6291488 | tf_op jit(solution)/shard_map/all_to_all | solution.py:462
  120.0 5.0 %all-to-all-start.1 = ((f32[8,4,4,32,128]{4,3,2,1,0:T(8,128)}), f32[8,4,4,32,128]{4,3,2,1,0:T(8,128)}, u32[]{:S(2)}, u32[]{:S(2)}) async-start(f32[8,4,4,32,128]{4,3,2,1,0:T(8,128)} %delay_1.1), calls=%async_computation.1 | async-start | bytes 4194304 | tf_op jit(solution)/shard_map/all_to_all | solution.py:462
  124.9 24.4 %delay_2.1 = (f32[8,12,4,16,128]{4,3,2,1,0:T(8,128)}, f32[8,12,4,16,128]{4,3,2,1,0:T(8,128)}) custom-call(f32[8,12,4,32,128]{4,3,2,1,0:T(8,128)} %all-to-all-done.2.x_ref, bf16[512,512]{1,0:T(8,128)(2,1)} %constant.128.clone.fh_ref, bf16[512,512]{1,0:T(8,128)(2,1)} %constant.129.clone.fl_ref, bf16[512,512]{1,0:T(8,128)(2,1)} %constant.130.clone.bh_ref, ...), custom_call_target="tpu_custom_call" | custom-call | flops 19327352832 | bytes 12582912 | tf_op jit(solution)/shard_map/delay_2/pallas_call | solution.py:216
  149.3 41.4 %all_to_all.25 = f32[8,12,4,16,128]{4,3,2,1,0:T(8,128)} all-to-all(f32[8,12,4,16,128]{4,3,2,1,0:T(8,128)} %get-tuple-element.49), channel_id=1, replica_groups=mesh['bl'=16,'ch'=8] {'ch'}, dimensions={0} | all-to-all | bytes 6291456 | tf_op jit(solution)/shard_map/all_to_all | solution.py:462
  190.7 4.5 %all-to-all-start.4 = ((f32[8,12,4,16,128]{4,3,2,1,0:T(8,128)}), f32[8,12,4,16,128]{4,3,2,1,0:T(8,128)}, u32[]{:S(2)}, u32[]{:S(2)}) async-start(f32[8,12,4,16,128]{4,3,2,1,0:T(8,128)} %get-tuple-element.53), calls=%async_computation.4 | async-start | bytes 6291456 | tf_op jit(solution)/shard_map/all_to_all | solution.py:462
  195.8 5.9 %tail_0.1 = (f32[4,2,8,4096]{3,2,1,0:T(8,128)}, f32[4,2,8,4096]{3,2,1,0:T(8,128)}, f32[64,128]{1,0:T(8,128)}) custom-call(f32[32,4,32,128]{3,2,1,0:T(8,128)} %bitcast.12.g1_ref, f32[96,4,16,128]{3,2,1,0:T(8,128)} %bitcast.58, bf16[64,128]{1,0:T(8,128)(2,1)} %convolution_convert_fusion.hidden_ref, bf16[2,64,8192]{2,1,0:T(8,128)(2,1)} %bitcast.56, ...), custom_call_target="tpu_custom_call" | custom-call | flops 268435456 | bytes 8388608 | tf_op jit(solution)/shard_map/tail_0/pallas_call | solution.py:277
  201.7 3.5 %collective-permute-start.5 = (f32[4,2,8,4096]{3,2,1,0:T(8,128)}, f32[4,2,8,4096]{3,2,1,0:T(8,128)S(1)}, u32[]{:S(2)}, u32[]{:S(2)}) collective-permute-start(f32[4,2,8,4096]{3,2,1,0:T(8,128)} %get-tuple-element.51), channel_id=1, source_target_pairs={{0,8},{8,0},{16,24},{24,16},{32,40},{40,32},{48,56},{56,48},{64,72... | collective-permute-start | bytes 3145736 | tf_op jit(solution)/shard_map/ppermute | solution.py:409
  205.3 2.5 collective-permute-done.5
  207.8 1.3 add.141
  209.1 1.0 copy-done.5
  211.0 1.2 collective-permute-start.6
  212.2 2.6 collective-permute-start.7
  214.7 1.2 collective-permute-start.8
  216.0 14.0 %all-to-all-done.4 = f32[8,12,4,16,128]{4,3,2,1,0:T(8,128)} async-done(((f32[8,12,4,16,128]{4,3,2,1,0:T(8,128)}), f32[8,12,4,16,128]{4,3,2,1,0:T(8,128)}, u32[]{:S(2)}, u32[]{:S(2)}) %all-to-all-start.4) | async-done | bytes 3145760 | tf_op jit(solution)/shard_map/all_to_all | solution.py:462
  230.0 6.0 %tail_2.1 = (f32[4,2,8,4096]{3,2,1,0:T(8,128)}, f32[4,2,8,4096]{3,2,1,0:T(8,128)}, f32[64,128]{1,0:T(8,128)}) custom-call(f32[32,4,32,128]{3,2,1,0:T(8,128)} %bitcast.12.g1_ref, f32[96,4,16,128]{3,2,1,0:T(8,128)} %bitcast.19.g2_ref, bf16[64,128]{1,0:T(8,128)(2,1)} %convolution_convert_fusion.hidden_ref, bf16[2,64,8192]{2,1,0:T(8,128)(2,1)} %bitcast.57, ...), custom_call_target="tpu_custom_call" | custom-call | flops 268435456 | bytes 8388608 | tf_op jit(solution)/shard_map/tail_2/pallas_call | solution.py:277
  236.0 4.5 %collective-permute-start.9 = (f32[4,2,8,4096]{3,2,1,0:T(8,128)}, f32[4,2,8,4096]{3,2,1,0:T(8,128)S(1)}, u32[]{:S(2)}, u32[]{:S(2)}) collective-permute-start(f32[4,2,8,4096]{3,2,1,0:T(8,128)} %get-tuple-element.57), channel_id=1, source_target_pairs={{0,8},{8,0},{16,24},{24,16},{32,40},{40,32},{48,56},{56,48},{64,72... | collective-permute-start | bytes 3145736 | tf_op jit(solution)/shard_map/ppermute | solution.py:409
  240.5 1.0 fusion.8
  241.6 1.7 collective-permute-start.15
  243.2 2.2 collective-permute-start.16
  245.4 1.4 add.145
  246.9 1.3 collective-permute-start.10
  248.2 2.6 collective-permute-start.11
  250.8 1.3 collective-permute-start.12
  252.6 2.5 collective-permute-done.17
  255.2 2.6 collective-permute-start.18
  257.8 1.3 collective-permute-start.19
  259.1 1.9 collective-permute-start.20
  261.0 1.4 collective-permute-done.19
  262.3 1.6 collective-permute-done.20
  264.6 1.7 collective-permute-start.22
  266.4 1.7 collective-permute-start.23
  268.1 1.7 collective-permute-start.13
  269.8 2.5 collective-permute-done.22.two_ref
  272.3 2.5 collective-permute-done.23.three_ref
  274.8 4.8 %scatter.1 = (f32[64,64]{1,0:T(8,128)}, f32[64,4096]{1,0:T(8,128)}, f32[64,2016]{1,0:T(8,128)}) custom-call(f32[4,64,128]{2,1,0:T(8,128)S(1)} %pad_maximum_fusion.1.own_ref, f32[4,64,128]{2,1,0:T(8,128)S(1)} %collective-permute-done.21.one_ref, f32[4,64,128]{2,1,0:T(8,128)S(1)} %collective-permute-done.22.two_ref, ...), custom_call_target="tpu_custom_call" | custom-call | flops 6000000000 | bytes 4194304 | tf_op jit(solution)/shard_map/scatter/pallas_call | solution.py:392
  279.7 0.9 copy.24
  (61 shorter events, 7.8 us)
Async XLA Ops:
  1.3 12.9 %collective-permute-start = (f32[8,128]{1,0:T(8,128)S(1)}, f32[8,128]{1,0:T(8,128)S(1)}, u32[]{:S(2)}, u32[]{:S(2)}) collective-permute-start(f32[8,128]{1,0:T(8,128)S(1)} %get-tuple-element.85), channel_id=1, source_target_pairs={{0,16},{8,24},{16,0},{24,8},{32,48},{40,56},{48,32},{56,40},{64,80... | collective-permute-start | bytes 12296 | tf_op jit(solution)/shard_map/ppermute | solution.py:409
  14.2 31.0 %all-to-all-start = ((f32[8,4,4,32,128]{4,3,2,1,0:T(8,128)}), f32[8,4,4,32,128]{4,3,2,1,0:T(8,128)}, u32[]{:S(2)}, u32[]{:S(2)}) async-start(f32[8,4,4,32,128]{4,3,2,1,0:T(8,128)} %bitcast.59), calls=%async_computation | async-start | bytes 4194304 | tf_op jit(solution)/shard_map/all_to_all | solution.py:462
  19.4 2.1 collective-permute-start.1
  21.4 13.4 %collective-permute-start.3 = (f32[4,8,128]{2,1,0:T(8,128)S(1)}, f32[4,8,128]{2,1,0:T(8,128)S(1)}, u32[]{:S(2)}, u32[]{:S(2)}) collective-permute-start(f32[4,8,128]{2,1,0:T(8,128)S(1)} %get-tuple-element.79), channel_id=1, source_target_pairs={{0,64},{8,72},{16,80},{24,88},{32,96},{40,104},{48,112},{56,120},{... | collective-permute-start | bytes 49160 | tf_op jit(solution)/shard_map/ppermute | solution.py:409
  24.2 10.7 %collective-permute-start.4 = (f32[4,8,128]{2,1,0:T(8,128)S(1)}, f32[4,8,128]{2,1,0:T(8,128)S(1)}, u32[]{:S(2)}, u32[]{:S(2)}) collective-permute-start(f32[4,8,128]{2,1,0:T(8,128)S(1)} %get-tuple-element.79), channel_id=1, source_target_pairs={{0,96},{8,104},{16,112},{24,120},{32,64},{40,72},{48,80},{56,88},{... | collective-permute-start | bytes 49160 | tf_op jit(solution)/shard_map/ppermute | solution.py:409
  25.0 9.8 %collective-permute-start.2 = (f32[4,8,128]{2,1,0:T(8,128)S(1)}, f32[4,8,128]{2,1,0:T(8,128)S(1)}, u32[]{:S(2)}, u32[]{:S(2)}) collective-permute-start(f32[4,8,128]{2,1,0:T(8,128)S(1)} %get-tuple-element.79), channel_id=1, source_target_pairs={{0,32},{8,40},{16,48},{24,56},{32,0},{40,8},{48,16},{56,24},{64,96... | collective-permute-start | bytes 49160 | tf_op jit(solution)/shard_map/ppermute | solution.py:409
  45.3 5.1 %copy-start.4 = (bf16[64,2,8192]{2,1,0:T(2,128)(2,1)S(1)}, bf16[64,2,8192]{2,1,0:T(2,128)(2,1)}, u32[]{:S(2)}) copy-start(bf16[64,2,8192]{2,1,0:T(2,128)(2,1)} %w_ref.3) | copy-start | bytes 6291460
  45.3 74.7 %all-to-all-start.2 = ((f32[8,12,4,32,128]{4,3,2,1,0:T(8,128)}), f32[8,12,4,32,128]{4,3,2,1,0:T(8,128)}, u32[]{:S(2)}, u32[]{:S(2)}) async-start(f32[8,12,4,32,128]{4,3,2,1,0:T(8,128)} %bitcast.55), calls=%async_computation.2 | async-start | bytes 12582912 | tf_op jit(solution)/shard_map/all_to_all | solution.py:462
  50.3 2.5 copy-start.6
  50.3 3.5 %copy-start.8 = (bf16[64,128]{1,0:T(8,128)(2,1)S(1)}, bf16[64,128]{1,0:T(8,128)(2,1)}, u32[]{:S(2)}) copy-start(bf16[64,128]{1,0:T(8,128)(2,1)} %get-tuple-element.38) | copy-start | bytes 49156
  120.0 29.4 %all-to-all-start.1 = ((f32[8,4,4,32,128]{4,3,2,1,0:T(8,128)}), f32[8,4,4,32,128]{4,3,2,1,0:T(8,128)}, u32[]{:S(2)}, u32[]{:S(2)}) async-start(f32[8,4,4,32,128]{4,3,2,1,0:T(8,128)} %delay_1.1), calls=%async_computation.1 | async-start | bytes 4194304 | tf_op jit(solution)/shard_map/all_to_all | solution.py:462
  190.7 39.3 %all-to-all-start.4 = ((f32[8,12,4,16,128]{4,3,2,1,0:T(8,128)}), f32[8,12,4,16,128]{4,3,2,1,0:T(8,128)}, u32[]{:S(2)}, u32[]{:S(2)}) async-start(f32[8,12,4,16,128]{4,3,2,1,0:T(8,128)} %get-tuple-element.53), calls=%async_computation.4 | async-start | bytes 6291456 | tf_op jit(solution)/shard_map/all_to_all | solution.py:462
  201.7 6.0 %collective-permute-start.5 = (f32[4,2,8,4096]{3,2,1,0:T(8,128)}, f32[4,2,8,4096]{3,2,1,0:T(8,128)S(1)}, u32[]{:S(2)}, u32[]{:S(2)}) collective-permute-start(f32[4,2,8,4096]{3,2,1,0:T(8,128)} %get-tuple-element.51), channel_id=1, source_target_pairs={{0,8},{8,0},{16,24},{24,16},{32,40},{40,32},{48,56},{56,48},{64,72... | collective-permute-start | bytes 3145736 | tf_op jit(solution)/shard_map/ppermute | solution.py:409
  209.1 1.0 copy-start.5
  211.0 29.5 %collective-permute-start.6 = (f32[2,8,4096]{2,1,0:T(8,128)}, f32[2,8,4096]{2,1,0:T(8,128)S(1)}, u32[]{:S(2)}, u32[]{:S(2)}) collective-permute-start(f32[2,8,4096]{2,1,0:T(8,128)} %get-tuple-element.72), channel_id=1, source_target_pairs={{0,32},{8,40},{16,48},{24,56},{32,64},{40,72},{48,80},{56,88},{64,... | collective-permute-start | bytes 786440 | tf_op jit(solution)/shard_map/ppermute | solution.py:428
  212.2 28.3 %collective-permute-start.7 = (f32[2,8,4096]{2,1,0:T(8,128)}, f32[2,8,4096]{2,1,0:T(8,128)S(1)}, u32[]{:S(2)}, u32[]{:S(2)}) collective-permute-start(f32[2,8,4096]{2,1,0:T(8,128)} %get-tuple-element.74), channel_id=1, source_target_pairs={{0,64},{8,72},{16,80},{24,88},{32,96},{40,104},{48,112},{56,120},{... | collective-permute-start | bytes 786440 | tf_op jit(solution)/shard_map/ppermute | solution.py:428
  214.7 25.7 %collective-permute-start.8 = (f32[2,8,4096]{2,1,0:T(8,128)}, f32[2,8,4096]{2,1,0:T(8,128)S(1)}, u32[]{:S(2)}, u32[]{:S(2)}) collective-permute-start(f32[2,8,4096]{2,1,0:T(8,128)} %get-tuple-element.73), channel_id=1, source_target_pairs={{0,96},{8,104},{16,112},{24,120},{32,0},{40,8},{48,16},{56,24},{64... | collective-permute-start | bytes 786440 | tf_op jit(solution)/shard_map/ppermute | solution.py:428
  236.0 16.0 %copy-start.7 = (f32[64,128]{1,0:T(8,128)S(1)}, f32[64,128]{1,0:T(8,128)}, u32[]{:S(2)}) copy-start(f32[64,128]{1,0:T(8,128)} %get-tuple-element.58) | copy-start | bytes 98308
  236.0 9.4 %collective-permute-start.9 = (f32[4,2,8,4096]{3,2,1,0:T(8,128)}, f32[4,2,8,4096]{3,2,1,0:T(8,128)S(1)}, u32[]{:S(2)}, u32[]{:S(2)}) collective-permute-start(f32[4,2,8,4096]{3,2,1,0:T(8,128)} %get-tuple-element.57), channel_id=1, source_target_pairs={{0,8},{8,0},{16,24},{24,16},{32,40},{40,32},{48,56},{56,48},{64,72... | collective-permute-start | bytes 3145736 | tf_op jit(solution)/shard_map/ppermute | solution.py:409
  241.5 9.3 %collective-permute-start.14 = (f32[64,128]{1,0:T(8,128)}, f32[64,128]{1,0:T(8,128)S(1)}, u32[]{:S(2)}, u32[]{:S(2)}) collective-permute-start(f32[64,128]{1,0:T(8,128)} %get-tuple-element.58), channel_id=1, source_target_pairs={{0,2},{1,3},{2,0},{3,1},{4,6},{5,7},{6,4},{7,5},{8,10},{9,11},{10,... | collective-permute-start | bytes 98312 | tf_op jit(solution)/shard_map/ppermute | solution.py:409
  241.6 10.5 %collective-permute-start.15 = (f32[64,128]{1,0:T(8,128)}, f32[64,128]{1,0:T(8,128)S(1)}, u32[]{:S(2)}, u32[]{:S(2)}) collective-permute-start(f32[64,128]{1,0:T(8,128)} %get-tuple-element.58), channel_id=1, source_target_pairs={{0,4},{1,5},{2,6},{3,7},{4,0},{5,1},{6,2},{7,3},{8,12},{9,13},{10,... | collective-permute-start | bytes 98312 | tf_op jit(solution)/shard_map/ppermute | solution.py:409
  243.2 8.8 %collective-permute-start.16 = (f32[64,128]{1,0:T(8,128)}, f32[64,128]{1,0:T(8,128)S(1)}, u32[]{:S(2)}, u32[]{:S(2)}) collective-permute-start(f32[64,128]{1,0:T(8,128)} %get-tuple-element.58), channel_id=1, source_target_pairs={{0,6},{1,7},{2,4},{3,5},{4,2},{5,3},{6,0},{7,1},{8,14},{9,15},{10,... | collective-permute-start | bytes 98312 | tf_op jit(solution)/shard_map/ppermute | solution.py:409
  245.4 29.4 %copy-start = (bf16[64,64]{1,0:T(8,128)(2,1)S(1)}, bf16[64,64]{1,0:T(8,128)(2,1)}, u32[]{:S(2)}) copy-start(bf16[64,64]{1,0:T(8,128)(2,1)} %w_in_ref.5) | copy-start | bytes 24580
  245.4 29.4 %copy-start.1 = (f32[64,2048]{1,0:T(8,128)S(1)}, f32[64,2048]{1,0:T(8,128)}, u32[]{:S(2)}) copy-start(f32[64,2048]{1,0:T(8,128)} %get-tuple-element.42.slope_ref) | copy-start | bytes 1572868
  245.4 29.4 %copy-start.2 = (bf16[64,2048]{1,0:T(8,128)(2,1)S(1)}, bf16[64,2048]{1,0:T(8,128)(2,1)}, u32[]{:S(2)}) copy-start(bf16[64,2048]{1,0:T(8,128)(2,1)} %get-tuple-element.41.inputs_ref) | copy-start | bytes 786436
  245.4 29.4 %copy-start.3 = (s32[8,2048]{1,0:T(8,128)S(1)}, s32[8,2048]{1,0:T(8,128)}, u32[]{:S(2)}) copy-start(s32[8,2048]{1,0:T(8,128)} %get-tuple-element.43.cells_ref) | copy-start | bytes 196612
  246.9 17.1 %collective-permute-start.10 = (f32[2,8,4096]{2,1,0:T(8,128)S(1)}, f32[2,8,4096]{2,1,0:T(8,128)S(1)}, u32[]{:S(2)}, u32[]{:S(2)}) collective-permute-start(f32[2,8,4096]{2,1,0:T(8,128)S(1)} %get-tuple-element.75), channel_id=1, source_target_pairs={{0,32},{8,40},{16,48},{24,56},{32,64},{40,72},{48,80},{56,88},{64,... | collective-permute-start | bytes 786440 | tf_op jit(solution)/shard_map/ppermute | solution.py:428
  248.2 15.8 %collective-permute-start.11 = (f32[2,8,4096]{2,1,0:T(8,128)S(1)}, f32[2,8,4096]{2,1,0:T(8,128)S(1)}, u32[]{:S(2)}, u32[]{:S(2)}) collective-permute-start(f32[2,8,4096]{2,1,0:T(8,128)S(1)} %get-tuple-element.77), channel_id=1, source_target_pairs={{0,64},{8,72},{16,80},{24,88},{32,96},{40,104},{48,112},{56,120},{... | collective-permute-start | bytes 786440 | tf_op jit(solution)/shard_map/ppermute | solution.py:428
  250.8 13.2 %collective-permute-start.12 = (f32[2,8,4096]{2,1,0:T(8,128)S(1)}, f32[2,8,4096]{2,1,0:T(8,128)S(1)}, u32[]{:S(2)}, u32[]{:S(2)}) collective-permute-start(f32[2,8,4096]{2,1,0:T(8,128)S(1)} %get-tuple-element.76), channel_id=1, source_target_pairs={{0,96},{8,104},{16,112},{24,120},{32,0},{40,8},{48,16},{56,24},{64... | collective-permute-start | bytes 786440 | tf_op jit(solution)/shard_map/ppermute | solution.py:428
  252.0 3.1 %collective-permute-start.17 = (f32[64,128]{1,0:T(8,128)S(1)}, f32[64,128]{1,0:T(8,128)S(1)}, u32[]{:S(2)}, u32[]{:S(2)}) collective-permute-start(f32[64,128]{1,0:T(8,128)S(1)} %add_add_fusion), channel_id=1, source_target_pairs={{0,1},{1,0},{2,3},{3,2},{4,5},{5,4},{6,7},{7,6},{8,9},{9,8},{10,11... | collective-permute-start | bytes 98312 | tf_op jit(solution)/shard_map/ppermute | solution.py:409
  255.2 3.9 %collective-permute-start.18 = (f32[64,128]{1,0:T(8,128)S(1)}, f32[64,128]{1,0:T(8,128)S(1)}, u32[]{:S(2)}, u32[]{:S(2)}) collective-permute-start(f32[64,128]{1,0:T(8,128)S(1)} %add.153), channel_id=1, source_target_pairs={{0,8},{8,0},{16,24},{24,16},{32,40},{40,32},{48,56},{56,48},{64,72... | collective-permute-start | bytes 98312 | tf_op jit(solution)/shard_map/ppermute | solution.py:409
  257.8 4.6 %collective-permute-start.19 = (f32[64,128]{1,0:T(8,128)S(1)}, f32[64,128]{1,0:T(8,128)S(1)}, u32[]{:S(2)}, u32[]{:S(2)}) collective-permute-start(f32[64,128]{1,0:T(8,128)S(1)} %add.153), channel_id=1, source_target_pairs={{0,16},{8,24},{16,0},{24,8},{32,48},{40,56},{48,32},{56,40},{64,80... | collective-permute-start | bytes 98312 | tf_op jit(solution)/shard_map/ppermute | solution.py:409
  259.1 4.9 %collective-permute-start.20 = (f32[64,128]{1,0:T(8,128)S(1)}, f32[64,128]{1,0:T(8,128)S(1)}, u32[]{:S(2)}, u32[]{:S(2)}) collective-permute-start(f32[64,128]{1,0:T(8,128)S(1)} %add.153), channel_id=1, source_target_pairs={{0,24},{8,16},{16,8},{24,0},{32,56},{40,48},{48,40},{56,32},{64,88... | collective-permute-start | bytes 98312 | tf_op jit(solution)/shard_map/ppermute | solution.py:409
  264.1 5.7 %collective-permute-start.21 = (f32[4,64,128]{2,1,0:T(8,128)S(1)}, f32[4,64,128]{2,1,0:T(8,128)S(1)}, u32[]{:S(2)}, u32[]{:S(2)}) collective-permute-start(f32[4,64,128]{2,1,0:T(8,128)S(1)} %pad_maximum_fusion.1.own_ref), channel_id=1, source_target_pairs={{0,32},{8,40},{16,48},{24,56},{32,0},{40,8},{48,16},{56,24},{64,96... | collective-permute-start | bytes 393224 | tf_op jit(solution)/shard_map/ppermute | solution.py:409
  264.6 7.7 %collective-permute-start.22 = (f32[4,64,128]{2,1,0:T(8,128)S(1)}, f32[4,64,128]{2,1,0:T(8,128)S(1)}, u32[]{:S(2)}, u32[]{:S(2)}) collective-permute-start(f32[4,64,128]{2,1,0:T(8,128)S(1)} %pad_maximum_fusion.1.own_ref), channel_id=1, source_target_pairs={{0,64},{8,72},{16,80},{24,88},{32,96},{40,104},{48,112},{56,120},{... | collective-permute-start | bytes 393224 | tf_op jit(solution)/shard_map/ppermute | solution.py:409
  266.4 8.4 %collective-permute-start.23 = (f32[4,64,128]{2,1,0:T(8,128)S(1)}, f32[4,64,128]{2,1,0:T(8,128)S(1)}, u32[]{:S(2)}, u32[]{:S(2)}) collective-permute-start(f32[4,64,128]{2,1,0:T(8,128)S(1)} %pad_maximum_fusion.1.own_ref), channel_id=1, source_target_pairs={{0,96},{8,104},{16,112},{24,120},{32,64},{40,72},{48,80},{56,88},{... | collective-permute-start | bytes 393224 | tf_op jit(solution)/shard_map/ppermute | solution.py:409
  268.1 11.5 %collective-permute-start.13 = (f32[2,4,8192]{2,1,0:T(4,128)S(1)}, f32[2,4,8192]{2,1,0:T(4,128)S(1)}, u32[]{:S(2)}, u32[]{:S(2)}) collective-permute-start(f32[2,4,8192]{2,1,0:T(4,128)S(1)} %pad_maximum_fusion), channel_id=1, source_target_pairs={{0,16},{8,24},{16,0},{24,8},{32,48},{40,56},{48,32},{56,40},{64,80... | collective-permute-start | bytes 786440 | tf_op jit(solution)/shard_map/ppermute | solution.py:409

commit v4 on v3

--- a/solution.py
+++ b/solution.py
@@ -72,7 +72,9 @@
 
 
 def trunk_kernel(uvw_ref, base_ref, flags_ref, table_ref, features_ref, w_in_ref, taper_ref,
-                 hidden_ref, hidden_t_ref, keep_ref, taper_here_ref):
+                 hidden_ref, hidden_t_ref, keep_ref, taper_here_ref, index_ref):
+    pair = jnp.concatenate([uvw_ref[...], base_ref[...]], axis=0).astype(F32)
+    index_ref[...] = jnp.concatenate([pair] * 4, axis=0)
     taper_here_ref[...] = taper_ref[pl.ds(lax.axis_index("ch"), 1), :]
     summed = dot(table_ref[...], one_hot_rows(uvw_ref[...], table_ref.shape[1]))
     summed = summed + dot(features_ref[...], one_hot_rows(base_ref[...], features_ref.shape[1]))
@@ -94,6 +96,7 @@
             jax.ShapeDtypeStruct((rows, units), BF16),
             jax.ShapeDtypeStruct(flags.shape, BF16),
             jax.ShapeDtypeStruct((1, taper.shape[1]), F32),
+            jax.ShapeDtypeStruct((8, rows), F32),
         ),
         compiler_params=params(),
         name="trunk",
@@ -451,7 +454,7 @@
     head_rows = rows * 4 // 16
 
     taper = jnp.asarray(taper_table()).reshape(members, local_channels)
-    hidden, hidden_t, keep, taper = trunk(
+    hidden, hidden_t, keep, taper, index = trunk(
         uvw_index, row_baseline, flags, uvw_table, baseline_features, w_in, taper
     )
     constants = [jnp.asarray(table) for table in tables()]
@@ -468,8 +471,6 @@
 
     part = residual_part(0, head_rows, hidden_t, w_out, observed, keep, taper)
     hidden_t = after(hidden_t, part)
-    index = jnp.stack([uvw_index, row_baseline]).astype(F32)
-    index = jnp.concatenate([index, jnp.zeros((6, rows), F32)], axis=0)
     index = jnp.stack([index, swap(index, "bl", 2)])
     sent_0 = exchange(after(part, index))
     index = after(index, part)

time: 281 us -> 281 us (level)
  transfers between devices with their start and end apart: 28 -> 28, of which waited for: 10 -> 10; matrix products, arithmetic and copies ran while one was open for 4% -> 4% of each run, Pallas kernels for 28% -> 27%
where the time goes in v4:
time: 281 us; the launch traced here: 280 us
  waiting for transfers between devices  86.3 us (31%)
  Pallas kernels  77.2 us (27%)
  starting transfers between devices  61.7 us (22%)
  blocking collectives  41.5 us (15%)
  local copies, waits for them, and re-layouts  6.87 us (2%)
  other arithmetic  4.64 us (2%)
    all_to_all x4, waiting for transfers between devices, exchange(): lax.all_to_all(values.reshape(members, -1, PLANES, size, LANES), 'ch', 0,...  72.1 us
    all_to_all x1, blocking collectives, exchange(): lax.all_to_all(values.reshape(members, -1, PLANES, size, LANES), 'ch', 0,...  41.5 us
    pallas_call x2, Pallas kernels, delay_filter(): pl.pallas_call(functools.partial(delay_kernel, pieces), grid=(rows // cou...  35 us
    ppermute x18, starting transfers between devices, swap(): return lax.ppermute(values, axis, [(i, i ^ distance) for i in range(size)])  32.4 us
    all_to_all x4, starting transfers between devices, exchange(): lax.all_to_all(values.reshape(members, -1, PLANES, size, LANES), 'ch', 0,...  19.7 us
    pallas_call x2, Pallas kernels, residual_part(): pl.pallas_call(functools.partial(residual_kernel, first_row, rows), grid=...  16.2 us
    ppermute x18, waiting for transfers between devices, swap(): return lax.ppermute(values, axis, [(i, i ^ distance) for i in range(size)])  14.2 us
    pallas_call x2, Pallas kernels, tail_part(): pl.pallas_call(functools.partial(tail_kernel, first), grid=(count, 2), in...  11.9 us
  transfers between devices with their start and end apart: 28, of which 10 were waited for; matrix products, arithmetic and copies ran while one was open for 4% of the time, Pallas kernels for 27%

profile of v4, /device:TPU:1, one launch (start us, length us, event | category | flops | bytes accessed | tf_op | source)
XLA Modules:
  0.0 280.0 jit_solution(12305532412192609927)
XLA Ops:
  0.6 2.7 trunk.1
  3.3 3.7 %collective-permute-start = (f32[8,128]{1,0:T(8,128)}, f32[8,128]{1,0:T(8,128)S(1)}, u32[]{:S(2)}, u32[]{:S(2)}) collective-permute-start(f32[8,128]{1,0:T(8,128)} %get-tuple-element.38), channel_id=1, source_target_pairs={{0,16},{8,24},{16,0},{24,8},{32,48},{40,56},{48,32},{56,40},{64,80... | collective-permute-start | bytes 12296 | tf_op jit(solution)/shard_map/ppermute | solution.py:412
  7.0 6.4 %residual_0.1 = f32[32,4,32,128]{3,2,1,0:T(8,128)} custom-call(bf16[128,64]{1,0:T(8,128)(2,1)} %get-tuple-element.47.hidden_ref, bf16[64,2,8192]{2,1,0:T(2,128)(2,1)} %w_ref.3, bf16[2,8192,128]{2,1,0:T(8,128)(2,1)} %observed_ref.3, bf16[128,32]{1,0:T(8,128)(2,1)} %get-tuple-element.36.keep_ref, f32[1,8192]{1,0:T(1,128)} %get-tuple-element.37.taper_ref), custom_call_target="tpu_custom_call" | custom-call | flops 201326592 | bytes 10485760 | tf_op jit(solution)/shard_map/residual_0/pallas_call | solution.py:144
  13.5 5.2 %all-to-all-start = ((f32[8,4,4,32,128]{4,3,2,1,0:T(8,128)}), f32[8,4,4,32,128]{4,3,2,1,0:T(8,128)}, u32[]{:S(2)}, u32[]{:S(2)}) async-start(f32[8,4,4,32,128]{4,3,2,1,0:T(8,128)} %bitcast.58), calls=%async_computation | async-start | bytes 4194304 | tf_op jit(solution)/shard_map/all_to_all | solution.py:465
  18.6 1.2 collective-permute-start.1
  20.7 2.7 collective-permute-start.3
  24.3 9.8 %residual_32.1 = f32[96,4,32,128]{3,2,1,0:T(8,128)} custom-call(bf16[128,64]{1,0:T(8,128)(2,1)} %get-tuple-element.47.hidden_ref, bf16[64,2,8192]{2,1,0:T(2,128)(2,1)} %w_ref.3, bf16[2,8192,128]{2,1,0:T(8,128)(2,1)} %observed_ref.3, bf16[128,32]{1,0:T(8,128)(2,1)} %get-tuple-element.36.keep_ref, f32[1,8192]{1,0:T(1,128)} %get-tuple-element.37.taper_ref), custom_call_target="tpu_custom_call" | custom-call | flops 603979776 | bytes 10485760 | tf_op jit(solution)/shard_map/residual_32/pallas_call | solution.py:144
  34.8 9.7 %all-to-all-done.x_ref = f32[8,4,4,32,128]{4,3,2,1,0:T(8,128)} async-done(((f32[8,4,4,32,128]{4,3,2,1,0:T(8,128)}), f32[8,4,4,32,128]{4,3,2,1,0:T(8,128)}, u32[]{:S(2)}, u32[]{:S(2)}) %all-to-all-start) | async-done | bytes 2097184 | tf_op jit(solution)/shard_map/all_to_all | solution.py:465
  44.5 5.1 %all-to-all-start.2 = ((f32[8,12,4,32,128]{4,3,2,1,0:T(8,128)}), f32[8,12,4,32,128]{4,3,2,1,0:T(8,128)}, u32[]{:S(2)}, u32[]{:S(2)}) async-start(f32[8,12,4,32,128]{4,3,2,1,0:T(8,128)} %bitcast.54), calls=%async_computation.2 | async-start | bytes 12582912 | tf_op jit(solution)/shard_map/all_to_all | solution.py:465
  49.7 2.5 copy.26
  53.9 10.6 %delay_1.1 = f32[8,4,4,32,128]{4,3,2,1,0:T(8,128)} custom-call(f32[8,4,4,32,128]{4,3,2,1,0:T(8,128)} %all-to-all-done.x_ref, bf16[512,512]{1,0:T(8,128)(2,1)} %constant.127.clone.fh_ref, bf16[512,512]{1,0:T(8,128)(2,1)} %constant.128.clone.fl_ref, bf16[512,512]{1,0:T(8,128)(2,1)} %constant.129.clone.bh_ref, bf16[512,512]{1,0:T(8,128)(2,1)} %constant.130.clone.bl_ref, ...), custom_call_target="tpu_custom_call" | custom-call | flops 6442450944 | bytes 12582912 | tf_op jit(solution)/shard_map/delay_1/pallas_call | solution.py:219
  64.4 6.6 %all_rows.1 = (bf16[64,2048]{1,0:T(8,128)(2,1)}, f32[64,2048]{1,0:T(8,128)}, s32[8,2048]{1,0:T(8,128)}) custom-call(f32[4,4,8,128]{3,2,1,0:T(8,128)} %pad_maximum_fusion.2.index_ref, bf16[64,4096]{1,0:T(8,128)(2,1)} %table_ref.3, bf16[64,2016]{1,0:T(8,128)(2,1)} %features_ref.3, bf16[64,64]{1,0:T(8,128)(2,1)} %w_in_ref.5), custom_call_target="tpu_custom_call" | custom-call | flops 6000000000 | bytes 1048576 | tf_op jit(solution)/shard_map/all_rows/pallas_call | solution.py:346
  71.1 48.2 %all-to-all-done.2.x_ref = f32[8,12,4,32,128]{4,3,2,1,0:T(8,128)} async-done(((f32[8,12,4,32,128]{4,3,2,1,0:T(8,128)}), f32[8,12,4,32,128]{4,3,2,1,0:T(8,128)}, u32[]{:S(2)}, u32[]{:S(2)}) %all-to-all-start.2) | async-done | bytes 6291488 | tf_op jit(solution)/shard_map/all_to_all | solution.py:465
  119.2 5.0 %all-to-all-start.1 = ((f32[8,4,4,32,128]{4,3,2,1,0:T(8,128)}), f32[8,4,4,32,128]{4,3,2,1,0:T(8,128)}, u32[]{:S(2)}, u32[]{:S(2)}) async-start(f32[8,4,4,32,128]{4,3,2,1,0:T(8,128)} %delay_1.1), calls=%async_computation.1 | async-start | bytes 4194304 | tf_op jit(solution)/shard_map/all_to_all | solution.py:465
  124.2 24.4 %delay_2.1 = (f32[8,12,4,16,128]{4,3,2,1,0:T(8,128)}, f32[8,12,4,16,128]{4,3,2,1,0:T(8,128)}) custom-call(f32[8,12,4,32,128]{4,3,2,1,0:T(8,128)} %all-to-all-done.2.x_ref, bf16[512,512]{1,0:T(8,128)(2,1)} %constant.127.clone.fh_ref, bf16[512,512]{1,0:T(8,128)(2,1)} %constant.128.clone.fl_ref, bf16[512,512]{1,0:T(8,128)(2,1)} %constant.129.clone.bh_ref, ...), custom_call_target="tpu_custom_call" | custom-call | flops 19327352832 | bytes 12582912 | tf_op jit(solution)/shard_map/delay_2/pallas_call | solution.py:219
  148.6 41.5 %all_to_all.25 = f32[8,12,4,16,128]{4,3,2,1,0:T(8,128)} all-to-all(f32[8,12,4,16,128]{4,3,2,1,0:T(8,128)} %get-tuple-element.51), channel_id=1, replica_groups=mesh['bl'=16,'ch'=8] {'ch'}, dimensions={0} | all-to-all | bytes 6291456 | tf_op jit(solution)/shard_map/all_to_all | solution.py:465
  190.1 4.5 %all-to-all-start.4 = ((f32[8,12,4,16,128]{4,3,2,1,0:T(8,128)}), f32[8,12,4,16,128]{4,3,2,1,0:T(8,128)}, u32[]{:S(2)}, u32[]{:S(2)}) async-start(f32[8,12,4,16,128]{4,3,2,1,0:T(8,128)} %get-tuple-element.55), calls=%async_computation.4 | async-start | bytes 6291456 | tf_op jit(solution)/shard_map/all_to_all | solution.py:465
  195.2 5.9 %tail_0.1 = (f32[4,2,8,4096]{3,2,1,0:T(8,128)}, f32[4,2,8,4096]{3,2,1,0:T(8,128)}, f32[64,128]{1,0:T(8,128)}) custom-call(f32[32,4,32,128]{3,2,1,0:T(8,128)} %bitcast.12.g1_ref, f32[96,4,16,128]{3,2,1,0:T(8,128)} %bitcast.57, bf16[64,128]{1,0:T(8,128)(2,1)} %convolution_convert_fusion.hidden_ref, bf16[2,64,8192]{2,1,0:T(8,128)(2,1)} %bitcast.55, ...), custom_call_target="tpu_custom_call" | custom-call | flops 268435456 | bytes 8388608 | tf_op jit(solution)/shard_map/tail_0/pallas_call | solution.py:280
  201.1 3.5 %collective-permute-start.5 = (f32[4,2,8,4096]{3,2,1,0:T(8,128)}, f32[4,2,8,4096]{3,2,1,0:T(8,128)S(1)}, u32[]{:S(2)}, u32[]{:S(2)}) collective-permute-start(f32[4,2,8,4096]{3,2,1,0:T(8,128)} %get-tuple-element.53), channel_id=1, source_target_pairs={{0,8},{8,0},{16,24},{24,16},{32,40},{40,32},{48,56},{56,48},{64,72... | collective-permute-start | bytes 3145736 | tf_op jit(solution)/shard_map/ppermute | solution.py:412
  204.6 2.5 collective-permute-done.5
  207.1 1.3 add.139
  208.5 1.0 copy-done.5
  210.3 1.3 collective-permute-start.6
  211.7 2.5 collective-permute-start.7
  214.1 1.0 collective-permute-start.8
  215.2 14.2 %all-to-all-done.4 = f32[8,12,4,16,128]{4,3,2,1,0:T(8,128)} async-done(((f32[8,12,4,16,128]{4,3,2,1,0:T(8,128)}), f32[8,12,4,16,128]{4,3,2,1,0:T(8,128)}, u32[]{:S(2)}, u32[]{:S(2)}) %all-to-all-start.4) | async-done | bytes 3145760 | tf_op jit(solution)/shard_map/all_to_all | solution.py:465
  229.4 6.0 %tail_2.1 = (f32[4,2,8,4096]{3,2,1,0:T(8,128)}, f32[4,2,8,4096]{3,2,1,0:T(8,128)}, f32[64,128]{1,0:T(8,128)}) custom-call(f32[32,4,32,128]{3,2,1,0:T(8,128)} %bitcast.12.g1_ref, f32[96,4,16,128]{3,2,1,0:T(8,128)} %bitcast.19.g2_ref, bf16[64,128]{1,0:T(8,128)(2,1)} %convolution_convert_fusion.hidden_ref, bf16[2,64,8192]{2,1,0:T(8,128)(2,1)} %bitcast.56, ...), custom_call_target="tpu_custom_call" | custom-call | flops 268435456 | bytes 8388608 | tf_op jit(solution)/shard_map/tail_2/pallas_call | solution.py:280
  235.4 4.4 %collective-permute-start.9 = (f32[4,2,8,4096]{3,2,1,0:T(8,128)}, f32[4,2,8,4096]{3,2,1,0:T(8,128)S(1)}, u32[]{:S(2)}, u32[]{:S(2)}) collective-permute-start(f32[4,2,8,4096]{3,2,1,0:T(8,128)} %get-tuple-element.59), channel_id=1, source_target_pairs={{0,8},{8,0},{16,24},{24,16},{32,40},{40,32},{48,56},{56,48},{64,72... | collective-permute-start | bytes 3145736 | tf_op jit(solution)/shard_map/ppermute | solution.py:412
  239.8 1.0 fusion.8
  240.9 1.7 collective-permute-start.15
  242.6 2.2 collective-permute-start.16
  244.8 1.4 add.143
  246.3 1.4 collective-permute-start.10
  247.7 2.5 collective-permute-start.11
  250.1 1.0 collective-permute-start.12
  251.8 2.5 collective-permute-done.17
  254.3 2.6 collective-permute-start.18
  256.9 1.5 collective-permute-start.19
  258.4 1.7 collective-permute-start.20
  260.1 1.4 collective-permute-done.19
  261.5 1.8 collective-permute-done.20
  263.8 2.0 collective-permute-start.22
  265.7 1.6 collective-permute-start.23
  267.4 1.6 collective-permute-start.13
  269.0 2.7 collective-permute-done.22.two_ref
  271.7 2.5 collective-permute-done.23.three_ref
  274.2 4.8 %scatter.1 = (f32[64,64]{1,0:T(8,128)}, f32[64,4096]{1,0:T(8,128)}, f32[64,2016]{1,0:T(8,128)}) custom-call(f32[4,64,128]{2,1,0:T(8,128)S(1)} %pad_maximum_fusion.1.own_ref, f32[4,64,128]{2,1,0:T(8,128)S(1)} %collective-permute-done.21.one_ref, f32[4,64,128]{2,1,0:T(8,128)S(1)} %collective-permute-done.22.two_ref, ...), custom_call_target="tpu_custom_call" | custom-call | flops 6000000000 | bytes 4194304 | tf_op jit(solution)/shard_map/scatter/pallas_call | solution.py:395
  279.1 0.9 copy.24
  (61 shorter events, 7.0 us)
Async XLA Ops:
  3.3 10.2 %collective-permute-start = (f32[8,128]{1,0:T(8,128)}, f32[8,128]{1,0:T(8,128)S(1)}, u32[]{:S(2)}, u32[]{:S(2)}) collective-permute-start(f32[8,128]{1,0:T(8,128)} %get-tuple-element.38), channel_id=1, source_target_pairs={{0,16},{8,24},{16,0},{24,8},{32,48},{40,56},{48,32},{56,40},{64,80... | collective-permute-start | bytes 12296 | tf_op jit(solution)/shard_map/ppermute | solution.py:412
  7.0 6.4 %copy-start.8 = (f32[8,128]{1,0:T(8,128)S(1)}, f32[8,128]{1,0:T(8,128)}, u32[]{:S(2)}) copy-start(f32[8,128]{1,0:T(8,128)} %get-tuple-element.38) | copy-start | bytes 12292
  13.5 31.0 %all-to-all-start = ((f32[8,4,4,32,128]{4,3,2,1,0:T(8,128)}), f32[8,4,4,32,128]{4,3,2,1,0:T(8,128)}, u32[]{:S(2)}, u32[]{:S(2)}) async-start(f32[8,4,4,32,128]{4,3,2,1,0:T(8,128)} %bitcast.58), calls=%async_computation | async-start | bytes 4194304 | tf_op jit(solution)/shard_map/all_to_all | solution.py:465
  18.6 2.1 collective-permute-start.1
  20.7 13.4 %collective-permute-start.3 = (f32[4,8,128]{2,1,0:T(8,128)S(1)}, f32[4,8,128]{2,1,0:T(8,128)S(1)}, u32[]{:S(2)}, u32[]{:S(2)}) collective-permute-start(f32[4,8,128]{2,1,0:T(8,128)S(1)} %get-tuple-element.81), channel_id=1, source_target_pairs={{0,64},{8,72},{16,80},{24,88},{32,96},{40,104},{48,112},{56,120},{... | collective-permute-start | bytes 49160 | tf_op jit(solution)/shard_map/ppermute | solution.py:412
  23.4 10.7 %collective-permute-start.4 = (f32[4,8,128]{2,1,0:T(8,128)S(1)}, f32[4,8,128]{2,1,0:T(8,128)S(1)}, u32[]{:S(2)}, u32[]{:S(2)}) collective-permute-start(f32[4,8,128]{2,1,0:T(8,128)S(1)} %get-tuple-element.81), channel_id=1, source_target_pairs={{0,96},{8,104},{16,112},{24,120},{32,64},{40,72},{48,80},{56,88},{... | collective-permute-start | bytes 49160 | tf_op jit(solution)/shard_map/ppermute | solution.py:412
  24.3 9.8 %collective-permute-start.2 = (f32[4,8,128]{2,1,0:T(8,128)S(1)}, f32[4,8,128]{2,1,0:T(8,128)S(1)}, u32[]{:S(2)}, u32[]{:S(2)}) collective-permute-start(f32[4,8,128]{2,1,0:T(8,128)S(1)} %get-tuple-element.81), channel_id=1, source_target_pairs={{0,32},{8,40},{16,48},{24,56},{32,0},{40,8},{48,16},{56,24},{64,96... | collective-permute-start | bytes 49160 | tf_op jit(solution)/shard_map/ppermute | solution.py:412
  44.5 5.1 %copy-start.4 = (bf16[64,2,8192]{2,1,0:T(2,128)(2,1)S(1)}, bf16[64,2,8192]{2,1,0:T(2,128)(2,1)}, u32[]{:S(2)}) copy-start(bf16[64,2,8192]{2,1,0:T(2,128)(2,1)} %w_ref.3) | copy-start | bytes 6291460
  44.5 74.7 %all-to-all-start.2 = ((f32[8,12,4,32,128]{4,3,2,1,0:T(8,128)}), f32[8,12,4,32,128]{4,3,2,1,0:T(8,128)}, u32[]{:S(2)}, u32[]{:S(2)}) async-start(f32[8,12,4,32,128]{4,3,2,1,0:T(8,128)} %bitcast.54), calls=%async_computation.2 | async-start | bytes 12582912 | tf_op jit(solution)/shard_map/all_to_all | solution.py:465
  49.6 2.5 copy-start.6
  49.6 3.5 %copy-start.9 = (bf16[64,128]{1,0:T(8,128)(2,1)S(1)}, bf16[64,128]{1,0:T(8,128)(2,1)}, u32[]{:S(2)}) copy-start(bf16[64,128]{1,0:T(8,128)(2,1)} %get-tuple-element.40) | copy-start | bytes 49156
  119.2 29.4 %all-to-all-start.1 = ((f32[8,4,4,32,128]{4,3,2,1,0:T(8,128)}), f32[8,4,4,32,128]{4,3,2,1,0:T(8,128)}, u32[]{:S(2)}, u32[]{:S(2)}) async-start(f32[8,4,4,32,128]{4,3,2,1,0:T(8,128)} %delay_1.1), calls=%async_computation.1 | async-start | bytes 4194304 | tf_op jit(solution)/shard_map/all_to_all | solution.py:465
  190.1 39.3 %all-to-all-start.4 = ((f32[8,12,4,16,128]{4,3,2,1,0:T(8,128)}), f32[8,12,4,16,128]{4,3,2,1,0:T(8,128)}, u32[]{:S(2)}, u32[]{:S(2)}) async-start(f32[8,12,4,16,128]{4,3,2,1,0:T(8,128)} %get-tuple-element.55), calls=%async_computation.4 | async-start | bytes 6291456 | tf_op jit(solution)/shard_map/all_to_all | solution.py:465
  201.1 6.0 %collective-permute-start.5 = (f32[4,2,8,4096]{3,2,1,0:T(8,128)}, f32[4,2,8,4096]{3,2,1,0:T(8,128)S(1)}, u32[]{:S(2)}, u32[]{:S(2)}) collective-permute-start(f32[4,2,8,4096]{3,2,1,0:T(8,128)} %get-tuple-element.53), channel_id=1, source_target_pairs={{0,8},{8,0},{16,24},{24,16},{32,40},{40,32},{48,56},{56,48},{64,72... | collective-permute-start | bytes 3145736 | tf_op jit(solution)/shard_map/ppermute | solution.py:412
  208.5 1.0 copy-start.5
  210.3 29.5 %collective-permute-start.6 = (f32[2,8,4096]{2,1,0:T(8,128)}, f32[2,8,4096]{2,1,0:T(8,128)S(1)}, u32[]{:S(2)}, u32[]{:S(2)}) collective-permute-start(f32[2,8,4096]{2,1,0:T(8,128)} %get-tuple-element.74), channel_id=1, source_target_pairs={{0,32},{8,40},{16,48},{24,56},{32,64},{40,72},{48,80},{56,88},{64,... | collective-permute-start | bytes 786440 | tf_op jit(solution)/shard_map/ppermute | solution.py:431
  211.7 28.2 %collective-permute-start.7 = (f32[2,8,4096]{2,1,0:T(8,128)}, f32[2,8,4096]{2,1,0:T(8,128)S(1)}, u32[]{:S(2)}, u32[]{:S(2)}) collective-permute-start(f32[2,8,4096]{2,1,0:T(8,128)} %get-tuple-element.76), channel_id=1, source_target_pairs={{0,64},{8,72},{16,80},{24,88},{32,96},{40,104},{48,112},{56,120},{... | collective-permute-start | bytes 786440 | tf_op jit(solution)/shard_map/ppermute | solution.py:431
  214.1 25.7 %collective-permute-start.8 = (f32[2,8,4096]{2,1,0:T(8,128)}, f32[2,8,4096]{2,1,0:T(8,128)S(1)}, u32[]{:S(2)}, u32[]{:S(2)}) collective-permute-start(f32[2,8,4096]{2,1,0:T(8,128)} %get-tuple-element.75), channel_id=1, source_target_pairs={{0,96},{8,104},{16,112},{24,120},{32,0},{40,8},{48,16},{56,24},{64... | collective-permute-start | bytes 786440 | tf_op jit(solution)/shard_map/ppermute | solution.py:431
  235.4 15.8 %copy-start.7 = (f32[64,128]{1,0:T(8,128)S(1)}, f32[64,128]{1,0:T(8,128)}, u32[]{:S(2)}) copy-start(f32[64,128]{1,0:T(8,128)} %get-tuple-element.60) | copy-start | bytes 98308
  235.4 9.4 %collective-permute-start.9 = (f32[4,2,8,4096]{3,2,1,0:T(8,128)}, f32[4,2,8,4096]{3,2,1,0:T(8,128)S(1)}, u32[]{:S(2)}, u32[]{:S(2)}) collective-permute-start(f32[4,2,8,4096]{3,2,1,0:T(8,128)} %get-tuple-element.59), channel_id=1, source_target_pairs={{0,8},{8,0},{16,24},{24,16},{32,40},{40,32},{48,56},{56,48},{64,72... | collective-permute-start | bytes 3145736 | tf_op jit(solution)/shard_map/ppermute | solution.py:412
  240.8 9.3 %collective-permute-start.14 = (f32[64,128]{1,0:T(8,128)}, f32[64,128]{1,0:T(8,128)S(1)}, u32[]{:S(2)}, u32[]{:S(2)}) collective-permute-start(f32[64,128]{1,0:T(8,128)} %get-tuple-element.60), channel_id=1, source_target_pairs={{0,2},{1,3},{2,0},{3,1},{4,6},{5,7},{6,4},{7,5},{8,10},{9,11},{10,... | collective-permute-start | bytes 98312 | tf_op jit(solution)/shard_map/ppermute | solution.py:412
  240.9 10.2 %collective-permute-start.15 = (f32[64,128]{1,0:T(8,128)}, f32[64,128]{1,0:T(8,128)S(1)}, u32[]{:S(2)}, u32[]{:S(2)}) collective-permute-start(f32[64,128]{1,0:T(8,128)} %get-tuple-element.60), channel_id=1, source_target_pairs={{0,4},{1,5},{2,6},{3,7},{4,0},{5,1},{6,2},{7,3},{8,12},{9,13},{10,... | collective-permute-start | bytes 98312 | tf_op jit(solution)/shard_map/ppermute | solution.py:412
  242.6 8.5 %collective-permute-start.16 = (f32[64,128]{1,0:T(8,128)}, f32[64,128]{1,0:T(8,128)S(1)}, u32[]{:S(2)}, u32[]{:S(2)}) collective-permute-start(f32[64,128]{1,0:T(8,128)} %get-tuple-element.60), channel_id=1, source_target_pairs={{0,6},{1,7},{2,4},{3,5},{4,2},{5,3},{6,0},{7,1},{8,14},{9,15},{10,... | collective-permute-start | bytes 98312 | tf_op jit(solution)/shard_map/ppermute | solution.py:412
  244.8 29.4 %copy-start = (bf16[64,64]{1,0:T(8,128)(2,1)S(1)}, bf16[64,64]{1,0:T(8,128)(2,1)}, u32[]{:S(2)}) copy-start(bf16[64,64]{1,0:T(8,128)(2,1)} %w_in_ref.5) | copy-start | bytes 24580
  244.8 29.4 %copy-start.1 = (f32[64,2048]{1,0:T(8,128)S(1)}, f32[64,2048]{1,0:T(8,128)}, u32[]{:S(2)}) copy-start(f32[64,2048]{1,0:T(8,128)} %get-tuple-element.44.slope_ref) | copy-start | bytes 1572868
  244.8 29.4 %copy-start.2 = (bf16[64,2048]{1,0:T(8,128)(2,1)S(1)}, bf16[64,2048]{1,0:T(8,128)(2,1)}, u32[]{:S(2)}) copy-start(bf16[64,2048]{1,0:T(8,128)(2,1)} %get-tuple-element.43.inputs_ref) | copy-start | bytes 786436
  244.8 29.4 %copy-start.3 = (s32[8,2048]{1,0:T(8,128)S(1)}, s32[8,2048]{1,0:T(8,128)}, u32[]{:S(2)}) copy-start(s32[8,2048]{1,0:T(8,128)} %get-tuple-element.45.cells_ref) | copy-start | bytes 196612
  246.3 17.0 %collective-permute-start.10 = (f32[2,8,4096]{2,1,0:T(8,128)S(1)}, f32[2,8,4096]{2,1,0:T(8,128)S(1)}, u32[]{:S(2)}, u32[]{:S(2)}) collective-permute-start(f32[2,8,4096]{2,1,0:T(8,128)S(1)} %get-tuple-element.77), channel_id=1, source_target_pairs={{0,32},{8,40},{16,48},{24,56},{32,64},{40,72},{48,80},{56,88},{64,... | collective-permute-start | bytes 786440 | tf_op jit(solution)/shard_map/ppermute | solution.py:431
  247.7 15.6 %collective-permute-start.11 = (f32[2,8,4096]{2,1,0:T(8,128)S(1)}, f32[2,8,4096]{2,1,0:T(8,128)S(1)}, u32[]{:S(2)}, u32[]{:S(2)}) collective-permute-start(f32[2,8,4096]{2,1,0:T(8,128)S(1)} %get-tuple-element.79), channel_id=1, source_target_pairs={{0,64},{8,72},{16,80},{24,88},{32,96},{40,104},{48,112},{56,120},{... | collective-permute-start | bytes 786440 | tf_op jit(solution)/shard_map/ppermute | solution.py:431
  250.1 13.2 %collective-permute-start.12 = (f32[2,8,4096]{2,1,0:T(8,128)S(1)}, f32[2,8,4096]{2,1,0:T(8,128)S(1)}, u32[]{:S(2)}, u32[]{:S(2)}) collective-permute-start(f32[2,8,4096]{2,1,0:T(8,128)S(1)} %get-tuple-element.78), channel_id=1, source_target_pairs={{0,96},{8,104},{16,112},{24,120},{32,0},{40,8},{48,16},{56,24},{64... | collective-permute-start | bytes 786440 | tf_op jit(solution)/shard_map/ppermute | solution.py:431
  251.2 3.1 %collective-permute-start.17 = (f32[64,128]{1,0:T(8,128)S(1)}, f32[64,128]{1,0:T(8,128)S(1)}, u32[]{:S(2)}, u32[]{:S(2)}) collective-permute-start(f32[64,128]{1,0:T(8,128)S(1)} %add_add_fusion), channel_id=1, source_target_pairs={{0,1},{1,0},{2,3},{3,2},{4,5},{5,4},{6,7},{7,6},{8,9},{9,8},{10,11... | collective-permute-start | bytes 98312 | tf_op jit(solution)/shard_map/ppermute | solution.py:412
  254.3 4.1 %collective-permute-start.18 = (f32[64,128]{1,0:T(8,128)S(1)}, f32[64,128]{1,0:T(8,128)S(1)}, u32[]{:S(2)}, u32[]{:S(2)}) collective-permute-start(f32[64,128]{1,0:T(8,128)S(1)} %add.151), channel_id=1, source_target_pairs={{0,8},{8,0},{16,24},{24,16},{32,40},{40,32},{48,56},{56,48},{64,72... | collective-permute-start | bytes 98312 | tf_op jit(solution)/shard_map/ppermute | solution.py:412
  256.9 4.6 %collective-permute-start.19 = (f32[64,128]{1,0:T(8,128)S(1)}, f32[64,128]{1,0:T(8,128)S(1)}, u32[]{:S(2)}, u32[]{:S(2)}) collective-permute-start(f32[64,128]{1,0:T(8,128)S(1)} %add.151), channel_id=1, source_target_pairs={{0,16},{8,24},{16,0},{24,8},{32,48},{40,56},{48,32},{56,40},{64,80... | collective-permute-start | bytes 98312 | tf_op jit(solution)/shard_map/ppermute | solution.py:412
  258.4 4.9 %collective-permute-start.20 = (f32[64,128]{1,0:T(8,128)S(1)}, f32[64,128]{1,0:T(8,128)S(1)}, u32[]{:S(2)}, u32[]{:S(2)}) collective-permute-start(f32[64,128]{1,0:T(8,128)S(1)} %add.151), channel_id=1, source_target_pairs={{0,24},{8,16},{16,8},{24,0},{32,56},{40,48},{48,40},{56,32},{64,88... | collective-permute-start | bytes 98312 | tf_op jit(solution)/shard_map/ppermute | solution.py:412
  263.4 5.6 %collective-permute-start.21 = (f32[4,64,128]{2,1,0:T(8,128)S(1)}, f32[4,64,128]{2,1,0:T(8,128)S(1)}, u32[]{:S(2)}, u32[]{:S(2)}) collective-permute-start(f32[4,64,128]{2,1,0:T(8,128)S(1)} %pad_maximum_fusion.1.own_ref), channel_id=1, source_target_pairs={{0,32},{8,40},{16,48},{24,56},{32,0},{40,8},{48,16},{56,24},{64,96... | collective-permute-start | bytes 393224 | tf_op jit(solution)/shard_map/ppermute | solution.py:412
  263.8 7.9 %collective-permute-start.22 = (f32[4,64,128]{2,1,0:T(8,128)S(1)}, f32[4,64,128]{2,1,0:T(8,128)S(1)}, u32[]{:S(2)}, u32[]{:S(2)}) collective-permute-start(f32[4,64,128]{2,1,0:T(8,128)S(1)} %pad_maximum_fusion.1.own_ref), channel_id=1, source_target_pairs={{0,64},{8,72},{16,80},{24,88},{32,96},{40,104},{48,112},{56,120},{... | collective-permute-start | bytes 393224 | tf_op jit(solution)/shard_map/ppermute | solution.py:412
  265.7 8.4 %collective-permute-start.23 = (f32[4,64,128]{2,1,0:T(8,128)S(1)}, f32[4,64,128]{2,1,0:T(8,128)S(1)}, u32[]{:S(2)}, u32[]{:S(2)}) collective-permute-start(f32[4,64,128]{2,1,0:T(8,128)S(1)} %pad_maximum_fusion.1.own_ref), channel_id=1, source_target_pairs={{0,96},{8,104},{16,112},{24,120},{32,64},{40,72},{48,80},{56,88},{... | collective-permute-start | bytes 393224 | tf_op jit(solution)/shard_map/ppermute | solution.py:412
  267.4 11.6 %collective-permute-start.13 = (f32[2,4,8192]{2,1,0:T(4,128)S(1)}, f32[2,4,8192]{2,1,0:T(4,128)S(1)}, u32[]{:S(2)}, u32[]{:S(2)}) collective-permute-start(f32[2,4,8192]{2,1,0:T(4,128)S(1)} %pad_maximum_fusion), channel_id=1, source_target_pairs={{0,16},{8,24},{16,0},{24,8},{32,48},{40,56},{48,32},{56,40},{64,80... | collective-permute-start | bytes 786440 | tf_op jit(solution)/shard_map/ppermute | solution.py:412

commit v5 on v3

--- a/solution.py
+++ b/solution.py
@@ -371,18 +371,18 @@
     for which, out_ref in ((0, grad_uvw_ref), (1, grad_base_ref)):
         index = cells_ref[which : which + 1, :]
         cells = out_ref.shape[1]
-        half = -(-cells // 2 // LANES) * LANES
-        upper = index >= half
-        index = jnp.where(upper, index - half, index)
+        quarter = -(-cells // 4 // LANES) * LANES
+        sides = [
+            (index >= side * quarter) & (index < (side + 1) * quarter) for side in range(4)
+        ]
         zero = jnp.zeros_like(terms)
-        sides = jnp.concatenate(
-            [jnp.where(upper, zero, terms), jnp.where(upper, terms, zero)], axis=0
-        )
-        for start in range(0, half, 512):
-            size = min(512, half - start)
-            sums = dot(one_hot_rows(index - start, size), sides, NT).T
-            for side in range(2):
-                first = side * half + start
+        apart = jnp.concatenate([jnp.where(here, terms, zero) for here in sides], axis=0)
+        index = index % quarter
+        for start in range(0, quarter, 512):
+            size = min(512, quarter - start)
+            sums = dot(one_hot_rows(index - start, size), apart, NT).T
+            for side in range(4):
+                first = side * quarter + start
                 wide = min(size, cells - first)
                 part = sums[side * 2 * units : (side + 1) * 2 * units, :wide]
                 out_ref[:, first : first + wide] = part[:units] + part[units:]
@@ -423,10 +423,9 @@
     return mine + swap(other, "bl", 1)
 
 
-def sum_far(both):
+def far_parts(both):
     ring = lambda d: [(i, (i + 4 * d) % 16) for i in range(16)]
-    got = [lax.ppermute(both[d], "bl", ring(d)) for d in (1, 2, 3)]
-    return both[0] + got[0] + got[1] + got[2]
+    return [both[0], *[lax.ppermute(both[d], "bl", ring(d)) for d in (1, 2, 3)]]
 
 
 def sum_near(total):
@@ -503,16 +502,16 @@
     )
     both = sum_cores(mine, other, 1)
     piece = after(arrive(late), both)
-    first = sum_far(both)
+    first = sum(far_parts(both))
     mine, other, hidden_grad = tail_part(
         counts[0], counts[1], back_0, piece, hidden_order, w, keep, taper, hidden_grad
     )
     both = sum_cores(mine, other, 1)
     hidden_grad = sum_over_ch(hidden_grad, both, first)
-    second = sum_far(both)
-    near = after(jnp.stack(met(hidden_grad, "bl", (1, 2, 3))), second)
+    second = far_parts(both)
+    near = after(jnp.stack(met(hidden_grad, "bl", (1, 2, 3))), *second[1:])
     blocks = met(near, "bl", (4, 8, 12))
-    grad_out = sum_near(jnp.concatenate([first, second], axis=2)).transpose(1, 0, 2)
+    grad_out = sum_near(jnp.concatenate([first, sum(second)], axis=2)).transpose(1, 0, 2)
     grad_in, grad_uvw, grad_base = scatter(
         blocks, known, w_in, uvw_table.shape[1], baseline_features.shape[1]
     )

time: 281 us -> 281 us (level)
  no operation moved by 1% of the time
where the time goes in v5:
time: 281 us; the launch traced here: 280 us
  waiting for transfers between devices  85.6 us (30%)
  Pallas kernels  77.2 us (27%)
  starting transfers between devices  62.4 us (22%)
  blocking collectives  41.4 us (15%)
  local copies, waits for them, and re-layouts  6.87 us (2%)
  other arithmetic  5.31 us (2%)
    all_to_all x4, waiting for transfers between devices, exchange(): lax.all_to_all(values.reshape(members, -1, PLANES, size, LANES), 'ch', 0,...  71.9 us
    all_to_all x1, blocking collectives, exchange(): lax.all_to_all(values.reshape(members, -1, PLANES, size, LANES), 'ch', 0,...  41.4 us
    pallas_call x2, Pallas kernels, delay_filter(): pl.pallas_call(functools.partial(delay_kernel, pieces), grid=(rows // cou...  35 us
    ppermute x18, starting transfers between devices, swap(): return lax.ppermute(values, axis, [(i, i ^ distance) for i in range(size)])  32.6 us
    all_to_all x4, starting transfers between devices, exchange(): lax.all_to_all(values.reshape(members, -1, PLANES, size, LANES), 'ch', 0,...  19.7 us
    pallas_call x2, Pallas kernels, residual_part(): pl.pallas_call(functools.partial(residual_kernel, first_row, rows), grid=...  16.2 us
    ppermute x18, waiting for transfers between devices, swap(): return lax.ppermute(values, axis, [(i, i ^ distance) for i in range(size)])  13.7 us
    pallas_call x2, Pallas kernels, tail_part(): pl.pallas_call(functools.partial(tail_kernel, first), grid=(count, 2), in...  11.9 us
  transfers between devices with their start and end apart: 28, of which 10 were waited for; matrix products, arithmetic and copies ran while one was open for 4% of the time, Pallas kernels for 28%

profile of v5, /device:TPU:1, one launch (start us, length us, event | category | flops | bytes accessed | tf_op | source)
XLA Modules:
  0.0 280.4 jit_solution(5573186582835910825)
XLA Ops:
  1.3 3.8 %collective-permute-start = (f32[8,128]{1,0:T(8,128)S(1)}, f32[8,128]{1,0:T(8,128)S(1)}, u32[]{:S(2)}, u32[]{:S(2)}) collective-permute-start(f32[8,128]{1,0:T(8,128)S(1)} %get-tuple-element.85), channel_id=1, source_target_pairs={{0,16},{8,24},{16,0},{24,8},{32,48},{40,56},{48,32},{56,40},{64,80... | collective-permute-start | bytes 12296 | tf_op jit(solution)/shard_map/ppermute | solution.py:409
  5.1 2.6 trunk.1
  7.8 6.4 %residual_0.1 = f32[32,4,32,128]{3,2,1,0:T(8,128)} custom-call(bf16[128,64]{1,0:T(8,128)(2,1)} %get-tuple-element.45.hidden_ref, bf16[64,2,8192]{2,1,0:T(2,128)(2,1)} %w_ref.3, bf16[2,8192,128]{2,1,0:T(8,128)(2,1)} %observed_ref.3, bf16[128,32]{1,0:T(8,128)(2,1)} %get-tuple-element.35.keep_ref, f32[1,8192]{1,0:T(1,128)} %get-tuple-element.36.taper_ref), custom_call_target="tpu_custom_call" | custom-call | flops 201326592 | bytes 10485760 | tf_op jit(solution)/shard_map/residual_0/pallas_call | solution.py:141
  14.2 5.2 %all-to-all-start = ((f32[8,4,4,32,128]{4,3,2,1,0:T(8,128)}), f32[8,4,4,32,128]{4,3,2,1,0:T(8,128)}, u32[]{:S(2)}, u32[]{:S(2)}) async-start(f32[8,4,4,32,128]{4,3,2,1,0:T(8,128)} %bitcast.59), calls=%async_computation | async-start | bytes 4194304 | tf_op jit(solution)/shard_map/all_to_all | solution.py:461
  19.4 1.2 collective-permute-start.1
  21.4 2.7 collective-permute-start.3
  25.0 9.8 %residual_32.1 = f32[96,4,32,128]{3,2,1,0:T(8,128)} custom-call(bf16[128,64]{1,0:T(8,128)(2,1)} %get-tuple-element.45.hidden_ref, bf16[64,2,8192]{2,1,0:T(2,128)(2,1)} %w_ref.3, bf16[2,8192,128]{2,1,0:T(8,128)(2,1)} %observed_ref.3, bf16[128,32]{1,0:T(8,128)(2,1)} %get-tuple-element.35.keep_ref, f32[1,8192]{1,0:T(1,128)} %get-tuple-element.36.taper_ref), custom_call_target="tpu_custom_call" | custom-call | flops 603979776 | bytes 10485760 | tf_op jit(solution)/shard_map/residual_32/pallas_call | solution.py:141
  35.5 9.7 %all-to-all-done.x_ref = f32[8,4,4,32,128]{4,3,2,1,0:T(8,128)} async-done(((f32[8,4,4,32,128]{4,3,2,1,0:T(8,128)}), f32[8,4,4,32,128]{4,3,2,1,0:T(8,128)}, u32[]{:S(2)}, u32[]{:S(2)}) %all-to-all-start) | async-done | bytes 2097184 | tf_op jit(solution)/shard_map/all_to_all | solution.py:461
  45.3 5.1 %all-to-all-start.2 = ((f32[8,12,4,32,128]{4,3,2,1,0:T(8,128)}), f32[8,12,4,32,128]{4,3,2,1,0:T(8,128)}, u32[]{:S(2)}, u32[]{:S(2)}) async-start(f32[8,12,4,32,128]{4,3,2,1,0:T(8,128)} %bitcast.55), calls=%async_computation.2 | async-start | bytes 12582912 | tf_op jit(solution)/shard_map/all_to_all | solution.py:461
  50.4 2.5 copy.26
  54.6 10.6 %delay_1.1 = f32[8,4,4,32,128]{4,3,2,1,0:T(8,128)} custom-call(f32[8,4,4,32,128]{4,3,2,1,0:T(8,128)} %all-to-all-done.x_ref, bf16[512,512]{1,0:T(8,128)(2,1)} %constant.128.clone.fh_ref, bf16[512,512]{1,0:T(8,128)(2,1)} %constant.129.clone.fl_ref, bf16[512,512]{1,0:T(8,128)(2,1)} %constant.130.clone.bh_ref, bf16[512,512]{1,0:T(8,128)(2,1)} %constant.131.clone.bl_ref, ...), custom_call_target="tpu_custom_call" | custom-call | flops 6442450944 | bytes 12582912 | tf_op jit(solution)/shard_map/delay_1/pallas_call | solution.py:216
  65.2 6.6 %all_rows.1 = (bf16[64,2048]{1,0:T(8,128)(2,1)}, f32[64,2048]{1,0:T(8,128)}, s32[8,2048]{1,0:T(8,128)}) custom-call(f32[4,4,8,128]{3,2,1,0:T(8,128)} %pad_maximum_fusion.2.index_ref, bf16[64,4096]{1,0:T(8,128)(2,1)} %table_ref.3, bf16[64,2016]{1,0:T(8,128)(2,1)} %features_ref.3, bf16[64,64]{1,0:T(8,128)(2,1)} %w_in_ref.5), custom_call_target="tpu_custom_call" | custom-call | flops 6000000000 | bytes 1048576 | tf_op jit(solution)/shard_map/all_rows/pallas_call | solution.py:343
  71.8 48.2 %all-to-all-done.2.x_ref = f32[8,12,4,32,128]{4,3,2,1,0:T(8,128)} async-done(((f32[8,12,4,32,128]{4,3,2,1,0:T(8,128)}), f32[8,12,4,32,128]{4,3,2,1,0:T(8,128)}, u32[]{:S(2)}, u32[]{:S(2)}) %all-to-all-start.2) | async-done | bytes 6291488 | tf_op jit(solution)/shard_map/all_to_all | solution.py:461
  120.0 5.0 %all-to-all-start.1 = ((f32[8,4,4,32,128]{4,3,2,1,0:T(8,128)}), f32[8,4,4,32,128]{4,3,2,1,0:T(8,128)}, u32[]{:S(2)}, u32[]{:S(2)}) async-start(f32[8,4,4,32,128]{4,3,2,1,0:T(8,128)} %delay_1.1), calls=%async_computation.1 | async-start | bytes 4194304 | tf_op jit(solution)/shard_map/all_to_all | solution.py:461
  124.9 24.4 %delay_2.1 = (f32[8,12,4,16,128]{4,3,2,1,0:T(8,128)}, f32[8,12,4,16,128]{4,3,2,1,0:T(8,128)}) custom-call(f32[8,12,4,32,128]{4,3,2,1,0:T(8,128)} %all-to-all-done.2.x_ref, bf16[512,512]{1,0:T(8,128)(2,1)} %constant.128.clone.fh_ref, bf16[512,512]{1,0:T(8,128)(2,1)} %constant.129.clone.fl_ref, bf16[512,512]{1,0:T(8,128)(2,1)} %constant.130.clone.bh_ref, ...), custom_call_target="tpu_custom_call" | custom-call | flops 19327352832 | bytes 12582912 | tf_op jit(solution)/shard_map/delay_2/pallas_call | solution.py:216
  149.3 41.4 %all_to_all.25 = f32[8,12,4,16,128]{4,3,2,1,0:T(8,128)} all-to-all(f32[8,12,4,16,128]{4,3,2,1,0:T(8,128)} %get-tuple-element.49), channel_id=1, replica_groups=mesh['bl'=16,'ch'=8] {'ch'}, dimensions={0} | all-to-all | bytes 6291456 | tf_op jit(solution)/shard_map/all_to_all | solution.py:461
  190.7 4.5 %all-to-all-start.4 = ((f32[8,12,4,16,128]{4,3,2,1,0:T(8,128)}), f32[8,12,4,16,128]{4,3,2,1,0:T(8,128)}, u32[]{:S(2)}, u32[]{:S(2)}) async-start(f32[8,12,4,16,128]{4,3,2,1,0:T(8,128)} %get-tuple-element.53), calls=%async_computation.4 | async-start | bytes 6291456 | tf_op jit(solution)/shard_map/all_to_all | solution.py:461
  195.8 5.9 %tail_0.1 = (f32[4,2,8,4096]{3,2,1,0:T(8,128)}, f32[4,2,8,4096]{3,2,1,0:T(8,128)}, f32[64,128]{1,0:T(8,128)}) custom-call(f32[32,4,32,128]{3,2,1,0:T(8,128)} %bitcast.12.g1_ref, f32[96,4,16,128]{3,2,1,0:T(8,128)} %bitcast.58, bf16[64,128]{1,0:T(8,128)(2,1)} %convolution_convert_fusion.hidden_ref, bf16[2,64,8192]{2,1,0:T(8,128)(2,1)} %bitcast.56, ...), custom_call_target="tpu_custom_call" | custom-call | flops 268435456 | bytes 8388608 | tf_op jit(solution)/shard_map/tail_0/pallas_call | solution.py:277
  201.7 3.5 %collective-permute-start.5 = (f32[4,2,8,4096]{3,2,1,0:T(8,128)}, f32[4,2,8,4096]{3,2,1,0:T(8,128)S(1)}, u32[]{:S(2)}, u32[]{:S(2)}) collective-permute-start(f32[4,2,8,4096]{3,2,1,0:T(8,128)} %get-tuple-element.51), channel_id=1, source_target_pairs={{0,8},{8,0},{16,24},{24,16},{32,40},{40,32},{48,56},{56,48},{64,72... | collective-permute-start | bytes 3145736 | tf_op jit(solution)/shard_map/ppermute | solution.py:409
  205.3 2.5 collective-permute-done.5
  207.8 1.3 add.141
  209.1 1.0 copy-done.5
  211.0 1.2 collective-permute-start.6
  212.2 2.6 collective-permute-start.7
  214.7 1.2 collective-permute-start.8
  216.0 14.0 %all-to-all-done.4 = f32[8,12,4,16,128]{4,3,2,1,0:T(8,128)} async-done(((f32[8,12,4,16,128]{4,3,2,1,0:T(8,128)}), f32[8,12,4,16,128]{4,3,2,1,0:T(8,128)}, u32[]{:S(2)}, u32[]{:S(2)}) %all-to-all-start.4) | async-done | bytes 3145760 | tf_op jit(solution)/shard_map/all_to_all | solution.py:461
  230.0 6.0 %tail_2.1 = (f32[4,2,8,4096]{3,2,1,0:T(8,128)}, f32[4,2,8,4096]{3,2,1,0:T(8,128)}, f32[64,128]{1,0:T(8,128)}) custom-call(f32[32,4,32,128]{3,2,1,0:T(8,128)} %bitcast.12.g1_ref, f32[96,4,16,128]{3,2,1,0:T(8,128)} %bitcast.19.g2_ref, bf16[64,128]{1,0:T(8,128)(2,1)} %convolution_convert_fusion.hidden_ref, bf16[2,64,8192]{2,1,0:T(8,128)(2,1)} %bitcast.57, ...), custom_call_target="tpu_custom_call" | custom-call | flops 268435456 | bytes 8388608 | tf_op jit(solution)/shard_map/tail_2/pallas_call | solution.py:277
  236.0 4.5 %collective-permute-start.9 = (f32[4,2,8,4096]{3,2,1,0:T(8,128)}, f32[4,2,8,4096]{3,2,1,0:T(8,128)S(1)}, u32[]{:S(2)}, u32[]{:S(2)}) collective-permute-start(f32[4,2,8,4096]{3,2,1,0:T(8,128)} %get-tuple-element.57), channel_id=1, source_target_pairs={{0,8},{8,0},{16,24},{24,16},{32,40},{40,32},{48,56},{56,48},{64,72... | collective-permute-start | bytes 3145736 | tf_op jit(solution)/shard_map/ppermute | solution.py:409
  240.5 1.0 fusion.8
  241.6 1.7 collective-permute-start.15
  243.2 2.2 collective-permute-start.16
  245.4 1.4 add.145
  246.9 1.3 collective-permute-start.10
  248.2 2.6 collective-permute-start.11
  250.8 1.3 collective-permute-start.12
  252.6 2.5 collective-permute-done.17
  255.2 2.6 collective-permute-start.18
  257.8 1.3 collective-permute-start.19
  259.1 1.9 collective-permute-start.20
  261.0 1.4 collective-permute-done.19
  262.3 1.6 collective-permute-done.20
  264.5 1.7 collective-permute-start.22
  266.2 1.8 collective-permute-start.23
  268.1 1.7 collective-permute-start.13
  269.8 2.3 collective-permute-done.22.two_ref
  272.1 2.5 collective-permute-done.23.three_ref
  274.6 4.8 %scatter.1 = (f32[64,64]{1,0:T(8,128)}, f32[64,4096]{1,0:T(8,128)}, f32[64,2016]{1,0:T(8,128)}) custom-call(f32[4,64,128]{2,1,0:T(8,128)S(1)} %pad_maximum_fusion.1.own_ref, f32[4,64,128]{2,1,0:T(8,128)S(1)} %collective-permute-done.21.one_ref, f32[4,64,128]{2,1,0:T(8,128)S(1)} %collective-permute-done.22.two_ref, ...), custom_call_target="tpu_custom_call" | custom-call | flops 6000000000 | bytes 4194304 | tf_op jit(solution)/shard_map/scatter/pallas_call | solution.py:392
  279.5 0.9 copy.24
  (61 shorter events, 7.8 us)
Async XLA Ops:
  1.3 12.9 %collective-permute-start = (f32[8,128]{1,0:T(8,128)S(1)}, f32[8,128]{1,0:T(8,128)S(1)}, u32[]{:S(2)}, u32[]{:S(2)}) collective-permute-start(f32[8,128]{1,0:T(8,128)S(1)} %get-tuple-element.85), channel_id=1, source_target_pairs={{0,16},{8,24},{16,0},{24,8},{32,48},{40,56},{48,32},{56,40},{64,80... | collective-permute-start | bytes 12296 | tf_op jit(solution)/shard_map/ppermute | solution.py:409
  14.2 31.0 %all-to-all-start = ((f32[8,4,4,32,128]{4,3,2,1,0:T(8,128)}), f32[8,4,4,32,128]{4,3,2,1,0:T(8,128)}, u32[]{:S(2)}, u32[]{:S(2)}) async-start(f32[8,4,4,32,128]{4,3,2,1,0:T(8,128)} %bitcast.59), calls=%async_computation | async-start | bytes 4194304 | tf_op jit(solution)/shard_map/all_to_all | solution.py:461
  19.4 2.1 collective-permute-start.1
  21.4 13.4 %collective-permute-start.3 = (f32[4,8,128]{2,1,0:T(8,128)S(1)}, f32[4,8,128]{2,1,0:T(8,128)S(1)}, u32[]{:S(2)}, u32[]{:S(2)}) collective-permute-start(f32[4,8,128]{2,1,0:T(8,128)S(1)} %get-tuple-element.79), channel_id=1, source_target_pairs={{0,64},{8,72},{16,80},{24,88},{32,96},{40,104},{48,112},{56,120},{... | collective-permute-start | bytes 49160 | tf_op jit(solution)/shard_map/ppermute | solution.py:409
  24.2 10.7 %collective-permute-start.4 = (f32[4,8,128]{2,1,0:T(8,128)S(1)}, f32[4,8,128]{2,1,0:T(8,128)S(1)}, u32[]{:S(2)}, u32[]{:S(2)}) collective-permute-start(f32[4,8,128]{2,1,0:T(8,128)S(1)} %get-tuple-element.79), channel_id=1, source_target_pairs={{0,96},{8,104},{16,112},{24,120},{32,64},{40,72},{48,80},{56,88},{... | collective-permute-start | bytes 49160 | tf_op jit(solution)/shard_map/ppermute | solution.py:409
  25.0 9.8 %collective-permute-start.2 = (f32[4,8,128]{2,1,0:T(8,128)S(1)}, f32[4,8,128]{2,1,0:T(8,128)S(1)}, u32[]{:S(2)}, u32[]{:S(2)}) collective-permute-start(f32[4,8,128]{2,1,0:T(8,128)S(1)} %get-tuple-element.79), channel_id=1, source_target_pairs={{0,32},{8,40},{16,48},{24,56},{32,0},{40,8},{48,16},{56,24},{64,96... | collective-permute-start | bytes 49160 | tf_op jit(solution)/shard_map/ppermute | solution.py:409
  45.3 5.1 %copy-start.4 = (bf16[64,2,8192]{2,1,0:T(2,128)(2,1)S(1)}, bf16[64,2,8192]{2,1,0:T(2,128)(2,1)}, u32[]{:S(2)}) copy-start(bf16[64,2,8192]{2,1,0:T(2,128)(2,1)} %w_ref.3) | copy-start | bytes 6291460
  45.3 74.7 %all-to-all-start.2 = ((f32[8,12,4,32,128]{4,3,2,1,0:T(8,128)}), f32[8,12,4,32,128]{4,3,2,1,0:T(8,128)}, u32[]{:S(2)}, u32[]{:S(2)}) async-start(f32[8,12,4,32,128]{4,3,2,1,0:T(8,128)} %bitcast.55), calls=%async_computation.2 | async-start | bytes 12582912 | tf_op jit(solution)/shard_map/all_to_all | solution.py:461
  50.3 2.5 copy-start.6
  50.3 3.5 %copy-start.8 = (bf16[64,128]{1,0:T(8,128)(2,1)S(1)}, bf16[64,128]{1,0:T(8,128)(2,1)}, u32[]{:S(2)}) copy-start(bf16[64,128]{1,0:T(8,128)(2,1)} %get-tuple-element.38) | copy-start | bytes 49156
  120.0 29.4 %all-to-all-start.1 = ((f32[8,4,4,32,128]{4,3,2,1,0:T(8,128)}), f32[8,4,4,32,128]{4,3,2,1,0:T(8,128)}, u32[]{:S(2)}, u32[]{:S(2)}) async-start(f32[8,4,4,32,128]{4,3,2,1,0:T(8,128)} %delay_1.1), calls=%async_computation.1 | async-start | bytes 4194304 | tf_op jit(solution)/shard_map/all_to_all | solution.py:461
  190.7 39.3 %all-to-all-start.4 = ((f32[8,12,4,16,128]{4,3,2,1,0:T(8,128)}), f32[8,12,4,16,128]{4,3,2,1,0:T(8,128)}, u32[]{:S(2)}, u32[]{:S(2)}) async-start(f32[8,12,4,16,128]{4,3,2,1,0:T(8,128)} %get-tuple-element.53), calls=%async_computation.4 | async-start | bytes 6291456 | tf_op jit(solution)/shard_map/all_to_all | solution.py:461
  201.7 6.0 %collective-permute-start.5 = (f32[4,2,8,4096]{3,2,1,0:T(8,128)}, f32[4,2,8,4096]{3,2,1,0:T(8,128)S(1)}, u32[]{:S(2)}, u32[]{:S(2)}) collective-permute-start(f32[4,2,8,4096]{3,2,1,0:T(8,128)} %get-tuple-element.51), channel_id=1, source_target_pairs={{0,8},{8,0},{16,24},{24,16},{32,40},{40,32},{48,56},{56,48},{64,72... | collective-permute-start | bytes 3145736 | tf_op jit(solution)/shard_map/ppermute | solution.py:409
  209.1 1.0 copy-start.5
  211.0 29.5 %collective-permute-start.6 = (f32[2,8,4096]{2,1,0:T(8,128)}, f32[2,8,4096]{2,1,0:T(8,128)S(1)}, u32[]{:S(2)}, u32[]{:S(2)}) collective-permute-start(f32[2,8,4096]{2,1,0:T(8,128)} %get-tuple-element.72), channel_id=1, source_target_pairs={{0,32},{8,40},{16,48},{24,56},{32,64},{40,72},{48,80},{56,88},{64,... | collective-permute-start | bytes 786440 | tf_op jit(solution)/shard_map/ppermute | solution.py:428
  212.2 28.3 %collective-permute-start.7 = (f32[2,8,4096]{2,1,0:T(8,128)}, f32[2,8,4096]{2,1,0:T(8,128)S(1)}, u32[]{:S(2)}, u32[]{:S(2)}) collective-permute-start(f32[2,8,4096]{2,1,0:T(8,128)} %get-tuple-element.74), channel_id=1, source_target_pairs={{0,64},{8,72},{16,80},{24,88},{32,96},{40,104},{48,112},{56,120},{... | collective-permute-start | bytes 786440 | tf_op jit(solution)/shard_map/ppermute | solution.py:428
  214.7 25.7 %collective-permute-start.8 = (f32[2,8,4096]{2,1,0:T(8,128)}, f32[2,8,4096]{2,1,0:T(8,128)S(1)}, u32[]{:S(2)}, u32[]{:S(2)}) collective-permute-start(f32[2,8,4096]{2,1,0:T(8,128)} %get-tuple-element.73), channel_id=1, source_target_pairs={{0,96},{8,104},{16,112},{24,120},{32,0},{40,8},{48,16},{56,24},{64... | collective-permute-start | bytes 786440 | tf_op jit(solution)/shard_map/ppermute | solution.py:428
  236.0 16.0 %copy-start.7 = (f32[64,128]{1,0:T(8,128)S(1)}, f32[64,128]{1,0:T(8,128)}, u32[]{:S(2)}) copy-start(f32[64,128]{1,0:T(8,128)} %get-tuple-element.58) | copy-start | bytes 98308
  236.0 9.4 %collective-permute-start.9 = (f32[4,2,8,4096]{3,2,1,0:T(8,128)}, f32[4,2,8,4096]{3,2,1,0:T(8,128)S(1)}, u32[]{:S(2)}, u32[]{:S(2)}) collective-permute-start(f32[4,2,8,4096]{3,2,1,0:T(8,128)} %get-tuple-element.57), channel_id=1, source_target_pairs={{0,8},{8,0},{16,24},{24,16},{32,40},{40,32},{48,56},{56,48},{64,72... | collective-permute-start | bytes 3145736 | tf_op jit(solution)/shard_map/ppermute | solution.py:409
  241.5 9.3 %collective-permute-start.14 = (f32[64,128]{1,0:T(8,128)}, f32[64,128]{1,0:T(8,128)S(1)}, u32[]{:S(2)}, u32[]{:S(2)}) collective-permute-start(f32[64,128]{1,0:T(8,128)} %get-tuple-element.58), channel_id=1, source_target_pairs={{0,2},{1,3},{2,0},{3,1},{4,6},{5,7},{6,4},{7,5},{8,10},{9,11},{10,... | collective-permute-start | bytes 98312 | tf_op jit(solution)/shard_map/ppermute | solution.py:409
  241.6 10.5 %collective-permute-start.15 = (f32[64,128]{1,0:T(8,128)}, f32[64,128]{1,0:T(8,128)S(1)}, u32[]{:S(2)}, u32[]{:S(2)}) collective-permute-start(f32[64,128]{1,0:T(8,128)} %get-tuple-element.58), channel_id=1, source_target_pairs={{0,4},{1,5},{2,6},{3,7},{4,0},{5,1},{6,2},{7,3},{8,12},{9,13},{10,... | collective-permute-start | bytes 98312 | tf_op jit(solution)/shard_map/ppermute | solution.py:409
  243.2 8.8 %collective-permute-start.16 = (f32[64,128]{1,0:T(8,128)}, f32[64,128]{1,0:T(8,128)S(1)}, u32[]{:S(2)}, u32[]{:S(2)}) collective-permute-start(f32[64,128]{1,0:T(8,128)} %get-tuple-element.58), channel_id=1, source_target_pairs={{0,6},{1,7},{2,4},{3,5},{4,2},{5,3},{6,0},{7,1},{8,14},{9,15},{10,... | collective-permute-start | bytes 98312 | tf_op jit(solution)/shard_map/ppermute | solution.py:409
  245.4 29.2 %copy-start = (bf16[64,64]{1,0:T(8,128)(2,1)S(1)}, bf16[64,64]{1,0:T(8,128)(2,1)}, u32[]{:S(2)}) copy-start(bf16[64,64]{1,0:T(8,128)(2,1)} %w_in_ref.5) | copy-start | bytes 24580
  245.4 29.2 %copy-start.1 = (f32[64,2048]{1,0:T(8,128)S(1)}, f32[64,2048]{1,0:T(8,128)}, u32[]{:S(2)}) copy-start(f32[64,2048]{1,0:T(8,128)} %get-tuple-element.42.slope_ref) | copy-start | bytes 1572868
  245.4 29.2 %copy-start.2 = (bf16[64,2048]{1,0:T(8,128)(2,1)S(1)}, bf16[64,2048]{1,0:T(8,128)(2,1)}, u32[]{:S(2)}) copy-start(bf16[64,2048]{1,0:T(8,128)(2,1)} %get-tuple-element.41.inputs_ref) | copy-start | bytes 786436
  245.4 29.2 %copy-start.3 = (s32[8,2048]{1,0:T(8,128)S(1)}, s32[8,2048]{1,0:T(8,128)}, u32[]{:S(2)}) copy-start(s32[8,2048]{1,0:T(8,128)} %get-tuple-element.43.cells_ref) | copy-start | bytes 196612
  246.9 17.1 %collective-permute-start.10 = (f32[2,8,4096]{2,1,0:T(8,128)S(1)}, f32[2,8,4096]{2,1,0:T(8,128)S(1)}, u32[]{:S(2)}, u32[]{:S(2)}) collective-permute-start(f32[2,8,4096]{2,1,0:T(8,128)S(1)} %get-tuple-element.75), channel_id=1, source_target_pairs={{0,32},{8,40},{16,48},{24,56},{32,64},{40,72},{48,80},{56,88},{64,... | collective-permute-start | bytes 786440 | tf_op jit(solution)/shard_map/ppermute | solution.py:428
  248.2 15.8 %collective-permute-start.11 = (f32[2,8,4096]{2,1,0:T(8,128)S(1)}, f32[2,8,4096]{2,1,0:T(8,128)S(1)}, u32[]{:S(2)}, u32[]{:S(2)}) collective-permute-start(f32[2,8,4096]{2,1,0:T(8,128)S(1)} %get-tuple-element.77), channel_id=1, source_target_pairs={{0,64},{8,72},{16,80},{24,88},{32,96},{40,104},{48,112},{56,120},{... | collective-permute-start | bytes 786440 | tf_op jit(solution)/shard_map/ppermute | solution.py:428
  250.8 13.2 %collective-permute-start.12 = (f32[2,8,4096]{2,1,0:T(8,128)S(1)}, f32[2,8,4096]{2,1,0:T(8,128)S(1)}, u32[]{:S(2)}, u32[]{:S(2)}) collective-permute-start(f32[2,8,4096]{2,1,0:T(8,128)S(1)} %get-tuple-element.76), channel_id=1, source_target_pairs={{0,96},{8,104},{16,112},{24,120},{32,0},{40,8},{48,16},{56,24},{64... | collective-permute-start | bytes 786440 | tf_op jit(solution)/shard_map/ppermute | solution.py:428
  252.0 3.1 %collective-permute-start.17 = (f32[64,128]{1,0:T(8,128)S(1)}, f32[64,128]{1,0:T(8,128)S(1)}, u32[]{:S(2)}, u32[]{:S(2)}) collective-permute-start(f32[64,128]{1,0:T(8,128)S(1)} %add_add_fusion), channel_id=1, source_target_pairs={{0,1},{1,0},{2,3},{3,2},{4,5},{5,4},{6,7},{7,6},{8,9},{9,8},{10,11... | collective-permute-start | bytes 98312 | tf_op jit(solution)/shard_map/ppermute | solution.py:409
  255.2 3.9 %collective-permute-start.18 = (f32[64,128]{1,0:T(8,128)S(1)}, f32[64,128]{1,0:T(8,128)S(1)}, u32[]{:S(2)}, u32[]{:S(2)}) collective-permute-start(f32[64,128]{1,0:T(8,128)S(1)} %add.153), channel_id=1, source_target_pairs={{0,8},{8,0},{16,24},{24,16},{32,40},{40,32},{48,56},{56,48},{64,72... | collective-permute-start | bytes 98312 | tf_op jit(solution)/shard_map/ppermute | solution.py:409
  257.8 4.6 %collective-permute-start.19 = (f32[64,128]{1,0:T(8,128)S(1)}, f32[64,128]{1,0:T(8,128)S(1)}, u32[]{:S(2)}, u32[]{:S(2)}) collective-permute-start(f32[64,128]{1,0:T(8,128)S(1)} %add.153), channel_id=1, source_target_pairs={{0,16},{8,24},{16,0},{24,8},{32,48},{40,56},{48,32},{56,40},{64,80... | collective-permute-start | bytes 98312 | tf_op jit(solution)/shard_map/ppermute | solution.py:409
  259.1 4.9 %collective-permute-start.20 = (f32[64,128]{1,0:T(8,128)S(1)}, f32[64,128]{1,0:T(8,128)S(1)}, u32[]{:S(2)}, u32[]{:S(2)}) collective-permute-start(f32[64,128]{1,0:T(8,128)S(1)} %add.153), channel_id=1, source_target_pairs={{0,24},{8,16},{16,8},{24,0},{32,56},{40,48},{48,40},{56,32},{64,88... | collective-permute-start | bytes 98312 | tf_op jit(solution)/shard_map/ppermute | solution.py:409
  264.0 5.8 %collective-permute-start.21 = (f32[4,64,128]{2,1,0:T(8,128)S(1)}, f32[4,64,128]{2,1,0:T(8,128)S(1)}, u32[]{:S(2)}, u32[]{:S(2)}) collective-permute-start(f32[4,64,128]{2,1,0:T(8,128)S(1)} %pad_maximum_fusion.1.own_ref), channel_id=1, source_target_pairs={{0,32},{8,40},{16,48},{24,56},{32,0},{40,8},{48,16},{56,24},{64,96... | collective-permute-start | bytes 393224 | tf_op jit(solution)/shard_map/ppermute | solution.py:409
  264.5 7.6 %collective-permute-start.22 = (f32[4,64,128]{2,1,0:T(8,128)S(1)}, f32[4,64,128]{2,1,0:T(8,128)S(1)}, u32[]{:S(2)}, u32[]{:S(2)}) collective-permute-start(f32[4,64,128]{2,1,0:T(8,128)S(1)} %pad_maximum_fusion.1.own_ref), channel_id=1, source_target_pairs={{0,64},{8,72},{16,80},{24,88},{32,96},{40,104},{48,112},{56,120},{... | collective-permute-start | bytes 393224 | tf_op jit(solution)/shard_map/ppermute | solution.py:409
  266.2 8.4 %collective-permute-start.23 = (f32[4,64,128]{2,1,0:T(8,128)S(1)}, f32[4,64,128]{2,1,0:T(8,128)S(1)}, u32[]{:S(2)}, u32[]{:S(2)}) collective-permute-start(f32[4,64,128]{2,1,0:T(8,128)S(1)} %pad_maximum_fusion.1.own_ref), channel_id=1, source_target_pairs={{0,96},{8,104},{16,112},{24,120},{32,64},{40,72},{48,80},{56,88},{... | collective-permute-start | bytes 393224 | tf_op jit(solution)/shard_map/ppermute | solution.py:409
  268.1 11.4 %collective-permute-start.13 = (f32[2,4,8192]{2,1,0:T(4,128)S(1)}, f32[2,4,8192]{2,1,0:T(4,128)S(1)}, u32[]{:S(2)}, u32[]{:S(2)}) collective-permute-start(f32[2,4,8192]{2,1,0:T(4,128)S(1)} %pad_maximum_fusion), channel_id=1, source_target_pairs={{0,16},{8,24},{16,0},{24,8},{32,48},{40,56},{48,32},{56,40},{64,80... | collective-permute-start | bytes 786440 | tf_op jit(solution)/shard_map/ppermute | solution.py:409
